TPU v7x, 32 devices: a whole 2x2x4 slice. The times are simulated.
32 devices in a mesh: lat: 2 (over y), lon: 16 (over z, x, core).
Axes of the slice: x: 2, y: 2, z: 4, core: 2. Of those that a mesh axis runs over, the one named last changes fastest.
Arguments:
- signal: bfloat16 [96, 128, 256], P('lat', 'lon'), may hold values from -6 to 6
- cotangent: bfloat16 [96, 128, 256], P('lat', 'lon'), may hold values from -6 to 6
- weights: bfloat16 [4, 256, 256], replicated, may hold values from -0.1875 to 0.1875
- band_kernel: bfloat16 [4, 96, 3, 17], replicated, may hold values from -1.25 to 1.25
- cycle_kernel: bfloat16 [4, 4, 3, 128], replicated, may hold values from -0.3125 to 0.3125
- support_width: int32 [96], replicated, may hold values from 1 to 8, as said below
Outputs:
- conv_output: bfloat16 [96, 128, 256], P('lat', 'lon')
- signal_grad: bfloat16 [96, 128, 256], P('lat', 'lon')
- weight_grad: float32 [4, 256, 256], replicated
Inputs may be any that keep to these rules, and one draw needn't show every extreme that they name: `support_width`: some row has the half-width 8.
All inputs are finite; a program needn't handle non-finite values.
Results may differ from a plain program's by a relative error of at most 0.0049.
Values may be sent and summed in bfloat16 or wider, within the bound.
No kernel may reach another device: no remote copies, remote signals or barrier semaphores. Data moves between devices by JAX's collectives and lax.ppermute only.
A program may use at most 64 MiB of HBM per device.

v0:
```python
import math

import jax
import jax.numpy as jnp
from jax import lax
from jax.sharding import PartitionSpec as P

K = 4
R = 1
H = 8
P_SIZE = 2


precise = lax.Precision.HIGHEST


def with_halo(x, sides, width, wrap):
    for axis, dim in sides:
        devices, length = (lax.axis_size(axis), x.shape[dim])
        up = [(i, (i + 1) % devices) for i in range(devices if wrap else devices - 1)]
        down = [(j, i) for i, j in up]
        last = lax.slice_in_dim(x, length - width, length, axis=dim)
        first = lax.slice_in_dim(x, 0, width, axis=dim)
        before = lax.ppermute(last, axis, up)
        after = lax.ppermute(first, axis, down)
        x = jnp.concatenate([before, x, after], axis=dim)
    return x


def lag_table(lon_count, forward):
    outputs = jnp.arange(lon_count, dtype=jnp.int32)[:, None, None]
    inputs = jnp.arange(lon_count + 2 * H, dtype=jnp.int32)[None, :, None]
    shifts = jnp.arange(2 * H + 1, dtype=jnp.int32)[None, None, :]
    if forward:
        matched = outputs - inputs + 2 * H == shifts
    else:
        matched = inputs - outputs == shifts
    return matched.astype(jnp.float32)


def local_coefficients(band_kernel, support_width, first_row, total_rows, row_count):
    padded_kernel = jnp.pad(band_kernel, ((0, 0), (R, R), (0, 0), (0, 0)))
    padded_width = jnp.pad(support_width, (R, R))
    kernel_rows = lax.dynamic_slice_in_dim(padded_kernel, first_row, row_count, 1).astype(
        jnp.float32
    )
    width_rows = lax.dynamic_slice_in_dim(padded_width, first_row, row_count, 0)
    global_rows = first_row - R + jnp.arange(row_count, dtype=jnp.int32)
    polar_rows = (global_rows < P_SIZE) | (global_rows >= total_rows - P_SIZE)
    offsets = jnp.abs(jnp.arange(2 * H + 1, dtype=jnp.int32) - H)
    allowed = (offsets[None, :] <= width_rows[:, None]) & jnp.logical_not(polar_rows)[:, None]
    return kernel_rows * allowed[None, :, None, :].astype(jnp.float32)


def local(signal, cotangent, weights, band_kernel, cycle_kernel, support_width):
    lat_count, lon_count, channels = signal.shape
    lat_index = lax.axis_index("lat")
    lon_index = lax.axis_index("lon")
    lat_devices = lax.axis_size("lat")
    lon_total = lon_count * lax.axis_size("lon")
    total_rows = lat_count * lat_devices
    first_row = lat_index * lat_count
    is_top = lat_index == 0
    is_polar = is_top | (lat_index == lat_devices - 1)
    coeffs = local_coefficients(
        band_kernel, support_width, first_row, total_rows, lat_count + 2 * R
    )
    forward_mats = jnp.einsum(
        "ktrd,amd->ktram",
        coeffs[:, R : R + lat_count],
        lag_table(lon_count, True),
        precision=precise,
    ).astype(jnp.bfloat16)
    backward_mats = jnp.einsum(
        "ktrd,amd->ktram", coeffs, lag_table(lon_count, False), precision=precise
    ).astype(jnp.bfloat16)
    pole_kernel = lax.dynamic_slice_in_dim(cycle_kernel, jnp.where(is_top, 0, P_SIZE), P_SIZE, 1)
    out_lons = lon_index * lon_count + jnp.arange(lon_count, dtype=jnp.int32)
    cycle_lons = jnp.arange(lon_total, dtype=jnp.int32)
    stacked = jnp.stack([signal, cotangent])
    rows_both = with_halo(stacked, (("lat", 1),), R, False)
    signal_slab = jnp.where(is_top, signal[: P_SIZE + R], signal[lat_count - P_SIZE - R :])
    ext_signal = with_halo(rows_both[0], (("lon", 1),), H, True)
    cycle_signal = lax.all_gather(signal_slab, "lon", axis=1, tiled=True)
    filtered = jnp.zeros((K, lat_count, lon_count, channels), jnp.float32)
    for lat_tap in range(2 * R + 1):
        filtered = filtered + jnp.einsum(
            "kiam,imc->kiac",
            forward_mats[:, :, lat_tap],
            ext_signal[lat_tap : lat_tap + lat_count],
            preferred_element_type=jnp.float32,
        )
    zero_rows = jnp.zeros((R,) + cycle_signal.shape[1:], cycle_signal.dtype)
    cycle_padded = jnp.where(
        is_top,
        jnp.concatenate([zero_rows, cycle_signal]),
        jnp.concatenate([cycle_signal, zero_rows]),
    )

    def polar_forward():
        circulant = pole_kernel[:, :, :, (out_lons[:, None] - cycle_lons[None, :]) % lon_total]
        result = jnp.zeros((K, P_SIZE, lon_count, channels), jnp.float32)
        for lat_tap in range(2 * R + 1):
            result = result + jnp.einsum(
                "kpam,pmc->kpac",
                circulant[:, :, lat_tap],
                cycle_padded[lat_tap : lat_tap + P_SIZE],
                preferred_element_type=jnp.float32,
            )
        return result

    def forward_skip():
        return jnp.zeros((K, P_SIZE, lon_count, channels), jnp.float32)

    polar_part = lax.cond(is_polar, polar_forward, forward_skip)
    remain = lat_count - P_SIZE
    filtered = filtered + jnp.where(
        is_top,
        jnp.pad(polar_part, ((0, 0), (0, remain), (0, 0), (0, 0))),
        jnp.pad(polar_part, ((0, 0), (remain, 0), (0, 0), (0, 0))),
    )
    filtered = filtered.astype(jnp.bfloat16)
    conv_output = jnp.einsum(
        "kiac,kce->iae", filtered, weights, preferred_element_type=jnp.float32
    ).astype(jnp.bfloat16)
    local_grad = jnp.einsum(
        "kiac,iae->kce", filtered, cotangent, preferred_element_type=jnp.float32
    )
    weight_grad = lax.psum(local_grad, ("lat", "lon")) * (1.0 / math.sqrt(total_rows * lon_total))
    mixed_rows = jnp.einsum(
        "tae,kce->ktac", rows_both[1], weights, preferred_element_type=jnp.float32
    ).astype(jnp.bfloat16)
    ext_grad = with_halo(mixed_rows, (("lon", 2),), H, True)
    mixed_slab = jnp.where(
        is_top, mixed_rows[:, R : R + P_SIZE], mixed_rows[:, R + lat_count - P_SIZE : R + lat_count]
    )
    cycle_mixed = lax.all_gather(mixed_slab, "lon", axis=2, tiled=True)
    signal_grad = jnp.zeros((lat_count, lon_count, channels), jnp.float32)
    for lat_tap in range(2 * R + 1):
        start = 2 * R - lat_tap
        signal_grad = signal_grad + jnp.einsum(
            "kjam,kjmc->jac",
            backward_mats[:, start : start + lat_count, lat_tap],
            ext_grad[:, start : start + lat_count],
            preferred_element_type=jnp.float32,
        )

    def polar_backward():
        circulant = pole_kernel[:, :, :, (cycle_lons[None, :] - out_lons[:, None]) % lon_total]
        result = jnp.zeros((P_SIZE + 2 * R, lon_count, channels), jnp.float32)
        for lat_tap in range(2 * R + 1):
            portion = jnp.einsum(
                "kpam,kpmc->pac",
                circulant[:, :, lat_tap],
                cycle_mixed,
                preferred_element_type=jnp.float32,
            )
            result = result + jnp.pad(portion, ((lat_tap, 2 * R - lat_tap), (0, 0), (0, 0)))
        return result

    def backward_skip():
        return jnp.zeros((P_SIZE + 2 * R, lon_count, channels), jnp.float32)

    polar_grad = lax.cond(is_polar, polar_backward, backward_skip)
    leftover = lat_count - P_SIZE - R
    signal_grad = signal_grad + jnp.where(
        is_top,
        jnp.pad(polar_grad[R:], ((0, leftover), (0, 0), (0, 0))),
        jnp.pad(polar_grad[: P_SIZE + R], ((leftover, 0), (0, 0), (0, 0))),
    )
    return (conv_output, signal_grad.astype(jnp.bfloat16), weight_grad)


def solution(mesh):
    placed = (P("lat", "lon", None), P("lat", "lon", None), P(), P(), P(), P())
    return jax.shard_map(
        local,
        mesh=mesh,
        in_specs=placed,
        out_specs=(P("lat", "lon", None), P("lat", "lon", None), P()),
        check_vma=False,
    )
```

profile of v0, /device:TPU:0, one launch (start us, length us, event | category | flops | bytes accessed | tf_op | source)
XLA Modules:
  0.0 223.0 jit_solution(4404802248755602315)
XLA Ops:
  7.2 0.0 copy-start
  7.2 0.0 all-reduce.17.cloned.1.call-start
  7.2 0.8 pad_maximum_fusion.4
  8.0 1.3 collective-permute-start.1
  9.3 4.9 %collective-permute-start = (bf16[2,1,8,256]{3,2,1,0:T(8,128)(2,1)S(1)}, bf16[2,1,8,256]{3,2,1,0:T(8,128)(2,1)S(1)}, u32[]{:S(2)}, u32[]{:S(2)}) collective-permute-start(bf16[2,1,8,256]{3,2,1,0:T(8,128)(2,1)S(1)} %get-tuple-element.104), channel_id=1, source_target_pairs={{0,16},{1,17},{2,18},{3,19},{4,20},{5,21},{6,22},{7,23},{8,24},{9,... | collective-permute-start | bytes 24584 | tf_op jit(solution)/shard_map/ppermute | solution.py:24
  14.2 0.7 slice_select_fusion.1
  15.0 0.8 copy.23
  15.8 0.7 pad_dynamic-slice_fusion
  16.5 0.1 and_convert_fusion
  16.6 0.1 convert_multiply_fusion
  16.7 0.7 convolution_convert_fusion.2
  17.4 0.0 copy-start.14
  17.4 0.1 slice_bitcast_fusion.30
  17.5 0.7 convolution_convert_fusion.1
  18.2 0.2 slice_bitcast_fusion.29
  18.4 23.3 %all_gather.6 = bf16[3,128,256]{2,1,0:T(8,128)(2,1)S(1)} all-gather(bf16[3,8,256]{2,1,0:T(8,128)(2,1)S(1)} %slice_select_fusion.1), channel_id=1, replica_groups=mesh['lat'=2,'lon'=16] {'lon'}, dimensions={1}, use_global_device_ids=true | all-gather | bytes 208896 | tf_op jit(solution)/shard_map/all_gather | solution.py:84
  41.7 0.9 copy.57
  42.6 1.3 copy.24
  43.9 1.3 copy.25
  45.2 0.6 copy.26
  45.9 1.4 copy.30
  47.2 1.3 copy.29
  48.5 1.3 copy.28
  49.9 10.9 %conditional.2 = (f32[4,48,8,256]{3,2,0,1:T(8,128)S(1)}, f32[4,48,8,256]{3,2,0,1:T(8,128)S(1)}) conditional(s32[]{:T(128)} %convert_element_type.57, () %tuple.39, (s32[8]{0:T(128)S(1)}, s32[128]{0:T(128)S(1)}, bf16[4,2,3,128]{0,1,3,2:T(2,128)(2,1)}, pred[]{:T(512)}, bf16[3,128,256]{2,1,0:T(8,128)(2,1)S(1)}) %tuple.40), branch_computations={%region_0.1_spmd, %region_1.2_spmd} | conditional | flops 12763136 | bytes 4645425 | solution.py:115
  49.9 0.1 fusion.4
  50.0 8.3 %gather_fusion = bf16[1024,4,2,3]{1,2,3,0:T(2,128)(2,1)S(1)} fusion(bf16[4,2,3,128]{0,1,3,2:T(2,128)(2,1)} %get-tuple-element.70, s32[1024]{0:T(1024)S(1)} %fusion.4), kind=kCustom, calls=%fused_computation | custom fusion | bytes 102400 | tf_op jit(solution)/shard_map/cond/branch_1_fun/gather | solution.py:101
  58.3 1.9 copy.53
  60.2 0.1 fusion.1
  60.3 0.1 convolution_add_fusion.1
  60.5 0.1 fusion
  60.6 0.2 fusion.54
  60.9 0.1 pad_maximum_fusion.2
  60.9 0.0 copy-start.8
  61.0 0.1 collective-permute-start.3
  61.0 0.5 collective-permute-start.2
  61.5 0.4 fusion.15
  62.0 4.1 %collective-permute-start.5 = (bf16[4,50,8,256]{3,2,0,1:T(8,128)(2,1)S(1)}, bf16[4,50,8,256]{3,2,0,1:T(8,128)(2,1)}, u32[]{:S(2)}, u32[]{:S(2)}) collective-permute-start(bf16[4,50,8,256]{3,2,0,1:T(8,128)(2,1)S(1)} %fusion.15), channel_id=1, source_target_pairs={{1,0},{2,1},{3,2},{4,3},{5,4},{6,5},{7,6},{8,7},{9,8},{10,9},{11,1... | collective-permute-start | bytes 2457608 | tf_op jit(solution)/shard_map/ppermute | solution.py:25
  66.0 3.1 %collective-permute-done.2 = bf16[50,8,256]{2,1,0:T(8,128)(2,1)S(1)} collective-permute-done((bf16[50,8,256]{2,1,0:T(8,128)(2,1)S(1)}, bf16[50,8,256]{2,1,0:T(8,128)(2,1)S(1)}, u32[]{:S(2)}, u32[]{:S(2)}) %collective-permute-start.2) | collective-permute-done | bytes 204832 | tf_op jit(solution)/shard_map/ppermute | solution.py:24
  69.2 0.3 fusion.39
  69.5 0.6 copy-done.9
  70.2 0.3 fusion.38
  70.5 1.1 copy-done.2
  71.6 0.5 fusion.14
  72.0 0.9 copy-done.3
  72.9 1.4 convolution_bitcast_fusion.3
  74.4 0.0 all-reduce.17.cloned.1.call-update
  74.4 27.1 %all_gather.7 = bf16[4,2,128,256]{3,2,0,1:T(8,128)(2,1)S(1)} all-gather(bf16[4,2,8,256]{3,2,0,1:T(8,128)(2,1)S(1)} %slice_select_fusion), channel_id=1, replica_groups=mesh['lat'=2,'lon'=16] {'lon'}, dimensions={2}, use_global_device_ids=true | all-gather | bytes 557056 | tf_op jit(solution)/shard_map/all_gather | solution.py:137
  101.5 15.0 %conditional.3 = (f32[48,8,256]{2,1,0:T(8,128)S(1)}, f32[48,8,256]{2,1,0:T(8,128)S(1)}) conditional(s32[]{:T(128)} %convert_element_type.57, () %tuple.41, (s32[128]{0:T(128)S(1)}, s32[8]{0:T(128)S(1)}, bf16[4,2,3,128]{0,1,3,2:T(2,128)(2,1)}, bf16[4,2,128,256]{3,2,0,1:T(8,128)(2,1)S(1)}) %tuple.42), branch_computations={%region_2.3_spmd, %region_3.4_spmd} | conditional | flops 12615680 | bytes 2892344 | solution.py:164
  101.5 0.1 fusion.7
  101.6 11.4 %gather_fusion.1 = bf16[1024,4,2,3]{1,2,3,0:T(2,128)(2,1)} fusion(bf16[4,2,3,128]{0,1,3,2:T(2,128)(2,1)} %get-tuple-element.75, s32[1024]{0:T(1024)S(1)} %fusion.7), kind=kCustom, calls=%fused_computation.1 | custom fusion | bytes 102400 | tf_op jit(solution)/shard_map/cond/branch_1_fun/gather | solution.py:149
  113.0 2.8 %copy.54 = bf16[8,128,4,2,3]{1,0,2,3,4:T(8,128)(2,1)S(1)} copy(bf16[8,128,4,2,3]{2,3,4,1,0:T(2,128)(2,1)} %bitcast.165) | data formatting | bytes 98304 | tf_op jit(solution)/shard_map/cond/branch_1_fun/gather | solution.py:149
  115.8 0.2 convolution_bitcast_fusion
  116.0 0.2 convolution_bitcast_fusion.1
  116.2 0.2 convolution_bitcast_fusion.2
  116.5 1.1 fusion.37
  117.6 91.1 %all-reduce.17.cloned.1.call-done = f32[4,256,256]{2,1,0:T(8,128)} async-done(((f32[4,256,256]{2,1,0:T(8,128)}), f32[4,256,256]{2,1,0:T(8,128)}) %all-reduce.17.cloned.1.call-update) | async-done | bytes 1048592 | tf_op jit(solution)/shard_map/psum | solution.py:129
  208.6 2.3 %broadcast_multiply_fusion = f32[4,256,256]{2,1,0:T(8,128)} fusion(f32[4,256,256]{2,1,0:T(8,128)} %all-reduce.17.cloned.1.call-done), kind=kLoop, calls=%fused_computation.69 | loop fusion | flops 262144 | bytes 2097152 | tf_op jit(solution)/shard_map/mul | solution.py:129
  210.9 1.6 pad_maximum_fusion
  212.6 0.7 fusion.22
  213.3 0.3 copy-done.7
  213.6 0.7 fusion.19
  214.3 0.3 copy-done.5
  214.6 0.1 copy-done.11
  214.7 1.4 fusion.34
  (43 shorter events, 0.3 us)
Async XLA Ops:
  7.2 54.4 %copy-start = (bf16[4,256,256]{2,1,0:T(8,128)(2,1)S(1)}, bf16[4,256,256]{2,1,0:T(8,128)(2,1)}, u32[]{:S(2)}) copy-start(bf16[4,256,256]{2,1,0:T(8,128)(2,1)} %param.12) | copy-start | bytes 1572868
  7.2 201.4 %all-reduce.17.cloned.1.call-start = ((), (), s32[]{:S(2)}) async-start(), calls=%async_computation | async-start | bytes 2097152 | tf_op jit(solution)/shard_map/psum | solution.py:129
  8.0 52.8 %collective-permute-start.1 = (bf16[2,1,8,256]{3,2,1,0:T(8,128)(2,1)S(1)}, bf16[2,1,8,256]{3,2,1,0:T(8,128)(2,1)S(1)}, u32[]{:S(2)}, u32[]{:S(2)}) collective-permute-start(bf16[2,1,8,256]{3,2,1,0:T(8,128)(2,1)S(1)} %get-tuple-element.105), channel_id=1, source_target_pairs={{16,0},{17,1},{18,2},{19,3},{20,4},{21,5},{22,6},{23,7},{24,8},{25... | collective-permute-start | bytes 24584 | tf_op jit(solution)/shard_map/ppermute | solution.py:25
  9.3 51.5 %collective-permute-start = (bf16[2,1,8,256]{3,2,1,0:T(8,128)(2,1)S(1)}, bf16[2,1,8,256]{3,2,1,0:T(8,128)(2,1)S(1)}, u32[]{:S(2)}, u32[]{:S(2)}) collective-permute-start(bf16[2,1,8,256]{3,2,1,0:T(8,128)(2,1)S(1)} %get-tuple-element.104), channel_id=1, source_target_pairs={{0,16},{1,17},{2,18},{3,19},{4,20},{5,21},{6,22},{7,23},{8,24},{9,... | collective-permute-start | bytes 24584 | tf_op jit(solution)/shard_map/ppermute | solution.py:24
  17.4 1.0 copy-start.14
  49.9 11.0 %copy-start.12 = (bf16[48,8,256]{2,1,0:T(8,128)(2,1)S(1)}, bf16[48,8,256]{2,1,0:T(8,128)(2,1)}, u32[]{:S(2)}) copy-start(bf16[48,8,256]{2,1,0:T(8,128)(2,1)} %param.10) | copy-start | bytes 589828
  49.9 11.0 %copy-start.13 = (bf16[48,8,256]{2,1,0:T(8,128)(2,1)S(1)}, bf16[48,8,256]{2,1,0:T(8,128)(2,1)}, u32[]{:S(2)}) copy-start(bf16[48,8,256]{2,1,0:T(8,128)(2,1)} %param.11) | copy-start | bytes 589828
  60.8 8.3 %copy-start.1 = (f32[4,48,8,256]{3,2,0,1:T(8,128)}, f32[4,48,8,256]{3,2,0,1:T(8,128)S(1)}, u32[]{:S(2)}) copy-start(f32[4,48,8,256]{3,2,0,1:T(8,128)S(1)} %get-tuple-element.86) | copy-start | bytes 4718596
  60.9 8.2 %copy-start.8 = (bf16[4,48,8,24]{3,2,0,1:T(8,128)(2,1)S(1)}, bf16[4,48,8,24]{3,2,0,1:T(8,128)(2,1)}, u32[]{:S(2)}) copy-start(bf16[4,48,8,24]{3,2,0,1:T(8,128)(2,1)} %copy.24) | copy-start | bytes 221188
  61.0 5.1 %collective-permute-start.3 = (bf16[50,8,256]{2,1,0:T(8,128)(2,1)S(1)}, bf16[50,8,256]{2,1,0:T(8,128)(2,1)S(1)}, u32[]{:S(2)}, u32[]{:S(2)}) collective-permute-start(bf16[50,8,256]{2,1,0:T(8,128)(2,1)S(1)} %slice_bitcast_fusion.26), channel_id=1, source_target_pairs={{1,0},{2,1},{3,2},{4,3},{5,4},{6,5},{7,6},{8,7},{9,8},{10,9},{11,1... | collective-permute-start | bytes 614408 | tf_op jit(solution)/shard_map/ppermute | solution.py:25
  61.0 8.0 %collective-permute-start.2 = (bf16[50,8,256]{2,1,0:T(8,128)(2,1)S(1)}, bf16[50,8,256]{2,1,0:T(8,128)(2,1)S(1)}, u32[]{:S(2)}, u32[]{:S(2)}) collective-permute-start(bf16[50,8,256]{2,1,0:T(8,128)(2,1)S(1)} %slice_bitcast_fusion.26), channel_id=1, source_target_pairs={{0,1},{1,2},{2,3},{3,4},{4,5},{5,6},{6,7},{7,8},{8,9},{9,10},{10,1... | collective-permute-start | bytes 614408 | tf_op jit(solution)/shard_map/ppermute | solution.py:24
  62.0 149.0 %collective-permute-start.5 = (bf16[4,50,8,256]{3,2,0,1:T(8,128)(2,1)S(1)}, bf16[4,50,8,256]{3,2,0,1:T(8,128)(2,1)}, u32[]{:S(2)}, u32[]{:S(2)}) collective-permute-start(bf16[4,50,8,256]{3,2,0,1:T(8,128)(2,1)S(1)} %fusion.15), channel_id=1, source_target_pairs={{1,0},{2,1},{3,2},{4,3},{5,4},{6,5},{7,6},{8,7},{9,8},{10,9},{11,1... | collective-permute-start | bytes 2457608 | tf_op jit(solution)/shard_map/ppermute | solution.py:25
  66.0 144.9 %collective-permute-start.4 = (bf16[4,50,8,256]{3,2,0,1:T(8,128)(2,1)S(1)}, bf16[4,50,8,256]{3,2,0,1:T(8,128)(2,1)}, u32[]{:S(2)}, u32[]{:S(2)}) collective-permute-start(bf16[4,50,8,256]{3,2,0,1:T(8,128)(2,1)S(1)} %fusion.15), channel_id=1, source_target_pairs={{0,1},{1,2},{2,3},{3,4},{4,5},{5,6},{6,7},{7,8},{8,9},{9,10},{10,1... | collective-permute-start | bytes 2457608 | tf_op jit(solution)/shard_map/ppermute | solution.py:24
  69.2 1.0 copy-start.9
  70.1 1.4 copy-start.2
  72.0 0.9 copy-start.3
  101.5 15.0 %copy-start.4 = (bf16[4,48,8,256]{3,2,0,1:T(8,128)(2,1)S(1)}, bf16[4,48,8,256]{3,2,0,1:T(8,128)(2,1)}, u32[]{:S(2)}) copy-start(bf16[4,48,8,256]{3,2,0,1:T(8,128)(2,1)} %copy-done.3) | copy-start | bytes 2359300
  116.5 92.1 %copy-start.10 = (f32[48,8,256]{2,1,0:T(8,128)}, f32[48,8,256]{2,1,0:T(8,128)S(1)}, u32[]{:S(2)}) copy-start(f32[48,8,256]{2,1,0:T(8,128)S(1)} %get-tuple-element.89) | copy-start | bytes 1179652
  210.9 1.6 copy-start.6
  212.6 1.0 copy-start.7
  213.6 1.0 copy-start.5
  213.6 1.1 copy-start.11
Sparse Core Ops, SparseCore 0:
  74.5 134.0 all-reduce.16
where the time goes:
time: 224 us; the launch traced here: 223 us
  waiting for transfers between devices  94.1 us (42%)
  blocking collectives  50.4 us (22%)
  local copies, waits for them, and re-layouts  38 us (17%)
  between operations  14.4 us (6%)
  starting transfers between devices  10.8 us (5%)
  matrix products  9.26 us (4%)
  other arithmetic  5.96 us (3%)
    psum x1, waiting for transfers between devices, local(): lax.psum(local_grad, ('lat', 'lon'))  91.1 us
    all_gather x1, blocking collectives, local(): cycle_mixed = lax.all_gather(mixed_slab, 'lon', axis=2, tiled=True)  27.1 us
    all_gather x1, blocking collectives, local(): cycle_signal = lax.all_gather(signal_slab, 'lon', axis=1, tiled=True)  23.3 us
    gather x2, local copies, waits for them, and re-layouts, polar_backward(): pole_kernel[:, :, :, (cycle_lons[None, :] - out_lons[:, None]) % lon_total]  14.2 us
    gather x2, local copies, waits for them, and re-layouts, polar_forward(): pole_kernel[:, :, :, (out_lons[:, None] - cycle_lons[None, :]) % lon_total]  10.2 us
    ppermute x3, starting transfers between devices, with_halo(): after = lax.ppermute(first, axis, down)  5.39 us
    ppermute x3, starting transfers between devices, with_halo(): before = lax.ppermute(last, axis, up)  5.37 us
    unnamed x32, local copies, waits for them, and re-layouts  5.04 us
  transfers between devices with their start and end apart: 7, of which 2 were waited for; matrix products, arithmetic and copies ran while one was open for 20% of the time, Pallas kernels for 0%

commit v1 on v0

v1 whole, which is shorter than its diff:
```python
import math

import jax
import jax.numpy as jnp
from jax import lax
from jax.sharding import Mesh, PartitionSpec as P

K = 4
R = 1
H = 8
P_SIZE = 2
TAPS = 2 * R + 1
LAGS = 2 * H + 1
SLAB = P_SIZE + R
LON = ("ring", "pair", "core")
CHIPS = ("lat", "ring", "pair")


def dot(spec, a, b):
    return jnp.einsum(spec, a, b, preferred_element_type=jnp.float32)


def bf16(x):
    return x.astype(jnp.bfloat16)


def band_coefficients(band_kernel, support_width, first_row, total_rows, row_count):
    padded_kernel = jnp.pad(band_kernel, ((0, 0), (R, R), (0, 0), (0, 0)))
    padded_width = jnp.pad(support_width, (R, R))
    kernel_rows = lax.dynamic_slice_in_dim(padded_kernel, first_row, row_count, 1)
    width_rows = lax.dynamic_slice_in_dim(padded_width, first_row, row_count, 0)
    global_rows = first_row - R + jnp.arange(row_count, dtype=jnp.int32)
    polar_rows = (global_rows < P_SIZE) | (global_rows >= total_rows - P_SIZE)
    offsets = jnp.abs(jnp.arange(LAGS, dtype=jnp.int32) - H)
    allowed = (offsets[None, :] <= width_rows[:, None]) & jnp.logical_not(polar_rows)[:, None]
    return jnp.where(allowed[None, :, None, :], kernel_rows, jnp.zeros_like(kernel_rows))


def band_matrices(rows, lon_count, forward):
    outputs = jnp.arange(lon_count, dtype=jnp.int32)[:, None, None]
    inputs = jnp.arange(lon_count + 2 * H, dtype=jnp.int32)[None, :, None]
    shifts = jnp.arange(LAGS, dtype=jnp.int32)[None, None, :]
    table = outputs - inputs + 2 * H == shifts if forward else inputs - outputs == shifts
    return bf16(dot("ktrd,amd->tkarm", rows, bf16(table)))


def windows(left, field, right):
    ext = jnp.concatenate([left, field, right], axis=1)
    ext = jnp.pad(ext, ((R, R), (0, 0), (0, 0)))
    return jnp.stack([ext[t : t + field.shape[0]] for t in range(TAPS)], axis=1)


def block_diagonal(a, b):
    upper = jnp.pad(a, ((0, 0), (0, 0), (0, b.shape[2]), (0, 0)))
    lower = jnp.pad(b, ((0, 0), (0, 0), (a.shape[2], 0), (0, 0)))
    return jnp.concatenate([upper, lower], axis=1)


def local(signal, cotangent, weights, band_kernel, cycle_kernel, support_width):
    lat_count, lon_count, channels = signal.shape
    lat_devices = lax.axis_size("lat")
    lon_devices = lax.axis_size(LON)
    lat_index = lax.axis_index("lat")
    lon_index = lax.axis_index(LON)
    core = lax.axis_index("core")
    chip = lon_index // 2
    lon_total = lon_count * lon_devices
    total_rows = lat_count * lat_devices
    first_row = lat_index * lat_count
    is_top = lat_index == 0
    is_polar = is_top | (lat_index == lat_devices - 1)
    swap = [(0, 1), (1, 0)]
    assert lon_count == H

    to_right = [(i, (i + 1) % lon_devices) for i in range(lon_devices)]
    to_left = [(j, i) for i, j in to_right]

    def sector_edges(field):
        return lax.ppermute(field, LON, to_right), lax.ppermute(field, LON, to_left)

    signal_left, signal_right = sector_edges(signal)

    both = jnp.stack([signal, cotangent])
    first, last = both[:, :R], both[:, lat_count - R :]
    if lat_devices == 2:
        edges = lax.ppermute(jnp.where(is_top, last, first), "lat", swap)
    else:
        up = [(i, i + 1) for i in range(lat_devices - 1)]
        down = [(j, i) for i, j in up]
        edges = jnp.concatenate([lax.ppermute(last, "lat", up), lax.ppermute(first, "lat", down)], axis=1)
    count = edges.shape[1]

    cot_left, cot_right = sector_edges(cotangent)
    edges, band_kernel, cycle_kernel, support_width = lax.optimization_barrier(
        (edges, band_kernel, cycle_kernel, support_width)
    )

    slab = jnp.concatenate(
        [
            jnp.where(is_top, signal[:SLAB], signal[lat_count - SLAB :]),
            edges[0],
            jnp.where(is_top, cotangent[:P_SIZE], cotangent[lat_count - P_SIZE :]),
            edges[1],
        ]
    )
    sectors = lon_devices // 2
    even = lax.all_to_all(jnp.broadcast_to(slab[None], (sectors,) + slab.shape), ("ring", "pair"), 0, 0)
    odd = lax.ppermute(even, "core", swap)
    circle = jnp.stack([jnp.where(core == 0, even, odd), jnp.where(core == 0, odd, even)], axis=1)
    circle = circle.reshape((lon_devices,) + slab.shape)
    circle = jnp.moveaxis(circle, 0, 1).reshape(slab.shape[0], lon_total, channels)
    signal_circle, cot_circle = circle[: SLAB + count], circle[SLAB + count :]

    coeffs = band_coefficients(band_kernel, support_width, first_row, total_rows, lat_count + 2 * R)
    forward = band_matrices(coeffs[:, R : R + lat_count], lon_count, True)

    def lag_vector(rows):
        return jnp.concatenate([rows[..., H:], jnp.zeros(rows.shape[:-1] + (lon_total - LAGS,), rows.dtype), rows[..., :H]], -1)

    reads = [coeffs[:, R, 0], coeffs[:, lat_count, 2 * R]]
    gives = [coeffs[:, 0, 2 * R], coeffs[:, lat_count + R, 0]]
    zero = jnp.zeros((K, lon_total), jnp.bfloat16)
    if count == 1:
        edge_forward = lag_vector(jnp.where(is_top, reads[1], reads[0]))[:, None, None]
        edge_adjoint = lag_vector(jnp.where(is_top, gives[1], gives[0]))[:, None, None]
    else:
        edge_forward = block_diagonal(lag_vector(reads[0])[:, None, None], lag_vector(reads[1])[:, None, None])
        edge_adjoint = block_diagonal(lag_vector(gives[0])[:, None, None], lag_vector(gives[1])[:, None, None])
    top_rows = [[cycle_kernel[:, p, s - p + R] if 0 <= s - p + R < TAPS else zero for s in range(SLAB)] for p in range(P_SIZE)]
    low_rows = [[cycle_kernel[:, P_SIZE + p, s - p] if 0 <= s - p < TAPS else zero for s in range(SLAB)] for p in range(P_SIZE)]
    slab_kernel = jnp.where(
        is_top,
        jnp.stack([jnp.stack(row, axis=1) for row in top_rows], axis=1),
        jnp.stack([jnp.stack(row, axis=1) for row in low_rows], axis=1),
    )
    slab_kernel = jnp.where(is_polar, slab_kernel, jnp.zeros_like(slab_kernel))
    lags = jnp.arange(lon_total, dtype=jnp.int32)[:, None, None]
    own_lons = lon_index * lon_count + jnp.arange(lon_count, dtype=jnp.int32)
    chip_lons = chip * 2 * lon_count + jnp.arange(2 * lon_count, dtype=jnp.int32)
    all_lons = jnp.arange(lon_total, dtype=jnp.int32)
    distance = (chip_lons[:, None] - all_lons[None, :]) % lon_total
    opposite = (all_lons[None, :] - own_lons[:, None]) % lon_total
    forward_cycle = bf16(dot("kpsd,dam->kpasm", block_diagonal(slab_kernel, edge_forward), bf16(distance[None] == lags)))
    adjoint_kernel = block_diagonal(jnp.swapaxes(slab_kernel, 1, 2), edge_adjoint)

    def placed(extra, polar_count):
        polar, edge = extra[:, :polar_count], extra[:, polar_count:]

        def rows(block, before):
            return jnp.pad(block, ((0, 0), (before, lat_count - block.shape[1] - before), (0, 0), (0, 0)))

        if count == 1:
            return jnp.where(
                is_top,
                rows(polar, 0) + rows(edge, lat_count - R),
                rows(polar, lat_count - polar_count) + rows(edge, 0),
            )
        out = jnp.where(is_top, rows(polar, 0), rows(polar, lat_count - polar_count))
        return out + rows(edge[:, :R], 0) + rows(edge[:, R:], lat_count - R)

    left, right, _, _ = lax.optimization_barrier((signal_left, signal_right, cot_left, cot_right))
    banded = dot("ikarm,irmc->ikac", forward, windows(left, signal, right))
    banded = jnp.moveaxis(banded, 1, 0)
    scale = 1.0 / math.sqrt(total_rows * lon_total)
    partial = (dot("kiac,iae->kce", bf16(banded), cotangent) * scale).reshape(2, -1, channels)
    given = bf16(jnp.where(core == 0, partial[1], partial[0]))
    kept = jnp.where(core == 0, partial[0], partial[1])
    kept = kept + lax.ppermute(given, "core", swap).astype(jnp.float32)

    extra = dot("kpasm,smc->kpac", forward_cycle, signal_circle)
    partner = jnp.where(core == 0, cot_right, cot_left)
    chip_rows = jnp.concatenate([jnp.where(core == 0, cotangent, partner), jnp.where(core == 0, partner, cotangent)], axis=1)
    polar_rows = jnp.where(is_top, chip_rows[:P_SIZE], chip_rows[lat_count - P_SIZE :])
    if count == 1:
        edge_rows = jnp.where(is_top, chip_rows[lat_count - R :], chip_rows[:R])
    else:
        edge_rows = jnp.concatenate([chip_rows[:R], chip_rows[lat_count - R :]])
    kept_extra = lax.dynamic_slice_in_dim(bf16(extra), core * (K // 2), K // 2, 0)
    extra_partial = dot("kpac,pae->kce", kept_extra, jnp.concatenate([polar_rows, edge_rows]))
    kept = kept + (extra_partial * scale).reshape(-1, channels)

    group = lat_devices * lon_devices // 2
    parts = lax.all_to_all(bf16(kept).reshape(group, -1, channels), CHIPS, 0, 0)
    chunk = bf16(jnp.sum(parts.astype(jnp.float32), axis=0))
    half = lax.all_to_all(jnp.broadcast_to(chunk[None], (group,) + chunk.shape), CHIPS, 0, 0)
    other = lax.ppermute(half, "core", swap)
    weight_grad = jnp.stack([jnp.where(core == 0, half, other), jnp.where(core == 0, other, half)])
    weight_grad = weight_grad.reshape(K, channels, channels).astype(jnp.float32)

    coeffs, adjoint_kernel, extra, kept = lax.optimization_barrier((coeffs, adjoint_kernel, extra, kept))
    own_extra = lax.dynamic_slice_in_dim(extra, core * lon_count, lon_count, 2)
    filtered = bf16(banded + placed(own_extra, P_SIZE))
    conv_output = bf16(dot("kiac,kce->iae", filtered, weights))

    adjoint_rows = jnp.stack([coeffs[:, t : t + lat_count, 2 * R - t] for t in range(TAPS)], axis=2)
    adjoint = band_matrices(adjoint_rows, lon_count, False)
    adjoint_cycle = bf16(dot("kspd,dbm->ksbpm", adjoint_kernel, bf16(opposite[None] == lags)))
    spread = dot("ikarm,irme->ikae", adjoint, windows(cot_left, cotangent, cot_right))
    spread = jnp.moveaxis(spread, 1, 0)
    spread = spread + placed(dot("ksbpm,pme->ksbe", adjoint_cycle, cot_circle), SLAB)
    signal_grad = bf16(dot("kjbe,kce->jbc", bf16(spread), weights))
    return conv_output, signal_grad, weight_grad


def solution(mesh):
    lat_devices, lon_devices = mesh.devices.shape
    split = Mesh(mesh.devices.reshape(lat_devices, lon_devices // 4, 2, 2), ("lat",) + LON)
    placed = (P("lat", LON, None), P("lat", LON, None), P(), P(), P(), P())
    return jax.shard_map(
        local,
        mesh=split,
        in_specs=placed,
        out_specs=(P("lat", LON, None), P("lat", LON, None), P()),
        check_vma=False,
    )
```

time: 224 us -> 69.6 us (0.31)
  waiting for transfers between devices: 94.1 us -> 19.8 us
  blocking collectives: 50.4 us -> 0 us
  local copies, waits for them, and re-layouts: 38 us -> 9.61 us
  between operations: 14.4 us -> 1.08 us
  starting transfers between devices: 10.8 us -> 23.7 us
    psum x1 -> x0, waiting for transfers between devices: 91.1 us -> none  [local(): lax.psum(local_grad, ('lat', 'lon'))]
    all_gather x2 -> x0, blocking collectives: 50.4 us -> none  [the longest x1 27.1 us: local(): cycle_mixed = lax.all_gather(mixed_slab, 'lon', axis=2, tiled=True)]
    gather x4 -> x0, local copies, waits for them, and re-layouts: 24.4 us -> none  [the longest x2 14.2 us: polar_backward(): pole_kernel[:, :, :, (cycle_lons[None, :] - out_lons[:, None]) % lon_total]]
    all_to_all x0 -> x3, waiting for transfers between devices: none -> 18.1 us  [the longest x1 9.62 us: local(): parts = lax.all_to_all(bf16(kept).reshape(group, -1, channels), CHIPS, 0, 0)]
    all_to_all x0 -> x3, starting transfers between devices: none -> 11.7 us  [the longest x1 4.18 us: local(): parts = lax.all_to_all(bf16(kept).reshape(group, -1, channels), CHIPS, 0, 0)]
    squeeze x9 -> x1, local copies, waits for them, and re-layouts: 7.55 us -> 0.01 us  [local(): edges[0]]
    unnamed x32 -> x17, local copies, waits for them, and re-layouts: 5.04 us -> 1.55 us
    mul x2 -> x0, other arithmetic: 2.42 us -> none  [the longest x1 2.3 us: local(): lax.psum(local_grad, ('lat', 'lon'))]
  transfers between devices with their start and end apart: 7 -> 11, of which waited for: 2 -> 4; matrix products, arithmetic and copies ran while one was open for 20% -> 29% of each run, Pallas kernels for 0% -> 0%
where the time goes in v1:
time: 69.6 us; the launch traced here: 68.7 us
  starting transfers between devices  23.7 us (34%)
  waiting for transfers between devices  19.8 us (28%)
  local copies, waits for them, and re-layouts  9.61 us (14%)
  matrix products  8.35 us (12%)
  other arithmetic  6.19 us (9%)
  between operations  1.08 us (2%)
    all_to_all x1, waiting for transfers between devices, local(): parts = lax.all_to_all(bf16(kept).reshape(group, -1, channels), CHIPS, 0, 0)  9.62 us
    ppermute x2, starting transfers between devices, sector_edges(): lax.ppermute(field, LON, to_left)  9.47 us
    dot_general x11, matrix products, dot(): return jnp.einsum(spec, a, b, preferred_element_type=jnp.float32)  8.35 us
    all_to_all x1, waiting for transfers between devices, local(): lax.all_to_all(jnp.broadcast_to(chunk[None], (group,) + chunk.shape), CHI...  5.08 us
    all_to_all x1, starting transfers between devices, local(): parts = lax.all_to_all(bf16(kept).reshape(group, -1, channels), CHIPS, 0, 0)  4.18 us
    all_to_all x1, starting transfers between devices, local(): lax.all_to_all(jnp.broadcast_to(slab[None], (sectors,) + slab.shape), ('r...  4.03 us
    all_to_all x1, starting transfers between devices, local(): lax.all_to_all(jnp.broadcast_to(chunk[None], (group,) + chunk.shape), CHI...  3.53 us
    all_to_all x1, waiting for transfers between devices, local(): lax.all_to_all(jnp.broadcast_to(slab[None], (sectors,) + slab.shape), ('r...  3.43 us
  transfers between devices with their start and end apart: 11, of which 4 were waited for; matrix products, arithmetic and copies ran while one was open for 29% of the time, Pallas kernels for 0%

profile of v1, /device:TPU:0, one launch (start us, length us, event | category | flops | bytes accessed | tf_op | source)
XLA Modules:
  0.0 68.7 jit_solution(16672145301641704320)
XLA Ops:
  0.6 0.0 copy-start
  0.6 0.5 collective-permute-start.1
  1.1 5.0 %collective-permute-start.2 = (bf16[48,8,256]{2,1,0:T(8,128)(2,1)}, bf16[48,8,256]{2,1,0:T(8,128)(2,1)S(1)}, u32[]{:S(2)}, u32[]{:S(2)}) collective-permute-start(bf16[48,8,256]{2,1,0:T(8,128)(2,1)} %param.6), channel_id=1, source_target_pairs={{1,0},{2,1},{3,2},{4,3},{5,4},{6,5},{7,6},{8,7},{9,8},{10,9},{11,1... | collective-permute-start | bytes 589832 | tf_op jit(solution)/shard_map/ppermute | solution.py:79
  6.2 0.0 collective-permute-start.3
  6.2 4.4 %collective-permute-start.4 = (bf16[48,8,256]{2,1,0:T(8,128)(2,1)}, bf16[48,8,256]{2,1,0:T(8,128)(2,1)S(1)}, u32[]{:S(2)}, u32[]{:S(2)}) collective-permute-start(bf16[48,8,256]{2,1,0:T(8,128)(2,1)} %param.7), channel_id=1, source_target_pairs={{1,0},{2,1},{3,2},{4,3},{5,4},{6,5},{7,6},{8,7},{9,8},{10,9},{11,1... | collective-permute-start | bytes 589832 | tf_op jit(solution)/shard_map/ppermute | solution.py:79
  10.6 0.7 %fusion.68 = bf16[2,1,8,256]{3,2,1,0:T(8,128)(2,1)S(1)} fusion(bf16[1,48,8,256]{3,2,1,0:T(8,128)(2,1)} %bitcast.214, bf16[1,48,8,256]{3,2,1,0:T(8,128)(2,1)} %bitcast.217, pred[]{:T(512)S(6)} %eq.37), kind=kLoop, calls=%fused_computation.118 | loop fusion | flops 12288 | bytes 401409 | tf_op jit(solution)/shard_map/jit(_where)/select_n | solution.py:86
  11.4 1.9 %collective-permute-start = (bf16[2,1,8,256]{3,2,1,0:T(8,128)(2,1)S(1)}, bf16[2,1,8,256]{3,2,1,0:T(8,128)(2,1)S(1)}, u32[]{:S(2)}, u32[]{:S(2)}) collective-permute-start(bf16[2,1,8,256]{3,2,1,0:T(8,128)(2,1)S(1)} %fusion.68), channel_id=1, source_target_pairs={{0,16},{16,0},{1,17},{17,1},{2,18},{18,2},{3,19},{19,3},{4,20},{20... | collective-permute-start | bytes 24584 | tf_op jit(solution)/shard_map/ppermute | solution.py:86
  13.3 0.7 %slice_select_fusion.4 = bf16[2,8,256]{2,1,0:T(8,128)(2,1)S(1)} fusion(bf16[48,8,256]{2,1,0:T(8,128)(2,1)} %param.7, pred[]{:T(512)S(6)} %eq.37), kind=kLoop, calls=%fused_computation.119 | loop fusion | flops 4096 | bytes 24577 | tf_op jit(solution)/shard_map/jit(_where)/select_n | solution.py:102
  14.0 0.7 %slice_select_fusion.3 = bf16[3,8,256]{2,1,0:T(8,128)(2,1)S(1)} fusion(bf16[48,8,256]{2,1,0:T(8,128)(2,1)} %param.6, pred[]{:T(512)S(6)} %eq.37), kind=kLoop, calls=%fused_computation.109 | loop fusion | flops 6144 | bytes 36865 | tf_op jit(solution)/shard_map/jit(_where)/select_n | solution.py:100
  14.8 0.1 add_select_fusion
  14.8 0.1 add_select_fusion.1
  15.0 0.1 pad.103.clone
  15.0 0.0 collective-permute-done
  15.0 0.7 %slice.164 = bf16[4,1,1,128]{3,1,2,0:T(2,128)(2,1)S(1)} slice(bf16[4,4,3,128]{3,1,2,0:T(4,128)(2,1)} %param.10), slice={[0:4], [3:4], [1:2], [0:128]} | slice | bytes 2048 | tf_op jit(solution)/shard_map/slice | solution.py:130
  15.7 0.7 %copy.75 = bf16[4,4,3,128]{3,0,2,1:T(4,128)(2,1)S(1)} copy(bf16[4,4,3,128]{3,1,2,0:T(4,128)(2,1)} %param.10) | data formatting | bytes 24576 | tf_op jit(solution)/shard_map/optimization_barrier | solution.py:94
  16.6 0.8 %copy.71 = bf16[4,96,3,17]{1,3,2,0:T(8,128)(2,1)S(1)} copy(bf16[4,96,3,17]{1,0,3,2:T(4,128)(2,1)} %param.9) | data formatting | bytes 78336 | tf_op jit(solution)/shard_map/optimization_barrier | solution.py:94
  17.4 0.7 %pad_dynamic-slice_fusion = s32[50]{0:T(128)S(1)} fusion(s32[]{:T(128)S(6)} %select_n.181, s32[96]{0:T(128)} %param.11), kind=kLoop, calls=%fused_computation.160 | loop fusion | bytes 588 | tf_op jit(solution)/shard_map/dynamic_slice | solution.py:31
  18.1 0.1 compare_and_fusion
  18.2 0.1 dynamic-slice_select_fusion
  18.3 0.2 fusion.49
  18.5 0.4 fusion.12
  18.9 0.0 copy-start.2
  18.9 1.1 %copy.74 = bf16[48,4,8,3,24]{4,2,3,1,0:T(8,128)(2,1)S(1)} copy(bf16[48,4,8,3,24]{0,4,3,1,2:T(8,128)(2,1)S(1)} %fusion.12) | data formatting | bytes 442368 | tf_op jit(solution)/shard_map/convert_element_type | solution.py:24
  20.0 0.1 slice.171
  20.0 0.1 slice.167
  20.1 0.1 maximum_bitcast_fusion.12
  20.2 0.7 %broadcast_in_dim.25 = bf16[8,7,8,256]{3,2,1,0:T(8,128)(2,1)} broadcast(bf16[7,8,256]{2,1,0:T(8,128)(2,1)S(1)} %pad_maximum_fusion.2), dimensions={1,2,3} | broadcast | bytes 258048 | tf_op jit(solution)/shard_map/broadcast_in_dim | solution.py:107
  20.9 4.0 %all-to-all-start = ((bf16[8,7,8,256]{3,2,1,0:T(8,128)(2,1)}), bf16[8,7,8,256]{3,2,1,0:T(8,128)(2,1)}, u32[]{:S(2)}, u32[]{:S(2)}) async-start(bf16[8,7,8,256]{3,2,1,0:T(8,128)(2,1)} %broadcast_in_dim.25), calls=%async_computation | async-start | bytes 458752 | tf_op jit(solution)/shard_map/all_to_all | solution.py:107
  25.0 0.3 fusion.19
  25.3 0.0 collective-permute-done.1
  25.3 0.0 collective-permute-done.2
  25.3 0.0 copy-start.3
  25.4 0.0 copy-start.1
  25.4 0.1 slice_bitcast_fusion.3
  25.6 0.5 copy-done.3
  26.0 0.3 copy-done.1
  26.4 0.6 fusion
  27.0 0.0 copy-start.4
  27.0 0.5 fusion.11
  27.5 0.7 copy-done.5
  28.2 0.1 collective-permute-start.6
  28.3 0.1 broadcast_select_fusion.1
  28.5 1.1 %slice_bitcast_fusion.1 = (bf16[48,1,24,256]{3,2,0,1:T(8,128)(2,1)}, bf16[48,1,24,256]{3,2,0,1:T(8,128)(2,1)}) fusion(bf16[48,24,256]{2,1,0:T(8,128)(2,1)S(1)} %get-tuple-element.33), kind=kLoop, calls=%fused_computation.37 | loop fusion | bytes 1769472 | tf_op jit(solution)/shard_map/stack | solution.py:50
  29.5 3.4 %all-to-all-done = bf16[8,7,8,256]{3,2,1,0:T(8,128)(2,1)} async-done(((bf16[8,7,8,256]{3,2,1,0:T(8,128)(2,1)}), bf16[8,7,8,256]{3,2,1,0:T(8,128)(2,1)}, u32[]{:S(2)}, u32[]{:S(2)}) %all-to-all-start) | async-done | bytes 229408 | tf_op jit(solution)/shard_map/all_to_all | solution.py:107
  33.0 0.1 slice_select_fusion
  33.0 1.6 %collective-permute-done.5 = bf16[8,7,8,256]{3,2,1,0:T(8,128)(2,1)S(1)} collective-permute-done((bf16[8,7,8,256]{3,2,1,0:T(8,128)(2,1)}, bf16[8,7,8,256]{3,2,1,0:T(8,128)(2,1)S(1)}, u32[]{:S(2)}, u32[]{:S(2)}) %collective-permute-start.5) | collective-permute-done | bytes 229408 | tf_op jit(solution)/shard_map/ppermute | solution.py:108
  34.7 1.0 %select_bitcast_fusion.3 = (bf16[8,1,7,8,256]{4,3,2,1,0:T(8,128)(2,1)S(1)}, bf16[8,1,7,8,256]{4,3,2,1,0:T(8,128)(2,1)S(1)}) fusion(bf16[8,7,8,256]{3,2,1,0:T(8,128)(2,1)} %all-to-all-done, bf16[8,7,8,256]{3,2,1,0:T(8,128)(2,1)S(1)} %collective-permute-done.5, pred[]{:T(512)S(6)} %eq.42), kind=kLoop, calls=%fused_computation.57 | loop fusion | flops 229376 | bytes 917505 | tf_op jit(solution)/shard_map/stack | solution.py:109
  35.7 0.2 convolution_bitcast_fusion.4
  35.9 0.3 fusion.14
  36.2 0.8 %bitcast_add_fusion.2 = bf16[512,256]{1,0:T(8,128)(2,1)} fusion(f32[2,256,256]{2,1,0:T(8,128)S(1)} %fusion.14, f32[2,256,256]{2,1,0:T(8,128)S(1)} %slice_select_fusion, bf16[512,256]{1,0:T(8,128)(2,1)S(1)} %collective-permute-done.6), kind=kLoop, calls=%fused_computation.43 | loop fusion | flops 524288 | bytes 1572864 | tf_op jit(solution)/shard_map/add | solution.py:180
  37.0 0.1 fusion.88
  37.1 4.2 %all-to-all-start.1 = ((bf16[16,32,256]{2,1,0:T(8,128)(2,1)}), bf16[16,32,256]{2,1,0:T(8,128)(2,1)S(1)}, u32[]{:S(2)}, u32[]{:S(2)}) async-start(bf16[16,32,256]{2,1,0:T(8,128)(2,1)} %bitcast.85), calls=%async_computation.1 | async-start | bytes 524288 | tf_op jit(solution)/shard_map/all_to_all | solution.py:183
  41.3 0.2 fusion.20
  41.6 0.4 fusion.13
  42.0 9.6 %all-to-all-done.1 = bf16[16,32,256]{2,1,0:T(8,128)(2,1)S(1)} async-done(((bf16[16,32,256]{2,1,0:T(8,128)(2,1)}), bf16[16,32,256]{2,1,0:T(8,128)(2,1)S(1)}, u32[]{:S(2)}, u32[]{:S(2)}) %all-to-all-start.1) | async-done | bytes 262176 | tf_op jit(solution)/shard_map/all_to_all | solution.py:183
  51.6 0.7 %broadcast_in_dim.26 = bf16[16,32,256]{2,1,0:T(8,128)(2,1)} broadcast(bf16[32,256]{1,0:T(8,128)(2,1)S(1)} %reduce_sum.12), dimensions={1,2} | broadcast | bytes 278528 | tf_op jit(solution)/shard_map/broadcast_in_dim | solution.py:185
  52.3 3.5 %all-to-all-start.2 = ((bf16[16,32,256]{2,1,0:T(8,128)(2,1)}), bf16[16,32,256]{2,1,0:T(8,128)(2,1)S(1)}, u32[]{:S(2)}, u32[]{:S(2)}) async-start(bf16[16,32,256]{2,1,0:T(8,128)(2,1)} %broadcast_in_dim.26), calls=%async_computation.2 | async-start | bytes 524288 | tf_op jit(solution)/shard_map/all_to_all | solution.py:185
  55.9 0.2 convolution_bitcast_fusion.5
  56.1 1.1 %copy.89 = bf16[48,4,8,3,24]{4,2,3,1,0:T(8,128)(2,1)S(1)} copy(bf16[48,4,8,3,24]{0,4,3,1,2:T(8,128)(2,1)S(1)} %fusion.13) | data formatting | bytes 442368 | tf_op jit(solution)/shard_map/convert_element_type | solution.py:24
  57.2 2.8 %fusion.16 = bf16[48,8,256]{2,1,0:T(8,128)(2,1)} fusion(f32[4,1,8,256]{3,2,0,1:T(8,128)S(1)} %slice.217, f32[4,3,8,256]{3,2,0,1:T(8,128)S(1)} %slice.216, bf16[48,4,8,3,24]{4,2,3,1,0:T(8,128)(2,1)S(1)} %copy.89, pred[]{:T(512)S(6)} %eq.37, bf16[4,256,256]{2,1,0:T(8,128)(2,1)S(1)} %copy-done, bf16[48,1,24,256]{3,2,0,1:T(8,128)(2,1)} %get-tuple-element.24, ...), kind=kOutput, calls=%fused_computation.25 | convolution fusion | flops 261783552 | bytes 2842625 | tf_op jit(solution)/shard_map/kjbe,kce->jbc/dot_general | solution.py:20
  60.0 5.1 %all-to-all-done.2 = bf16[16,32,256]{2,1,0:T(8,128)(2,1)S(1)} async-done(((bf16[16,32,256]{2,1,0:T(8,128)(2,1)}), bf16[16,32,256]{2,1,0:T(8,128)(2,1)S(1)}, u32[]{:S(2)}, u32[]{:S(2)}) %all-to-all-start.2) | async-done | bytes 262176 | tf_op jit(solution)/shard_map/all_to_all | solution.py:185
  65.1 2.5 %fusion.15 = bf16[48,8,256]{2,1,0:T(8,128)(2,1)} fusion(f32[48,4,8,256,1]{3,2,4,1,0:T(8,128)} %copy-done.5, f32[4,1,8,256]{3,2,0,1:T(8,128)S(1)} %constant_dynamic-slice_fusion.1, f32[4,2,8,256]{3,2,0,1:T(8,128)S(1)} %constant_dynamic-slice_fusion, pred[]{:T(512)S(6)} %eq.37, bf16[4,256,256]{2,1,0:T(8,128)(2,1)S(1)} %copy-done), kind=kOutput, calls=%fused_computation.24 | convolution fusion | flops 203390976 | bytes 2392065 | tf_op jit(solution)/shard_map/kiac,kce->iae/dot_general | solution.py:20
  67.6 0.1 pad_maximum_fusion
  67.7 1.1 %convert.2 = f32[4,256,256]{2,1,0:T(8,128)} convert(bf16[4,256,256]{2,1,0:T(8,128)(2,1)S(1)} %bitcast.213) | non-fusion elementwise | flops 262144 | bytes 1572864 | tf_op jit(solution)/shard_map/convert_element_type | solution.py:188
  (43 shorter events, 0.5 us)
Async XLA Ops:
  0.6 56.5 %copy-start = (bf16[4,256,256]{2,1,0:T(8,128)(2,1)S(1)}, bf16[4,256,256]{2,1,0:T(8,128)(2,1)}, u32[]{:S(2)}) copy-start(bf16[4,256,256]{2,1,0:T(8,128)(2,1)} %param.8) | copy-start | bytes 1572868
  0.6 24.7 %collective-permute-start.1 = (bf16[48,8,256]{2,1,0:T(8,128)(2,1)}, bf16[48,8,256]{2,1,0:T(8,128)(2,1)S(1)}, u32[]{:S(2)}, u32[]{:S(2)}) collective-permute-start(bf16[48,8,256]{2,1,0:T(8,128)(2,1)} %param.6), channel_id=1, source_target_pairs={{0,1},{1,2},{2,3},{3,4},{4,5},{5,6},{6,7},{7,8},{8,9},{9,10},{10,1... | collective-permute-start | bytes 589832 | tf_op jit(solution)/shard_map/ppermute | solution.py:79
  1.1 24.2 %collective-permute-start.2 = (bf16[48,8,256]{2,1,0:T(8,128)(2,1)}, bf16[48,8,256]{2,1,0:T(8,128)(2,1)S(1)}, u32[]{:S(2)}, u32[]{:S(2)}) collective-permute-start(bf16[48,8,256]{2,1,0:T(8,128)(2,1)} %param.6), channel_id=1, source_target_pairs={{1,0},{2,1},{3,2},{4,3},{5,4},{6,5},{7,6},{8,7},{9,8},{10,9},{11,1... | collective-permute-start | bytes 589832 | tf_op jit(solution)/shard_map/ppermute | solution.py:79
  6.2 19.1 %collective-permute-start.3 = (bf16[48,8,256]{2,1,0:T(8,128)(2,1)}, bf16[48,8,256]{2,1,0:T(8,128)(2,1)S(1)}, u32[]{:S(2)}, u32[]{:S(2)}) collective-permute-start(bf16[48,8,256]{2,1,0:T(8,128)(2,1)} %param.7), channel_id=1, source_target_pairs={{0,1},{1,2},{2,3},{3,4},{4,5},{5,6},{6,7},{7,8},{8,9},{9,10},{10,1... | collective-permute-start | bytes 589832 | tf_op jit(solution)/shard_map/ppermute | solution.py:79
  6.2 19.2 %collective-permute-start.4 = (bf16[48,8,256]{2,1,0:T(8,128)(2,1)}, bf16[48,8,256]{2,1,0:T(8,128)(2,1)S(1)}, u32[]{:S(2)}, u32[]{:S(2)}) collective-permute-start(bf16[48,8,256]{2,1,0:T(8,128)(2,1)} %param.7), channel_id=1, source_target_pairs={{1,0},{2,1},{3,2},{4,3},{5,4},{6,5},{7,6},{8,7},{9,8},{10,9},{11,1... | collective-permute-start | bytes 589832 | tf_op jit(solution)/shard_map/ppermute | solution.py:79
  11.4 3.7 %collective-permute-start = (bf16[2,1,8,256]{3,2,1,0:T(8,128)(2,1)S(1)}, bf16[2,1,8,256]{3,2,1,0:T(8,128)(2,1)S(1)}, u32[]{:S(2)}, u32[]{:S(2)}) collective-permute-start(bf16[2,1,8,256]{3,2,1,0:T(8,128)(2,1)S(1)} %fusion.68), channel_id=1, source_target_pairs={{0,16},{16,0},{1,17},{17,1},{2,18},{18,2},{3,19},{19,3},{4,20},{20... | collective-permute-start | bytes 24584 | tf_op jit(solution)/shard_map/ppermute | solution.py:86
  18.9 6.5 %copy-start.2 = (bf16[48,8,256]{2,1,0:T(8,128)(2,1)S(1)}, bf16[48,8,256]{2,1,0:T(8,128)(2,1)}, u32[]{:S(2)}) copy-start(bf16[48,8,256]{2,1,0:T(8,128)(2,1)} %param.6) | copy-start | bytes 589828
  20.9 12.1 %all-to-all-start = ((bf16[8,7,8,256]{3,2,1,0:T(8,128)(2,1)}), bf16[8,7,8,256]{3,2,1,0:T(8,128)(2,1)}, u32[]{:S(2)}, u32[]{:S(2)}) async-start(bf16[8,7,8,256]{3,2,1,0:T(8,128)(2,1)} %broadcast_in_dim.25), calls=%async_computation | async-start | bytes 458752 | tf_op jit(solution)/shard_map/all_to_all | solution.py:107
  25.3 0.7 copy-start.3
  25.4 1.0 %copy-start.1 = (bf16[48,8,256]{2,1,0:T(8,128)(2,1)S(1)}, bf16[48,8,256]{2,1,0:T(8,128)(2,1)}, u32[]{:S(2)}) copy-start(bf16[48,8,256]{2,1,0:T(8,128)(2,1)} %param.7) | copy-start | bytes 589828
  27.0 1.2 %copy-start.5 = (f32[48,4,8,256,1]{3,2,4,1,0:T(8,128)}, f32[48,4,8,256,1]{3,2,4,1,0:T(8,128)S(1)}, u32[]{:S(2)}) copy-start(f32[48,4,8,256,1]{3,2,4,1,0:T(8,128)S(1)} %fusion) | copy-start | bytes 4718596
  27.0 1.3 %copy-start.4 = (bf16[48,8,256]{2,1,0:T(8,128)(2,1)S(1)}, bf16[48,8,256]{2,1,0:T(8,128)(2,1)}, u32[]{:S(2)}) copy-start(bf16[48,8,256]{2,1,0:T(8,128)(2,1)} %copy-done.3) | copy-start | bytes 589828
  28.2 8.0 %collective-permute-start.6 = (bf16[512,256]{1,0:T(8,128)(2,1)S(1)}, bf16[512,256]{1,0:T(8,128)(2,1)S(1)}, u32[]{:S(2)}, u32[]{:S(2)}) collective-permute-start(bf16[512,256]{1,0:T(8,128)(2,1)S(1)} %bitcast.220), channel_id=1, source_target_pairs={{0,1},{1,0},{2,3},{3,2},{4,5},{5,4},{6,7},{7,6},{8,9},{9,8},{10,11... | collective-permute-start | bytes 786440 | tf_op jit(solution)/shard_map/ppermute | solution.py:168
  33.0 1.7 %collective-permute-start.5 = (bf16[8,7,8,256]{3,2,1,0:T(8,128)(2,1)}, bf16[8,7,8,256]{3,2,1,0:T(8,128)(2,1)S(1)}, u32[]{:S(2)}, u32[]{:S(2)}) collective-permute-start(bf16[8,7,8,256]{3,2,1,0:T(8,128)(2,1)} %all-to-all-done), channel_id=1, source_target_pairs={{0,1},{1,0},{2,3},{3,2},{4,5},{5,4},{6,7},{7,6},{8,9},{9,8},{10,11... | collective-permute-start | bytes 688136 | tf_op jit(solution)/shard_map/ppermute | solution.py:108
  37.1 14.5 %all-to-all-start.1 = ((bf16[16,32,256]{2,1,0:T(8,128)(2,1)}), bf16[16,32,256]{2,1,0:T(8,128)(2,1)S(1)}, u32[]{:S(2)}, u32[]{:S(2)}) async-start(bf16[16,32,256]{2,1,0:T(8,128)(2,1)} %bitcast.85), calls=%async_computation.1 | async-start | bytes 524288 | tf_op jit(solution)/shard_map/all_to_all | solution.py:183
  52.3 12.7 %all-to-all-start.2 = ((bf16[16,32,256]{2,1,0:T(8,128)(2,1)}), bf16[16,32,256]{2,1,0:T(8,128)(2,1)S(1)}, u32[]{:S(2)}, u32[]{:S(2)}) async-start(bf16[16,32,256]{2,1,0:T(8,128)(2,1)} %broadcast_in_dim.26), calls=%async_computation.2 | async-start | bytes 524288 | tf_op jit(solution)/shard_map/all_to_all | solution.py:185
  65.1 2.5 %collective-permute-start.7 = (bf16[16,32,256]{2,1,0:T(8,128)(2,1)S(1)}, bf16[16,32,256]{2,1,0:T(8,128)(2,1)S(1)}, u32[]{:S(2)}, u32[]{:S(2)}) collective-permute-start(bf16[16,32,256]{2,1,0:T(8,128)(2,1)S(1)} %all-to-all-done.2), channel_id=1, source_target_pairs={{0,1},{1,0},{2,3},{3,2},{4,5},{5,4},{6,7},{7,6},{8,9},{9,8},{10,11... | collective-permute-start | bytes 786440 | tf_op jit(solution)/shard_map/ppermute | solution.py:186

commit v2 on v1

--- a/solution.py
+++ b/solution.py
@@ -68,7 +68,8 @@
     total_rows = lat_count * lat_devices
     first_row = lat_index * lat_count
     is_top = lat_index == 0
-    is_polar = is_top | (lat_index == lat_devices - 1)
+    is_bottom = lat_index == lat_devices - 1
+    is_polar = is_top | is_bottom
     swap = [(0, 1), (1, 0)]
     assert lon_count == H
 
@@ -78,39 +79,53 @@
     def sector_edges(field):
         return lax.ppermute(field, LON, to_right), lax.ppermute(field, LON, to_left)
 
+    def polar_slab(field, height):
+        return lax.dynamic_slice_in_dim(field, jnp.where(is_top, 0, lat_count - height), height, 0)
+
     signal_left, signal_right = sector_edges(signal)
 
-    both = jnp.stack([signal, cotangent])
-    first, last = both[:, :R], both[:, lat_count - R :]
+    polar_rows = jnp.concatenate([polar_slab(signal, SLAB), polar_slab(cotangent, P_SIZE)])
+    fill = jnp.zeros((SLAB + P_SIZE - 2 * R, lon_count, channels), signal.dtype)
+    first = jnp.concatenate([signal[:R], cotangent[:R], fill])
+    last = jnp.concatenate([signal[lat_count - R :], cotangent[lat_count - R :], fill])
+    target = jnp.arange(lat_devices, dtype=jnp.int32)[:, None, None, None]
+    chunks = jnp.where(target == lat_index, polar_rows[None], jnp.where(target > lat_index, last[None], first[None]))
+    sectors = lon_devices // 2
+    sent = jnp.broadcast_to(chunks[:, None], (lat_devices, sectors) + polar_rows.shape)
+    got = lax.all_to_all(sent.reshape((-1,) + polar_rows.shape), CHIPS, 0, 0).reshape(sent.shape)
+
+    def from_band(band):
+        return lax.dynamic_index_in_dim(got, band, 0, keepdims=False)
+
+    polar_got = from_band(lat_index)
     if lat_devices == 2:
-        edges = lax.ppermute(jnp.where(is_top, last, first), "lat", swap)
+        edges = [from_band(1 - lat_index)]
     else:
-        up = [(i, i + 1) for i in range(lat_devices - 1)]
-        down = [(j, i) for i, j in up]
-        edges = jnp.concatenate([lax.ppermute(last, "lat", up), lax.ppermute(first, "lat", down)], axis=1)
-    count = edges.shape[1]
-
-    cot_left, cot_right = sector_edges(cotangent)
-    edges, band_kernel, cycle_kernel, support_width = lax.optimization_barrier(
-        (edges, band_kernel, cycle_kernel, support_width)
-    )
-
-    slab = jnp.concatenate(
-        [
-            jnp.where(is_top, signal[:SLAB], signal[lat_count - SLAB :]),
-            edges[0],
-            jnp.where(is_top, cotangent[:P_SIZE], cotangent[lat_count - P_SIZE :]),
-            edges[1],
+        zero_edge = jnp.zeros_like(polar_got)
+        edges = [
+            jnp.where(is_top, zero_edge, from_band(jnp.maximum(lat_index - 1, 0))),
+            jnp.where(is_bottom, zero_edge, from_band(jnp.minimum(lat_index + 1, lat_devices - 1))),
         ]
-    )
-    sectors = lon_devices // 2
-    even = lax.all_to_all(jnp.broadcast_to(slab[None], (sectors,) + slab.shape), ("ring", "pair"), 0, 0)
-    odd = lax.ppermute(even, "core", swap)
+    count = len(edges)
+    if count == 1:
+        facing = jnp.where(is_top, cotangent[lat_count - R :], cotangent[:R])
+    else:
+        facing = jnp.concatenate([cotangent[:R], cotangent[lat_count - R :]])
+    even = jnp.concatenate(
+        [polar_got[:, :SLAB]] + [e[:, :R] for e in edges] + [polar_got[:, SLAB:]] + [e[:, R : 2 * R] for e in edges], axis=1
+    )
+    rows = even.shape[1]
+    swapped = lax.ppermute(jnp.concatenate([even.reshape((-1,) + even.shape[2:]), facing]), "core", swap)
+    odd = swapped[: sectors * rows].reshape(even.shape)
+    partner_facing = swapped[sectors * rows :]
     circle = jnp.stack([jnp.where(core == 0, even, odd), jnp.where(core == 0, odd, even)], axis=1)
-    circle = circle.reshape((lon_devices,) + slab.shape)
-    circle = jnp.moveaxis(circle, 0, 1).reshape(slab.shape[0], lon_total, channels)
+    circle = circle.reshape((lon_devices,) + even.shape[1:])
+    circle = jnp.moveaxis(circle, 0, 1).reshape(rows, lon_total, channels)
     signal_circle, cot_circle = circle[: SLAB + count], circle[SLAB + count :]
 
+    signal_left, signal_right, band_kernel, cycle_kernel, support_width, _ = lax.optimization_barrier(
+        (signal_left, signal_right, band_kernel, cycle_kernel, support_width, sent)
+    )
     coeffs = band_coefficients(band_kernel, support_width, first_row, total_rows, lat_count + 2 * R)
     forward = band_matrices(coeffs[:, R : R + lat_count], lon_count, True)
 
@@ -158,35 +173,28 @@
         out = jnp.where(is_top, rows(polar, 0), rows(polar, lat_count - polar_count))
         return out + rows(edge[:, :R], 0) + rows(edge[:, R:], lat_count - R)
 
-    left, right, _, _ = lax.optimization_barrier((signal_left, signal_right, cot_left, cot_right))
-    banded = dot("ikarm,irmc->ikac", forward, windows(left, signal, right))
+    banded = dot("ikarm,irmc->ikac", forward, windows(signal_left, signal, signal_right))
     banded = jnp.moveaxis(banded, 1, 0)
     scale = 1.0 / math.sqrt(total_rows * lon_total)
     partial = (dot("kiac,iae->kce", bf16(banded), cotangent) * scale).reshape(2, -1, channels)
     given = bf16(jnp.where(core == 0, partial[1], partial[0]))
     kept = jnp.where(core == 0, partial[0], partial[1])
+    given, late = lax.optimization_barrier((given, cotangent))
+    cot_left, cot_right = sector_edges(late)
     kept = kept + lax.ppermute(given, "core", swap).astype(jnp.float32)
 
     extra = dot("kpasm,smc->kpac", forward_cycle, signal_circle)
-    partner = jnp.where(core == 0, cot_right, cot_left)
-    chip_rows = jnp.concatenate([jnp.where(core == 0, cotangent, partner), jnp.where(core == 0, partner, cotangent)], axis=1)
-    polar_rows = jnp.where(is_top, chip_rows[:P_SIZE], chip_rows[lat_count - P_SIZE :])
-    if count == 1:
-        edge_rows = jnp.where(is_top, chip_rows[lat_count - R :], chip_rows[:R])
-    else:
-        edge_rows = jnp.concatenate([chip_rows[:R], chip_rows[lat_count - R :]])
+    chip_polar = lax.dynamic_slice_in_dim(cot_circle[:P_SIZE], chip * 2 * lon_count, 2 * lon_count, 1)
+    facing_pair = [jnp.where(core == 0, facing, partner_facing), jnp.where(core == 0, partner_facing, facing)]
+    chip_facing = jnp.concatenate(facing_pair, axis=1)
     kept_extra = lax.dynamic_slice_in_dim(bf16(extra), core * (K // 2), K // 2, 0)
-    extra_partial = dot("kpac,pae->kce", kept_extra, jnp.concatenate([polar_rows, edge_rows]))
+    extra_partial = dot("kpac,pae->kce", kept_extra, jnp.concatenate([chip_polar, chip_facing]))
     kept = kept + (extra_partial * scale).reshape(-1, channels)
 
     group = lat_devices * lon_devices // 2
     parts = lax.all_to_all(bf16(kept).reshape(group, -1, channels), CHIPS, 0, 0)
     chunk = bf16(jnp.sum(parts.astype(jnp.float32), axis=0))
     half = lax.all_to_all(jnp.broadcast_to(chunk[None], (group,) + chunk.shape), CHIPS, 0, 0)
-    other = lax.ppermute(half, "core", swap)
-    weight_grad = jnp.stack([jnp.where(core == 0, half, other), jnp.where(core == 0, other, half)])
-    weight_grad = weight_grad.reshape(K, channels, channels).astype(jnp.float32)
-
     coeffs, adjoint_kernel, extra, kept = lax.optimization_barrier((coeffs, adjoint_kernel, extra, kept))
     own_extra = lax.dynamic_slice_in_dim(extra, core * lon_count, lon_count, 2)
     filtered = bf16(banded + placed(own_extra, P_SIZE))
@@ -195,10 +203,15 @@
     adjoint_rows = jnp.stack([coeffs[:, t : t + lat_count, 2 * R - t] for t in range(TAPS)], axis=2)
     adjoint = band_matrices(adjoint_rows, lon_count, False)
     adjoint_cycle = bf16(dot("kspd,dbm->ksbpm", adjoint_kernel, bf16(opposite[None] == lags)))
+    cot_left, cot_right, _ = lax.optimization_barrier((cot_left, cot_right, chunk))
     spread = dot("ikarm,irme->ikae", adjoint, windows(cot_left, cotangent, cot_right))
     spread = jnp.moveaxis(spread, 1, 0)
     spread = spread + placed(dot("ksbpm,pme->ksbe", adjoint_cycle, cot_circle), SLAB)
     signal_grad = bf16(dot("kjbe,kce->jbc", bf16(spread), weights))
+    half, conv_output, signal_grad = lax.optimization_barrier((half, conv_output, signal_grad))
+    other = lax.ppermute(half, "core", swap)
+    weight_grad = jnp.stack([jnp.where(core == 0, half, other), jnp.where(core == 0, other, half)])
+    weight_grad = weight_grad.reshape(K, channels, channels).astype(jnp.float32)
     return conv_output, signal_grad, weight_grad
 
 

time: 69.6 us -> 60.6 us (0.87)
  waiting for transfers between devices: 19.8 us -> 14.3 us
  other arithmetic: 6.19 us -> 3.89 us
  starting transfers between devices: 23.7 us -> 23 us
    all_to_all x1, waiting for transfers between devices: 3.43 us -> 0.01 us  [local(): lax.all_to_all(sent.reshape((-1,) + polar_rows.shape), CHIPS, 0, 0)]
    all_to_all x1, waiting for transfers between devices: 9.62 us -> 6.33 us  [local(): parts = lax.all_to_all(bf16(kept).reshape(group, -1, channels), CHIPS, 0, 0)]
    select_n x7 -> x4, other arithmetic: 2.5 us -> 0.32 us  [the longest x1 0.18 us: local(): jnp.where(is_top, gives[1], gives[0])]
    ppermute x1, waiting for transfers between devices: 0.01 us -> 1.53 us  [local(): other = lax.ppermute(half, 'core', swap)]
    dynamic_slice x0 -> x3, local copies, waits for them, and re-layouts: none -> 1.42 us  [the longest x2 1.41 us: polar_slab(): lax.dynamic_slice_in_dim(field, jnp.where(is_top, 0, lat_count - height),...]
    ppermute x2 -> x1, starting transfers between devices: 1.93 us -> 0.56 us  [local(): lax.ppermute(jnp.concatenate([even.reshape((-1,) + even.shape[2:]), facin...]
    another operation x2 -> x1, other arithmetic: 1.04 us -> 0.05 us  [local(): jnp.stack([jnp.where(core == 0, even, odd), jnp.where(core == 0, odd, eve...]
    ppermute x2 -> x1, waiting for transfers between devices: 1.63 us -> 0.78 us  [local(): lax.ppermute(jnp.concatenate([even.reshape((-1,) + even.shape[2:]), facin...]
  transfers between devices with their start and end apart: 11 -> 10, of which waited for: 4 -> 4; matrix products, arithmetic and copies ran while one was open for 29% -> 32% of each run, Pallas kernels for 0% -> 0%
where the time goes in v2:
time: 60.6 us; the launch traced here: 59.9 us
  starting transfers between devices  23 us (38%)
  waiting for transfers between devices  14.3 us (24%)
  local copies, waits for them, and re-layouts  9.29 us (15%)
  matrix products  8.22 us (14%)
  other arithmetic  3.89 us (6%)
  between operations  1.23 us (2%)
    ppermute x2, starting transfers between devices, sector_edges(): lax.ppermute(field, LON, to_left)  9.46 us
    dot_general x11, matrix products, dot(): return jnp.einsum(spec, a, b, preferred_element_type=jnp.float32)  8.22 us
    all_to_all x1, waiting for transfers between devices, local(): parts = lax.all_to_all(bf16(kept).reshape(group, -1, channels), CHIPS, 0, 0)  6.33 us
    all_to_all x1, waiting for transfers between devices, local(): lax.all_to_all(jnp.broadcast_to(chunk[None], (group,) + chunk.shape), CHI...  5.63 us
    all_to_all x1, starting transfers between devices, local(): lax.all_to_all(sent.reshape((-1,) + polar_rows.shape), CHIPS, 0, 0)  4.57 us
    all_to_all x1, starting transfers between devices, local(): parts = lax.all_to_all(bf16(kept).reshape(group, -1, channels), CHIPS, 0, 0)  4.22 us
    all_to_all x1, starting transfers between devices, local(): lax.all_to_all(jnp.broadcast_to(chunk[None], (group,) + chunk.shape), CHI...  3.53 us
    convert_element_type x2, local copies, waits for them, and re-layouts, bf16(): return x.astype(jnp.bfloat16)  2.12 us
  transfers between devices with their start and end apart: 10, of which 4 were waited for; matrix products, arithmetic and copies ran while one was open for 32% of the time, Pallas kernels for 0%

profile of v2, /device:TPU:0, one launch (start us, length us, event | category | flops | bytes accessed | tf_op | source)
XLA Modules:
  0.0 59.9 jit_solution(6149253110410543049)
XLA Ops:
  0.6 0.0 copy-start
  0.7 0.5 collective-permute-start
  1.2 5.0 %collective-permute-start.1 = (bf16[48,8,256]{2,1,0:T(8,128)(2,1)}, bf16[48,8,256]{2,1,0:T(8,128)(2,1)S(1)}, u32[]{:S(2)}, u32[]{:S(2)}) collective-permute-start(bf16[48,8,256]{2,1,0:T(8,128)(2,1)} %param.6), channel_id=1, source_target_pairs={{1,0},{2,1},{3,2},{4,3},{5,4},{6,5},{7,6},{8,7},{9,8},{10,9},{11,1... | collective-permute-start | bytes 589832 | tf_op jit(solution)/shard_map/ppermute | solution.py:80
  6.2 0.7 %fusion.85 = (bf16[1,8,256]{2,1,0:T(8,128)(2,1)S(1)}, bf16[1,8,256]{2,1,0:T(8,128)(2,1)S(1)}) fusion(bf16[48,8,256]{2,1,0:T(8,128)(2,1)} %param.6), kind=kLoop, calls=%fused_computation.183 | loop fusion | bytes 16384 | tf_op jit(solution)/shard_map/slice | solution.py:90
  6.9 0.7 %fusion.86 = (bf16[1,8,256]{2,1,0:T(8,128)(2,1)S(1)}, bf16[1,8,256]{2,1,0:T(8,128)(2,1)S(1)}, bf16[1,8,256]{2,1,0:T(8,128)(2,1)S(1)}) fusion(bf16[48,8,256]{2,1,0:T(8,128)(2,1)} %param.7, pred[]{:T(512)S(6)} %eq.89), kind=kLoop, calls=%fused_computation.184 | loop fusion | flops 2048 | bytes 20481 | tf_op jit(solution)/shard_map/slice | solution.py:90
  7.6 0.7 %constant_dynamic-slice_fusion.3 = bf16[2,8,256]{2,1,0:T(8,128)(2,1)S(1)} fusion(bf16[48,8,256]{2,1,0:T(8,128)(2,1)} %param.7, s32[]{:T(128)S(6)} %select_n.192), kind=kLoop, calls=%fused_computation.149 | loop fusion | bytes 16388 | tf_op jit(solution)/shard_map/dynamic_slice | solution.py:83
  8.3 0.7 %constant_dynamic-slice_fusion.4 = bf16[3,8,256]{2,1,0:T(8,128)(2,1)S(1)} fusion(bf16[48,8,256]{2,1,0:T(8,128)(2,1)} %param.6, s32[]{:T(128)S(6)} %select_n.191), kind=kLoop, calls=%fused_computation.150 | loop fusion | bytes 24580 | tf_op jit(solution)/shard_map/dynamic_slice | solution.py:83
  9.0 0.1 pad.134.clone
  9.1 0.1 maximum_maximum_fusion
  9.2 0.1 select_select_fusion
  9.3 0.7 %broadcast_in_dim.68 = bf16[2,8,5,8,256]{4,3,2,1,0:T(8,128)(2,1)} broadcast(bf16[2,5,8,256]{3,2,1,0:T(8,128)(2,1)S(1)} %select_select_fusion), dimensions={0,2,3,4} | broadcast | bytes 368640 | tf_op jit(solution)/shard_map/broadcast_in_dim | solution.py:94
  10.0 4.6 %all-to-all-start = ((bf16[16,5,8,256]{3,2,1,0:T(8,128)(2,1)}), bf16[16,5,8,256]{3,2,1,0:T(8,128)(2,1)S(1)}, u32[]{:S(2)}, u32[]{:S(2)}) async-start(bf16[16,5,8,256]{3,2,1,0:T(8,128)(2,1)} %bitcast.37), calls=%async_computation | async-start | bytes 655360 | tf_op jit(solution)/shard_map/all_to_all | solution.py:95
  14.7 0.1 add_select_fusion
  14.8 0.1 pad.108.clone
  14.9 0.1 add_select_fusion.1
  15.0 0.0 collective-permute-done
  15.0 0.8 %copy.80 = bf16[4,96,3,17]{1,3,2,0:T(8,128)(2,1)S(1)} copy(bf16[4,96,3,17]{1,0,3,2:T(4,128)(2,1)} %param.9) | data formatting | bytes 78336 | tf_op jit(solution)/shard_map/optimization_barrier | solution.py:126
  15.8 0.0 copy-start.2
  15.8 0.1 pad_dynamic-slice_fusion
  15.9 0.1 compare_and_fusion
  16.0 0.1 dynamic-slice_select_fusion
  16.1 0.2 fusion.44
  16.3 0.4 fusion.13
  16.7 1.1 %copy.83 = bf16[48,4,8,3,24]{4,2,3,1,0:T(8,128)(2,1)S(1)} copy(bf16[48,4,8,3,24]{0,4,3,1,2:T(8,128)(2,1)S(1)} %fusion.13) | data formatting | bytes 442368 | tf_op jit(solution)/shard_map/convert_element_type | solution.py:24
  17.8 0.1 slice_bitcast_fusion.3
  17.9 0.0 copy-start.3
  17.9 0.6 %fusion = f32[48,4,8,256,1]{3,2,4,1,0:T(8,128)S(1)} fusion(bf16[48,4,8,3,24]{4,2,3,1,0:T(8,128)(2,1)S(1)} %copy.83, bf16[48,1,24,256]{3,2,1,0:T(8,128)(2,1)S(1)} %get-tuple-element.38, bf16[48,1,24,256]{3,2,1,0:T(8,128)(2,1)S(1)} %bitcast.236, bf16[48,1,24,256]{3,2,1,0:T(8,128)(2,1)S(1)} %get-tuple-element.37), kind=kOutput, calls=%fused_computation.1 | convolution fusion | flops 58392576 | bytes 3563520 | tf_op jit(solution)/shard_map/ikarm,irmc->ikac/dot_general | solution.py:20
  18.5 0.3 copy-done.3
  18.8 0.5 fusion.12
  19.3 0.7 %copy-done.6 = f32[48,4,8,256,1]{3,2,4,1,0:T(8,128)} copy-done((f32[48,4,8,256,1]{3,2,4,1,0:T(8,128)}, f32[48,4,8,256,1]{3,2,4,1,0:T(8,128)S(1)}, u32[]{:S(2)}) %copy-start.6) | copy-done | bytes 1572888
  20.1 0.1 collective-permute-start.4
  20.1 4.4 %collective-permute-start.5 = (bf16[48,8,256]{2,1,0:T(8,128)(2,1)S(1)}, bf16[48,8,256]{2,1,0:T(8,128)(2,1)S(1)}, u32[]{:S(2)}, u32[]{:S(2)}) collective-permute-start(bf16[48,8,256]{2,1,0:T(8,128)(2,1)S(1)} %copy-done.3), channel_id=1, source_target_pairs={{1,0},{2,1},{3,2},{4,3},{5,4},{6,5},{7,6},{8,7},{9,8},{10,9},{11,1... | collective-permute-start | bytes 589832 | tf_op jit(solution)/shard_map/ppermute | solution.py:80
  24.6 0.1 slice.188
  24.6 0.1 slice.174
  24.7 0.1 collective-permute-start.2
  24.8 0.1 maximum_bitcast_fusion.17
  25.0 0.1 slice_select_fusion
  25.3 0.6 collective-permute-start.3
  25.9 0.3 fusion.18
  26.2 0.8 %collective-permute-done.3 = bf16[57,8,256]{2,1,0:T(8,128)(2,1)S(1)} collective-permute-done((bf16[57,8,256]{2,1,0:T(8,128)(2,1)S(1)}, bf16[57,8,256]{2,1,0:T(8,128)(2,1)S(1)}, u32[]{:S(2)}, u32[]{:S(2)}) %collective-permute-start.3) | collective-permute-done | bytes 233504 | tf_op jit(solution)/shard_map/ppermute | solution.py:118
  27.0 0.1 broadcast_select_fusion.1
  27.2 0.2 convolution_bitcast_fusion.4
  27.4 0.3 fusion.15
  27.7 0.8 %bitcast_add_fusion.2 = bf16[512,256]{1,0:T(8,128)(2,1)} fusion(f32[2,256,256]{2,1,0:T(8,128)S(1)} %fusion.15, f32[2,256,256]{2,1,0:T(8,128)S(1)} %slice_select_fusion, bf16[512,256]{1,0:T(8,128)(2,1)S(1)} %collective-permute-done.2), kind=kLoop, calls=%fused_computation.46 | loop fusion | flops 524288 | bytes 1572864 | tf_op jit(solution)/shard_map/add | solution.py:192
  28.5 0.2 fusion.19
  28.7 0.2 convolution_bitcast_fusion.5
  28.9 0.0 copy-start.1
  28.9 4.2 %all-to-all-start.1 = ((bf16[16,32,256]{2,1,0:T(8,128)(2,1)}), bf16[16,32,256]{2,1,0:T(8,128)(2,1)S(1)}, u32[]{:S(2)}, u32[]{:S(2)}) async-start(bf16[16,32,256]{2,1,0:T(8,128)(2,1)} %bitcast.62), calls=%async_computation.1 | async-start | bytes 524288 | tf_op jit(solution)/shard_map/all_to_all | solution.py:195
  33.2 0.1 fusion.87
  33.3 0.4 fusion.14
  33.6 1.1 %copy.101 = bf16[48,4,8,3,24]{4,2,3,1,0:T(8,128)(2,1)S(1)} copy(bf16[48,4,8,3,24]{0,4,3,1,2:T(8,128)(2,1)S(1)} %fusion.14) | data formatting | bytes 442368 | tf_op jit(solution)/shard_map/convert_element_type | solution.py:24
  34.8 2.5 %fusion.16 = bf16[48,8,256]{2,1,0:T(8,128)(2,1)} fusion(f32[48,4,8,256,1]{3,2,4,1,0:T(8,128)} %copy-done.6, f32[4,1,8,256]{3,2,0,1:T(8,128)S(1)} %constant_dynamic-slice_fusion.1, f32[4,2,8,256]{3,2,0,1:T(8,128)S(1)} %constant_dynamic-slice_fusion, pred[]{:T(512)S(6)} %eq.89, bf16[4,256,256]{2,1,0:T(8,128)(2,1)S(1)} %copy-done), kind=kOutput, calls=%fused_computation.27 | convolution fusion | flops 203390976 | bytes 2392065 | tf_op jit(solution)/shard_map/kiac,kce->iae/dot_general | solution.py:20
  37.2 6.3 %all-to-all-done.1 = bf16[16,32,256]{2,1,0:T(8,128)(2,1)S(1)} async-done(((bf16[16,32,256]{2,1,0:T(8,128)(2,1)}), bf16[16,32,256]{2,1,0:T(8,128)(2,1)S(1)}, u32[]{:S(2)}, u32[]{:S(2)}) %all-to-all-start.1) | async-done | bytes 262176 | tf_op jit(solution)/shard_map/all_to_all | solution.py:195
  43.6 0.7 %broadcast_in_dim.107 = bf16[16,32,256]{2,1,0:T(8,128)(2,1)} broadcast(bf16[32,256]{1,0:T(8,128)(2,1)S(1)} %reduce_sum.12), dimensions={1,2} | broadcast | bytes 278528 | tf_op jit(solution)/shard_map/broadcast_in_dim | solution.py:197
  44.3 3.5 %all-to-all-start.2 = ((bf16[16,32,256]{2,1,0:T(8,128)(2,1)}), bf16[16,32,256]{2,1,0:T(8,128)(2,1)S(1)}, u32[]{:S(2)}, u32[]{:S(2)}) async-start(bf16[16,32,256]{2,1,0:T(8,128)(2,1)} %broadcast_in_dim.107), calls=%async_computation.2 | async-start | bytes 524288 | tf_op jit(solution)/shard_map/all_to_all | solution.py:197
  47.9 0.0 slice-start
  47.9 0.0 slice-start.1
  48.0 0.9 %slice_bitcast_fusion.1 = (bf16[48,1,24,256]{3,2,1,0:T(8,128)(2,1)S(1)}, bf16[48,1,24,256]{3,2,1,0:T(8,128)(2,1)}) fusion(bf16[48,24,256]{2,1,0:T(8,128)(2,1)S(1)} %constant_dynamic-update-slice_fusion.3), kind=kLoop, calls=%fused_computation.40 | loop fusion | bytes 1769472 | tf_op jit(solution)/shard_map/stack | solution.py:50
  48.9 2.7 %fusion.17 = bf16[48,8,256]{2,1,0:T(8,128)(2,1)} fusion(f32[4,1,8,256]{3,2,0,1:T(8,128)S(1)} %slice-done, f32[4,3,8,256]{3,2,0,1:T(8,128)S(1)} %slice-done.1, bf16[48,4,8,3,24]{4,2,3,1,0:T(8,128)(2,1)S(1)} %copy.101, bf16[48,1,24,256]{3,2,1,0:T(8,128)(2,1)} %get-tuple-element.36, bf16[48,1,24,256]{3,2,1,0:T(8,128)(2,1)S(1)} %bitcast.237, ...), kind=kOutput, calls=%fused_computation.28 | convolution fusion | flops 261783552 | bytes 2842625 | tf_op jit(solution)/shard_map/kjbe,kce->jbc/dot_general | solution.py:20
  51.5 5.6 %all-to-all-done.2 = bf16[16,32,256]{2,1,0:T(8,128)(2,1)S(1)} async-done(((bf16[16,32,256]{2,1,0:T(8,128)(2,1)}), bf16[16,32,256]{2,1,0:T(8,128)(2,1)S(1)}, u32[]{:S(2)}, u32[]{:S(2)}) %all-to-all-start.2) | async-done | bytes 262176 | tf_op jit(solution)/shard_map/all_to_all | solution.py:197
  57.2 1.5 %collective-permute-done.6 = bf16[16,32,256]{2,1,0:T(8,128)(2,1)S(1)} collective-permute-done((bf16[16,32,256]{2,1,0:T(8,128)(2,1)S(1)}, bf16[16,32,256]{2,1,0:T(8,128)(2,1)S(1)}, u32[]{:S(2)}, u32[]{:S(2)}) %collective-permute-start.6) | collective-permute-done | bytes 262176 | tf_op jit(solution)/shard_map/ppermute | solution.py:212
  58.7 0.1 select_bitcast_fusion.1
  58.8 0.1 pad_maximum_fusion
  58.8 1.1 %convert.2 = f32[4,256,256]{2,1,0:T(8,128)} convert(bf16[4,256,256]{2,1,0:T(8,128)(2,1)S(1)} %bitcast.234) | non-fusion elementwise | flops 262144 | bytes 1572864 | tf_op jit(solution)/shard_map/convert_element_type | solution.py:214
  (60 shorter events, 0.6 us)
Async XLA Ops:
  0.6 34.1 %copy-start = (bf16[4,256,256]{2,1,0:T(8,128)(2,1)S(1)}, bf16[4,256,256]{2,1,0:T(8,128)(2,1)}, u32[]{:S(2)}) copy-start(bf16[4,256,256]{2,1,0:T(8,128)(2,1)} %param.8) | copy-start | bytes 1572868
  0.6 15.2 %copy-start.5 = (s32[96]{0:T(128)S(1)}, s32[96]{0:T(128)}, u32[]{:S(2)}) copy-start(s32[96]{0:T(128)} %param.11) | copy-start | bytes 1156
  0.7 14.3 %collective-permute-start = (bf16[48,8,256]{2,1,0:T(8,128)(2,1)}, bf16[48,8,256]{2,1,0:T(8,128)(2,1)S(1)}, u32[]{:S(2)}, u32[]{:S(2)}) collective-permute-start(bf16[48,8,256]{2,1,0:T(8,128)(2,1)} %param.6), channel_id=1, source_target_pairs={{0,1},{1,2},{2,3},{3,4},{4,5},{5,6},{6,7},{7,8},{8,9},{9,10},{10,1... | collective-permute-start | bytes 589832 | tf_op jit(solution)/shard_map/ppermute | solution.py:80
  1.2 13.8 %collective-permute-start.1 = (bf16[48,8,256]{2,1,0:T(8,128)(2,1)}, bf16[48,8,256]{2,1,0:T(8,128)(2,1)S(1)}, u32[]{:S(2)}, u32[]{:S(2)}) collective-permute-start(bf16[48,8,256]{2,1,0:T(8,128)(2,1)} %param.6), channel_id=1, source_target_pairs={{1,0},{2,1},{3,2},{4,3},{5,4},{6,5},{7,6},{8,7},{9,8},{10,9},{11,1... | collective-permute-start | bytes 589832 | tf_op jit(solution)/shard_map/ppermute | solution.py:80
  10.0 15.1 %all-to-all-start = ((bf16[16,5,8,256]{3,2,1,0:T(8,128)(2,1)}), bf16[16,5,8,256]{3,2,1,0:T(8,128)(2,1)S(1)}, u32[]{:S(2)}, u32[]{:S(2)}) async-start(bf16[16,5,8,256]{3,2,1,0:T(8,128)(2,1)} %bitcast.37), calls=%async_computation | async-start | bytes 655360 | tf_op jit(solution)/shard_map/all_to_all | solution.py:95
  15.8 2.0 %copy-start.2 = (bf16[48,8,256]{2,1,0:T(8,128)(2,1)S(1)}, bf16[48,8,256]{2,1,0:T(8,128)(2,1)}, u32[]{:S(2)}) copy-start(bf16[48,8,256]{2,1,0:T(8,128)(2,1)} %param.6) | copy-start | bytes 589828
  17.9 0.9 %copy-start.3 = (bf16[48,8,256]{2,1,0:T(8,128)(2,1)S(1)}, bf16[48,8,256]{2,1,0:T(8,128)(2,1)}, u32[]{:S(2)}) copy-start(bf16[48,8,256]{2,1,0:T(8,128)(2,1)} %param.7) | copy-start | bytes 589828
  18.8 1.2 %copy-start.6 = (f32[48,4,8,256,1]{3,2,4,1,0:T(8,128)}, f32[48,4,8,256,1]{3,2,4,1,0:T(8,128)S(1)}, u32[]{:S(2)}) copy-start(f32[48,4,8,256,1]{3,2,4,1,0:T(8,128)S(1)} %fusion) | copy-start | bytes 4718596
  18.8 5.9 %copy-start.4 = (bf16[4,4,3,128]{3,1,2,0:T(4,128)(2,1)S(1)}, bf16[4,4,3,128]{3,1,2,0:T(4,128)(2,1)}, u32[]{:S(2)}) copy-start(bf16[4,4,3,128]{3,1,2,0:T(4,128)(2,1)} %param.10) | copy-start | bytes 36868
  20.1 27.8 %collective-permute-start.4 = (bf16[48,8,256]{2,1,0:T(8,128)(2,1)S(1)}, bf16[48,8,256]{2,1,0:T(8,128)(2,1)S(1)}, u32[]{:S(2)}, u32[]{:S(2)}) collective-permute-start(bf16[48,8,256]{2,1,0:T(8,128)(2,1)S(1)} %copy-done.3), channel_id=1, source_target_pairs={{0,1},{1,2},{2,3},{3,4},{4,5},{5,6},{6,7},{7,8},{8,9},{9,10},{10,1... | collective-permute-start | bytes 589832 | tf_op jit(solution)/shard_map/ppermute | solution.py:80
  20.1 27.8 %collective-permute-start.5 = (bf16[48,8,256]{2,1,0:T(8,128)(2,1)S(1)}, bf16[48,8,256]{2,1,0:T(8,128)(2,1)S(1)}, u32[]{:S(2)}, u32[]{:S(2)}) collective-permute-start(bf16[48,8,256]{2,1,0:T(8,128)(2,1)S(1)} %copy-done.3), channel_id=1, source_target_pairs={{1,0},{2,1},{3,2},{4,3},{5,4},{6,5},{7,6},{8,7},{9,8},{10,9},{11,1... | collective-permute-start | bytes 589832 | tf_op jit(solution)/shard_map/ppermute | solution.py:80
  24.7 2.9 %collective-permute-start.2 = (bf16[512,256]{1,0:T(8,128)(2,1)S(1)}, bf16[512,256]{1,0:T(8,128)(2,1)S(1)}, u32[]{:S(2)}, u32[]{:S(2)}) collective-permute-start(bf16[512,256]{1,0:T(8,128)(2,1)S(1)} %bitcast.240), channel_id=1, source_target_pairs={{0,1},{1,0},{2,3},{3,2},{4,5},{5,4},{6,7},{7,6},{8,9},{9,8},{10,11... | collective-permute-start | bytes 786440 | tf_op jit(solution)/shard_map/ppermute | solution.py:184
  25.3 1.7 %collective-permute-start.3 = (bf16[57,8,256]{2,1,0:T(8,128)(2,1)S(1)}, bf16[57,8,256]{2,1,0:T(8,128)(2,1)S(1)}, u32[]{:S(2)}, u32[]{:S(2)}) collective-permute-start(bf16[57,8,256]{2,1,0:T(8,128)(2,1)S(1)} %pad_maximum_fusion.2), channel_id=1, source_target_pairs={{0,1},{1,0},{2,3},{3,2},{4,5},{5,4},{6,7},{7,6},{8,9},{9,8},{10,11... | collective-permute-start | bytes 700424 | tf_op jit(solution)/shard_map/ppermute | solution.py:118
  28.9 5.8 %copy-start.1 = (f32[4,4,8,256]{3,2,0,1:T(8,128)}, f32[4,4,8,256]{3,2,0,1:T(8,128)S(1)}, u32[]{:S(2)}) copy-start(f32[4,4,8,256]{3,2,0,1:T(8,128)S(1)} %convolution_bitcast_fusion.5) | copy-start | bytes 393220
  28.9 14.6 %all-to-all-start.1 = ((bf16[16,32,256]{2,1,0:T(8,128)(2,1)}), bf16[16,32,256]{2,1,0:T(8,128)(2,1)S(1)}, u32[]{:S(2)}, u32[]{:S(2)}) async-start(bf16[16,32,256]{2,1,0:T(8,128)(2,1)} %bitcast.62), calls=%async_computation.1 | async-start | bytes 524288 | tf_op jit(solution)/shard_map/all_to_all | solution.py:195
  44.3 12.9 %all-to-all-start.2 = ((bf16[16,32,256]{2,1,0:T(8,128)(2,1)}), bf16[16,32,256]{2,1,0:T(8,128)(2,1)S(1)}, u32[]{:S(2)}, u32[]{:S(2)}) async-start(bf16[16,32,256]{2,1,0:T(8,128)(2,1)} %broadcast_in_dim.107), calls=%async_computation.2 | async-start | bytes 524288 | tf_op jit(solution)/shard_map/all_to_all | solution.py:197
  47.9 1.0 %slice-start = ((f32[4,4,8,256]{3,2,0,1:T(8,128)}), f32[4,1,8,256]{3,2,0,1:T(8,128)S(1)}, s32[]{:S(2)}) async-start(f32[4,4,8,256]{3,2,0,1:T(8,128)} %copy-done.1), calls=%async_computation.3 | async-start | bytes 65536 | tf_op jit(solution)/shard_map/slice | solution.py:162
  47.9 1.0 %slice-start.1 = ((f32[4,4,8,256]{3,2,0,1:T(8,128)}), f32[4,3,8,256]{3,2,0,1:T(8,128)S(1)}, s32[]{:S(2)}) async-start(f32[4,4,8,256]{3,2,0,1:T(8,128)} %copy-done.1), calls=%async_computation.4 | async-start | bytes 196608 | tf_op jit(solution)/shard_map/slice | solution.py:162
  57.2 1.5 %collective-permute-start.6 = (bf16[16,32,256]{2,1,0:T(8,128)(2,1)S(1)}, bf16[16,32,256]{2,1,0:T(8,128)(2,1)S(1)}, u32[]{:S(2)}, u32[]{:S(2)}) collective-permute-start(bf16[16,32,256]{2,1,0:T(8,128)(2,1)S(1)} %all-to-all-done.2), channel_id=1, source_target_pairs={{0,1},{1,0},{2,3},{3,2},{4,5},{5,4},{6,7},{7,6},{8,9},{9,8},{10,11... | collective-permute-start | bytes 786440 | tf_op jit(solution)/shard_map/ppermute | solution.py:212

commit v3 on v2

--- a/solution.py
+++ b/solution.py
@@ -83,11 +83,12 @@
         return lax.dynamic_slice_in_dim(field, jnp.where(is_top, 0, lat_count - height), height, 0)
 
     signal_left, signal_right = sector_edges(signal)
-
-    polar_rows = jnp.concatenate([polar_slab(signal, SLAB), polar_slab(cotangent, P_SIZE)])
+    both = lax.optimization_barrier(jnp.stack([signal, cotangent]))
+
+    polar_rows = jnp.concatenate([polar_slab(both[0], SLAB), polar_slab(both[1], P_SIZE)])
     fill = jnp.zeros((SLAB + P_SIZE - 2 * R, lon_count, channels), signal.dtype)
-    first = jnp.concatenate([signal[:R], cotangent[:R], fill])
-    last = jnp.concatenate([signal[lat_count - R :], cotangent[lat_count - R :], fill])
+    first = jnp.concatenate([both[0, :R], both[1, :R], fill])
+    last = jnp.concatenate([both[0, lat_count - R :], both[1, lat_count - R :], fill])
     target = jnp.arange(lat_devices, dtype=jnp.int32)[:, None, None, None]
     chunks = jnp.where(target == lat_index, polar_rows[None], jnp.where(target > lat_index, last[None], first[None]))
     sectors = lon_devices // 2
@@ -108,9 +109,9 @@
         ]
     count = len(edges)
     if count == 1:
-        facing = jnp.where(is_top, cotangent[lat_count - R :], cotangent[:R])
+        facing = jnp.where(is_top, both[1, lat_count - R :], both[1, :R])
     else:
-        facing = jnp.concatenate([cotangent[:R], cotangent[lat_count - R :]])
+        facing = jnp.concatenate([both[1, :R], both[1, lat_count - R :]])
     even = jnp.concatenate(
         [polar_got[:, :SLAB]] + [e[:, :R] for e in edges] + [polar_got[:, SLAB:]] + [e[:, R : 2 * R] for e in edges], axis=1
     )
@@ -123,8 +124,8 @@
     circle = jnp.moveaxis(circle, 0, 1).reshape(rows, lon_total, channels)
     signal_circle, cot_circle = circle[: SLAB + count], circle[SLAB + count :]
 
-    signal_left, signal_right, band_kernel, cycle_kernel, support_width, _ = lax.optimization_barrier(
-        (signal_left, signal_right, band_kernel, cycle_kernel, support_width, sent)
+    band_kernel, cycle_kernel, support_width, _ = lax.optimization_barrier(
+        (band_kernel, cycle_kernel, support_width, sent)
     )
     coeffs = band_coefficients(band_kernel, support_width, first_row, total_rows, lat_count + 2 * R)
     forward = band_matrices(coeffs[:, R : R + lat_count], lon_count, True)
@@ -149,6 +150,30 @@
         jnp.stack([jnp.stack(row, axis=1) for row in low_rows], axis=1),
     )
     slab_kernel = jnp.where(is_polar, slab_kernel, jnp.zeros_like(slab_kernel))
+    def placed(extra, polar_count):
+        polar, edge = extra[:, :polar_count], extra[:, polar_count:]
+
+        def rows(block, before):
+            return jnp.pad(block, ((0, 0), (before, lat_count - block.shape[1] - before), (0, 0), (0, 0)))
+
+        if count == 1:
+            return jnp.where(
+                is_top,
+                rows(polar, 0) + rows(edge, lat_count - R),
+                rows(polar, lat_count - polar_count) + rows(edge, 0),
+            )
+        out = jnp.where(is_top, rows(polar, 0), rows(polar, lat_count - polar_count))
+        return out + rows(edge[:, :R], 0) + rows(edge[:, R:], lat_count - R)
+
+    banded = dot("ikarm,irmc->ikac", forward, windows(signal_left, signal, signal_right))
+    banded = bf16(jnp.moveaxis(banded, 1, 0))
+    scale = 1.0 / math.sqrt(total_rows * lon_total)
+    partial = (dot("kiac,iae->kce", banded, cotangent) * scale).reshape(2, -1, channels)
+    given = bf16(jnp.where(core == 0, partial[1], partial[0]))
+    kept = jnp.where(core == 0, partial[0], partial[1])
+    kept = kept + lax.ppermute(given, "core", swap).astype(jnp.float32)
+
+    slab_kernel, edge_forward, edge_adjoint, _ = lax.optimization_barrier((slab_kernel, edge_forward, edge_adjoint, given))
     lags = jnp.arange(lon_total, dtype=jnp.int32)[:, None, None]
     own_lons = lon_index * lon_count + jnp.arange(lon_count, dtype=jnp.int32)
     chip_lons = chip * 2 * lon_count + jnp.arange(2 * lon_count, dtype=jnp.int32)
@@ -158,30 +183,6 @@
     forward_cycle = bf16(dot("kpsd,dam->kpasm", block_diagonal(slab_kernel, edge_forward), bf16(distance[None] == lags)))
     adjoint_kernel = block_diagonal(jnp.swapaxes(slab_kernel, 1, 2), edge_adjoint)
 
-    def placed(extra, polar_count):
-        polar, edge = extra[:, :polar_count], extra[:, polar_count:]
-
-        def rows(block, before):
-            return jnp.pad(block, ((0, 0), (before, lat_count - block.shape[1] - before), (0, 0), (0, 0)))
-
-        if count == 1:
-            return jnp.where(
-                is_top,
-                rows(polar, 0) + rows(edge, lat_count - R),
-                rows(polar, lat_count - polar_count) + rows(edge, 0),
-            )
-        out = jnp.where(is_top, rows(polar, 0), rows(polar, lat_count - polar_count))
-        return out + rows(edge[:, :R], 0) + rows(edge[:, R:], lat_count - R)
-
-    banded = dot("ikarm,irmc->ikac", forward, windows(signal_left, signal, signal_right))
-    banded = jnp.moveaxis(banded, 1, 0)
-    scale = 1.0 / math.sqrt(total_rows * lon_total)
-    partial = (dot("kiac,iae->kce", bf16(banded), cotangent) * scale).reshape(2, -1, channels)
-    given = bf16(jnp.where(core == 0, partial[1], partial[0]))
-    kept = jnp.where(core == 0, partial[0], partial[1])
-    given, late = lax.optimization_barrier((given, cotangent))
-    cot_left, cot_right = sector_edges(late)
-    kept = kept + lax.ppermute(given, "core", swap).astype(jnp.float32)
 
     extra = dot("kpasm,smc->kpac", forward_cycle, signal_circle)
     chip_polar = lax.dynamic_slice_in_dim(cot_circle[:P_SIZE], chip * 2 * lon_count, 2 * lon_count, 1)
@@ -195,7 +196,8 @@
     parts = lax.all_to_all(bf16(kept).reshape(group, -1, channels), CHIPS, 0, 0)
     chunk = bf16(jnp.sum(parts.astype(jnp.float32), axis=0))
     half = lax.all_to_all(jnp.broadcast_to(chunk[None], (group,) + chunk.shape), CHIPS, 0, 0)
-    coeffs, adjoint_kernel, extra, kept = lax.optimization_barrier((coeffs, adjoint_kernel, extra, kept))
+    coeffs, adjoint_kernel, extra, late, kept = lax.optimization_barrier((coeffs, adjoint_kernel, extra, cotangent, kept))
+    cot_left, cot_right = sector_edges(late)
     own_extra = lax.dynamic_slice_in_dim(extra, core * lon_count, lon_count, 2)
     filtered = bf16(banded + placed(own_extra, P_SIZE))
     conv_output = bf16(dot("kiac,kce->iae", filtered, weights))
@@ -203,7 +205,6 @@
     adjoint_rows = jnp.stack([coeffs[:, t : t + lat_count, 2 * R - t] for t in range(TAPS)], axis=2)
     adjoint = band_matrices(adjoint_rows, lon_count, False)
     adjoint_cycle = bf16(dot("kspd,dbm->ksbpm", adjoint_kernel, bf16(opposite[None] == lags)))
-    cot_left, cot_right, _ = lax.optimization_barrier((cot_left, cot_right, chunk))
     spread = dot("ikarm,irme->ikae", adjoint, windows(cot_left, cotangent, cot_right))
     spread = jnp.moveaxis(spread, 1, 0)
     spread = spread + placed(dot("ksbpm,pme->ksbe", adjoint_cycle, cot_circle), SLAB)

time: 60.6 us -> 60.9 us (level)
  starting transfers between devices: 23 us -> 21.3 us
  other arithmetic: 3.89 us -> 5.56 us
  waiting for transfers between devices: 14.3 us -> 15.1 us
    all_to_all x1, waiting for transfers between devices: 6.33 us -> 3.3 us  [local(): parts = lax.all_to_all(bf16(kept).reshape(group, -1, channels), CHIPS, 0, 0)]
    all_to_all x1, waiting for transfers between devices: 0.01 us -> 2.2 us  [local(): lax.all_to_all(sent.reshape((-1,) + polar_rows.shape), CHIPS, 0, 0)]
    ppermute x2, starting transfers between devices: 9.46 us -> 7.59 us  [sector_edges(): lax.ppermute(field, LON, to_left)]
    unnamed x19 -> x21, local copies, waits for them, and re-layouts: 1.07 us -> 2.58 us
    dynamic_slice x2, local copies, waits for them, and re-layouts: 1.41 us -> 0.01 us  [polar_slab(): lax.dynamic_slice_in_dim(field, jnp.where(is_top, 0, lat_count - height),...]
    all_to_all x1, waiting for transfers between devices: 5.63 us -> 6.7 us  [local(): lax.all_to_all(jnp.broadcast_to(chunk[None], (group,) + chunk.shape), CHI...]
    another operation x0 -> x1, other arithmetic: none -> 1.06 us  [local(): both = lax.optimization_barrier(jnp.stack([signal, cotangent]))]
    all_to_all x1, starting transfers between devices: 3.53 us -> 4.53 us  [local(): lax.all_to_all(jnp.broadcast_to(chunk[None], (group,) + chunk.shape), CHI...]
  transfers between devices with their start and end apart: 10 -> 10, of which waited for: 4 -> 6; matrix products, arithmetic and copies ran while one was open for 32% -> 31% of each run, Pallas kernels for 0% -> 0%
where the time goes in v3:
time: 60.9 us; the launch traced here: 60.3 us
  starting transfers between devices  21.3 us (35%)
  waiting for transfers between devices  15.1 us (25%)
  local copies, waits for them, and re-layouts  8.97 us (15%)
  matrix products  8.01 us (13%)
  other arithmetic  5.56 us (9%)
  between operations  1.27 us (2%)
    dot_general x11, matrix products, dot(): return jnp.einsum(spec, a, b, preferred_element_type=jnp.float32)  8.01 us
    ppermute x2, starting transfers between devices, sector_edges(): lax.ppermute(field, LON, to_left)  7.59 us
    all_to_all x1, waiting for transfers between devices, local(): lax.all_to_all(jnp.broadcast_to(chunk[None], (group,) + chunk.shape), CHI...  6.7 us
    all_to_all x1, starting transfers between devices, local(): lax.all_to_all(sent.reshape((-1,) + polar_rows.shape), CHIPS, 0, 0)  4.57 us
    all_to_all x1, starting transfers between devices, local(): lax.all_to_all(jnp.broadcast_to(chunk[None], (group,) + chunk.shape), CHI...  4.53 us
    all_to_all x1, starting transfers between devices, local(): parts = lax.all_to_all(bf16(kept).reshape(group, -1, channels), CHIPS, 0, 0)  3.54 us
    all_to_all x1, waiting for transfers between devices, local(): parts = lax.all_to_all(bf16(kept).reshape(group, -1, channels), CHIPS, 0, 0)  3.3 us
    unnamed x21, local copies, waits for them, and re-layouts  2.58 us
  transfers between devices with their start and end apart: 10, of which 6 were waited for; matrix products, arithmetic and copies ran while one was open for 31% of the time, Pallas kernels for 0%

profile of v3, /device:TPU:0, one launch (start us, length us, event | category | flops | bytes accessed | tf_op | source)
XLA Modules:
  0.0 60.3 jit_solution(16420213437913551057)
XLA Ops:
  0.6 0.0 copy-start
  0.6 0.5 collective-permute-start
  1.2 5.0 %collective-permute-start.1 = (bf16[48,8,256]{2,1,0:T(8,128)(2,1)}, bf16[48,8,256]{2,1,0:T(8,128)(2,1)S(1)}, u32[]{:S(2)}, u32[]{:S(2)}) collective-permute-start(bf16[48,8,256]{2,1,0:T(8,128)(2,1)} %param.6), channel_id=1, source_target_pairs={{1,0},{2,1},{3,2},{4,3},{5,4},{6,5},{7,6},{8,7},{9,8},{10,9},{11,1... | collective-permute-start | bytes 589832 | tf_op jit(solution)/shard_map/ppermute | solution.py:80
  6.2 1.1 %pad_maximum_fusion.2 = bf16[2,48,8,256]{3,2,1,0:T(8,128)(2,1)S(1)} fusion(bf16[1,48,8,256]{3,2,1,0:T(8,128)(2,1)} %bitcast.255, bf16[1,48,8,256]{3,2,1,0:T(8,128)(2,1)} %bitcast.254), kind=kLoop, calls=%fused_computation.54 | loop fusion | flops 196608 | bytes 786432 | tf_op jit(solution)/shard_map/stack | solution.py:86
  7.2 0.0 copy-start.5
  7.3 0.0 copy-start.4
  7.3 0.0 copy-start.6
  7.4 0.1 pad.134.clone
  7.4 0.1 maximum_maximum_fusion
  7.5 0.1 select_select_fusion
  7.6 0.8 %broadcast_in_dim.68 = bf16[2,8,5,8,256]{4,3,2,1,0:T(8,128)(2,1)} broadcast(bf16[2,5,8,256]{3,2,1,0:T(8,128)(2,1)S(1)} %select_select_fusion), dimensions={0,2,3,4} | broadcast | bytes 368640 | tf_op jit(solution)/shard_map/broadcast_in_dim | solution.py:95
  8.4 4.6 %all-to-all-start = ((bf16[16,5,8,256]{3,2,1,0:T(8,128)(2,1)}), bf16[16,5,8,256]{3,2,1,0:T(8,128)(2,1)S(1)}, u32[]{:S(2)}, u32[]{:S(2)}) async-start(bf16[16,5,8,256]{3,2,1,0:T(8,128)(2,1)} %bitcast.46), calls=%async_computation | async-start | bytes 655360 | tf_op jit(solution)/shard_map/all_to_all | solution.py:96
  13.1 0.6 pad.108.clone
  13.7 0.1 add_select_fusion.1
  13.8 0.1 add_select_fusion
  13.9 0.6 slice_bitcast_fusion.18
  14.5 0.1 pad_dynamic-slice_fusion
  14.6 0.1 compare_and_fusion
  14.6 0.1 dynamic-slice_select_fusion
  14.8 0.2 fusion.43
  14.9 0.1 slice.186
  15.0 0.1 slice.182
  15.1 0.4 fusion.13
  15.5 1.1 %copy.83 = bf16[48,4,8,3,24]{4,2,3,1,0:T(8,128)(2,1)S(1)} copy(bf16[48,4,8,3,24]{0,4,3,1,2:T(8,128)(2,1)S(1)} %fusion.13) | data formatting | bytes 442368 | tf_op jit(solution)/shard_map/convert_element_type | solution.py:24
  16.6 0.7 %maximum_bitcast_fusion.19 = (bf16[4,1,3,128]{3,0,2,1:T(4,128)(2,1)S(1)}, bf16[4,1,3,128]{3,0,2,1:T(4,128)(2,1)S(1)}) fusion(bf16[4,1,128]{2,0,1:T(4,128)(2,1)S(1)} %bitcast.260, bf16[4,1,128]{2,0,1:T(4,128)(2,1)S(1)} %get-tuple-element.61, bf16[4,1,128]{2,0,1:T(4,128)(2,1)S(1)} %broadcast.249, bf16[4,1,128]{2,0,1:T(4,128)(2,1)S(1)} %get-tuple-element.67, ...), kind=kLoop, calls=%fused_computation.150 | loop fusion | flops 6144 | bytes 11264 | tf_op jit(solution)/shard_map/stack | solution.py:150
  17.3 0.7 %maximum_bitcast_fusion.21 = (bf16[4,1,1,128]{3,0,2,1:T(4,128)(2,1)S(1)}, bf16[4,1,1,128]{3,0,2,1:T(4,128)(2,1)S(1)}) fusion(bf16[4,8]{1,0:T(4,128)(2,1)S(1)} %bitcast.258, bf16[4,9]{1,0:T(4,128)(2,1)S(1)} %slice.186, bf16[128]{0:T(256)(128)(2,1)} %pad.108.clone, bf16[4,8]{1,0:T(4,128)(2,1)S(1)} %bitcast.259, bf16[4,9]{1,0:T(4,128)(2,1)S(1)} %slice.182), kind=kLoop, calls=%fused_computation.167 | loop fusion | flops 5632 | bytes 2576 | tf_op jit(solution)/shard_map/broadcast_in_dim | solution.py:141
  18.0 0.9 %constant_dynamic-update-slice_fusion.2 = bf16[48,24,256]{2,1,0:T(8,128)(2,1)S(1)} fusion(bf16[48,8,256]{2,1,0:T(8,128)(2,1)} %collective-permute-done), kind=kLoop, calls=%fused_computation.106 | loop fusion | bytes 393216
  19.0 0.1 slice_bitcast_fusion.3
  19.1 0.0 copy-start.2
  19.1 0.7 %fusion.12 = bf16[4,48,8,256]{3,2,0,1:T(8,128)(2,1)S(1)} fusion(bf16[48,4,8,3,24]{4,2,3,1,0:T(8,128)(2,1)S(1)} %copy.83, bf16[48,1,24,256]{3,2,1,0:T(8,128)(2,1)S(1)} %get-tuple-element.34, bf16[48,1,24,256]{3,2,1,0:T(8,128)(2,1)S(1)} %bitcast.250, bf16[48,1,24,256]{3,2,1,0:T(8,128)(2,1)S(1)} %get-tuple-element.33), kind=kOutput, calls=%fused_computation.20 | convolution fusion | flops 58785792 | bytes 2777088 | tf_op jit(solution)/shard_map/ikarm,irmc->ikac/dot_general | solution.py:20
  19.8 0.2 copy-done.2
  20.1 0.5 fusion.11
  20.6 0.4 copy-done.7
  21.0 0.1 collective-permute-start.2
  21.1 0.1 slice_select_fusion
  21.2 2.2 %all-to-all-done = bf16[16,5,8,256]{3,2,1,0:T(8,128)(2,1)S(1)} async-done(((bf16[16,5,8,256]{3,2,1,0:T(8,128)(2,1)}), bf16[16,5,8,256]{3,2,1,0:T(8,128)(2,1)S(1)}, u32[]{:S(2)}, u32[]{:S(2)}) %all-to-all-start) | async-done | bytes 327712 | tf_op jit(solution)/shard_map/all_to_all | solution.py:96
  23.5 0.1 collective-permute-start.3
  23.6 0.3 fusion.18
  24.0 1.1 %collective-permute-done.3 = bf16[57,8,256]{2,1,0:T(8,128)(2,1)S(1)} collective-permute-done((bf16[57,8,256]{2,1,0:T(8,128)(2,1)S(1)}, bf16[57,8,256]{2,1,0:T(8,128)(2,1)S(1)}, u32[]{:S(2)}, u32[]{:S(2)}) %collective-permute-start.3) | collective-permute-done | bytes 233504 | tf_op jit(solution)/shard_map/ppermute | solution.py:119
  25.1 0.1 broadcast_select_fusion.1
  25.3 0.2 convolution_bitcast_fusion.4
  25.5 0.3 fusion.15
  25.8 0.8 %bitcast_add_fusion.1 = bf16[512,256]{1,0:T(8,128)(2,1)} fusion(f32[2,256,256]{2,1,0:T(8,128)S(1)} %fusion.15, f32[2,256,256]{2,1,0:T(8,128)S(1)} %slice_select_fusion, bf16[512,256]{1,0:T(8,128)(2,1)S(1)} %collective-permute-done.2), kind=kLoop, calls=%fused_computation.46 | loop fusion | flops 524288 | bytes 1572864 | tf_op jit(solution)/shard_map/add | solution.py:193
  26.6 0.2 fusion.19
  26.8 0.2 convolution_bitcast_fusion.5
  27.1 2.6 %collective-permute-start.5 = (bf16[48,8,256]{2,1,0:T(8,128)(2,1)S(1)}, bf16[48,8,256]{2,1,0:T(8,128)(2,1)S(1)}, u32[]{:S(2)}, u32[]{:S(2)}) collective-permute-start(bf16[48,8,256]{2,1,0:T(8,128)(2,1)S(1)} %copy-done.2), channel_id=1, source_target_pairs={{1,0},{2,1},{3,2},{4,3},{5,4},{6,5},{7,6},{8,7},{9,8},{10,9},{11,1... | collective-permute-start | bytes 589832 | tf_op jit(solution)/shard_map/ppermute | solution.py:80
  29.6 0.1 fusion.84
  29.7 3.5 %all-to-all-start.1 = ((bf16[16,32,256]{2,1,0:T(8,128)(2,1)}), bf16[16,32,256]{2,1,0:T(8,128)(2,1)S(1)}, u32[]{:S(2)}, u32[]{:S(2)}) async-start(bf16[16,32,256]{2,1,0:T(8,128)(2,1)} %bitcast.71), calls=%async_computation.1 | async-start | bytes 524288 | tf_op jit(solution)/shard_map/all_to_all | solution.py:196
  33.3 0.4 fusion.14
  33.7 1.1 %copy.101 = bf16[48,4,8,3,24]{4,2,3,1,0:T(8,128)(2,1)S(1)} copy(bf16[48,4,8,3,24]{0,4,3,1,2:T(8,128)(2,1)S(1)} %fusion.14) | data formatting | bytes 442368 | tf_op jit(solution)/shard_map/convert_element_type | solution.py:24
  34.8 2.2 %fusion.16 = bf16[48,8,256]{2,1,0:T(8,128)(2,1)} fusion(f32[4,1,8,256]{3,2,0,1:T(8,128)S(1)} %constant_dynamic-slice_fusion.1, f32[4,2,8,256]{3,2,0,1:T(8,128)S(1)} %constant_dynamic-slice_fusion, bf16[4,48,8,256]{3,2,0,1:T(8,128)(2,1)} %copy-done.7, pred[]{:T(512)S(6)} %eq.89, bf16[4,256,256]{2,1,0:T(8,128)(2,1)S(1)} %copy-done), kind=kOutput, calls=%fused_computation.27 | convolution fusion | flops 203784192 | bytes 1605633 | tf_op jit(solution)/shard_map/kiac,kce->iae/dot_general | solution.py:20
  36.9 0.6 %collective-permute-done.4 = bf16[48,8,256]{2,1,0:T(8,128)(2,1)} collective-permute-done((bf16[48,8,256]{2,1,0:T(8,128)(2,1)S(1)}, bf16[48,8,256]{2,1,0:T(8,128)(2,1)}, u32[]{:S(2)}, u32[]{:S(2)}) %collective-permute-start.4) | collective-permute-done | bytes 196640 | tf_op jit(solution)/shard_map/ppermute | solution.py:80
  37.6 0.9 %constant_dynamic-update-slice_fusion.5 = bf16[48,24,256]{2,1,0:T(8,128)(2,1)S(1)} fusion(bf16[48,8,256]{2,1,0:T(8,128)(2,1)} %collective-permute-done.4), kind=kLoop, calls=%fused_computation.109 | loop fusion | bytes 393216
  38.6 3.3 %all-to-all-done.1 = bf16[16,32,256]{2,1,0:T(8,128)(2,1)S(1)} async-done(((bf16[16,32,256]{2,1,0:T(8,128)(2,1)}), bf16[16,32,256]{2,1,0:T(8,128)(2,1)S(1)}, u32[]{:S(2)}, u32[]{:S(2)}) %all-to-all-start.1) | async-done | bytes 262176 | tf_op jit(solution)/shard_map/all_to_all | solution.py:196
  41.9 0.7 %broadcast_in_dim.108 = bf16[16,32,256]{2,1,0:T(8,128)(2,1)} broadcast(bf16[32,256]{1,0:T(8,128)(2,1)S(1)} %reduce_sum.12), dimensions={1,2} | broadcast | bytes 278528 | tf_op jit(solution)/shard_map/broadcast_in_dim | solution.py:198
  42.6 4.5 %all-to-all-start.2 = ((bf16[16,32,256]{2,1,0:T(8,128)(2,1)}), bf16[16,32,256]{2,1,0:T(8,128)(2,1)S(1)}, u32[]{:S(2)}, u32[]{:S(2)}) async-start(bf16[16,32,256]{2,1,0:T(8,128)(2,1)} %broadcast_in_dim.108), calls=%async_computation.2 | async-start | bytes 524288 | tf_op jit(solution)/shard_map/all_to_all | solution.py:198
  47.2 0.9 %slice_bitcast_fusion.1 = (bf16[48,1,24,256]{3,2,1,0:T(8,128)(2,1)S(1)}, bf16[48,1,24,256]{3,2,1,0:T(8,128)(2,1)}) fusion(bf16[48,24,256]{2,1,0:T(8,128)(2,1)S(1)} %constant_dynamic-update-slice_fusion.3), kind=kLoop, calls=%fused_computation.40 | loop fusion | bytes 1769472 | tf_op jit(solution)/shard_map/stack | solution.py:50
  48.1 2.7 %fusion.17 = bf16[48,8,256]{2,1,0:T(8,128)(2,1)} fusion(f32[4,1,8,256]{3,2,0,1:T(8,128)S(1)} %slice-done, f32[4,3,8,256]{3,2,0,1:T(8,128)S(1)} %slice-done.1, bf16[48,4,8,3,24]{4,2,3,1,0:T(8,128)(2,1)S(1)} %copy.101, bf16[48,1,24,256]{3,2,1,0:T(8,128)(2,1)} %get-tuple-element.32, bf16[48,1,24,256]{3,2,1,0:T(8,128)(2,1)S(1)} %bitcast.251, ...), kind=kOutput, calls=%fused_computation.28 | convolution fusion | flops 261783552 | bytes 2842625 | tf_op jit(solution)/shard_map/kjbe,kce->jbc/dot_general | solution.py:20
  50.8 6.7 %all-to-all-done.2 = bf16[16,32,256]{2,1,0:T(8,128)(2,1)S(1)} async-done(((bf16[16,32,256]{2,1,0:T(8,128)(2,1)}), bf16[16,32,256]{2,1,0:T(8,128)(2,1)S(1)}, u32[]{:S(2)}, u32[]{:S(2)}) %all-to-all-start.2) | async-done | bytes 262176 | tf_op jit(solution)/shard_map/all_to_all | solution.py:198
  57.5 0.4 collective-permute-start.6
  57.9 1.2 %collective-permute-done.6 = bf16[16,32,256]{2,1,0:T(8,128)(2,1)S(1)} collective-permute-done((bf16[16,32,256]{2,1,0:T(8,128)(2,1)S(1)}, bf16[16,32,256]{2,1,0:T(8,128)(2,1)S(1)}, u32[]{:S(2)}, u32[]{:S(2)}) %collective-permute-start.6) | collective-permute-done | bytes 262176 | tf_op jit(solution)/shard_map/ppermute | solution.py:213
  59.1 0.1 select_bitcast_fusion.1
  59.1 0.1 pad_maximum_fusion
  59.2 1.1 %convert.2 = f32[4,256,256]{2,1,0:T(8,128)} convert(bf16[4,256,256]{2,1,0:T(8,128)(2,1)S(1)} %bitcast.248) | non-fusion elementwise | flops 262144 | bytes 1572864 | tf_op jit(solution)/shard_map/convert_element_type | solution.py:215
  (62 shorter events, 0.6 us)
Async XLA Ops:
  0.6 34.1 %copy-start = (bf16[4,256,256]{2,1,0:T(8,128)(2,1)S(1)}, bf16[4,256,256]{2,1,0:T(8,128)(2,1)}, u32[]{:S(2)}) copy-start(bf16[4,256,256]{2,1,0:T(8,128)(2,1)} %param.8) | copy-start | bytes 1572868
  0.6 17.4 %collective-permute-start = (bf16[48,8,256]{2,1,0:T(8,128)(2,1)}, bf16[48,8,256]{2,1,0:T(8,128)(2,1)}, u32[]{:S(2)}, u32[]{:S(2)}) collective-permute-start(bf16[48,8,256]{2,1,0:T(8,128)(2,1)} %param.6), channel_id=1, source_target_pairs={{0,1},{1,2},{2,3},{3,4},{4,5},{5,6},{6,7},{7,8},{8,9},{9,10},{10,1... | collective-permute-start | bytes 589832 | tf_op jit(solution)/shard_map/ppermute | solution.py:80
  1.2 17.9 %collective-permute-start.1 = (bf16[48,8,256]{2,1,0:T(8,128)(2,1)}, bf16[48,8,256]{2,1,0:T(8,128)(2,1)S(1)}, u32[]{:S(2)}, u32[]{:S(2)}) collective-permute-start(bf16[48,8,256]{2,1,0:T(8,128)(2,1)} %param.6), channel_id=1, source_target_pairs={{1,0},{2,1},{3,2},{4,3},{5,4},{6,5},{7,6},{8,7},{9,8},{10,9},{11,1... | collective-permute-start | bytes 589832 | tf_op jit(solution)/shard_map/ppermute | solution.py:80
  7.2 5.8 %copy-start.5 = (bf16[4,4,3,128]{3,1,2,0:T(4,128)(2,1)S(1)}, bf16[4,4,3,128]{3,1,2,0:T(4,128)(2,1)}, u32[]{:S(2)}) copy-start(bf16[4,4,3,128]{3,1,2,0:T(4,128)(2,1)} %param.10) | copy-start | bytes 36868
  7.3 7.2 %copy-start.4 = (bf16[4,96,3,17]{1,0,3,2:T(4,128)(2,1)S(1)}, bf16[4,96,3,17]{1,0,3,2:T(4,128)(2,1)}, u32[]{:S(2)}) copy-start(bf16[4,96,3,17]{1,0,3,2:T(4,128)(2,1)} %param.9) | copy-start | bytes 117508
  7.3 7.2 %copy-start.6 = (s32[96]{0:T(128)S(1)}, s32[96]{0:T(128)}, u32[]{:S(2)}) copy-start(s32[96]{0:T(128)} %param.11) | copy-start | bytes 1156
  8.4 15.0 %all-to-all-start = ((bf16[16,5,8,256]{3,2,1,0:T(8,128)(2,1)}), bf16[16,5,8,256]{3,2,1,0:T(8,128)(2,1)S(1)}, u32[]{:S(2)}, u32[]{:S(2)}) async-start(bf16[16,5,8,256]{3,2,1,0:T(8,128)(2,1)} %bitcast.46), calls=%async_computation | async-start | bytes 655360 | tf_op jit(solution)/shard_map/all_to_all | solution.py:96
  15.5 3.5 %copy-start.1 = (bf16[48,8,256]{2,1,0:T(8,128)(2,1)S(1)}, bf16[48,8,256]{2,1,0:T(8,128)(2,1)}, u32[]{:S(2)}) copy-start(bf16[48,8,256]{2,1,0:T(8,128)(2,1)} %param.6) | copy-start | bytes 589828
  19.1 0.9 %copy-start.2 = (bf16[48,8,256]{2,1,0:T(8,128)(2,1)S(1)}, bf16[48,8,256]{2,1,0:T(8,128)(2,1)}, u32[]{:S(2)}) copy-start(bf16[48,8,256]{2,1,0:T(8,128)(2,1)} %param.7) | copy-start | bytes 589828
  20.1 0.9 %copy-start.7 = (bf16[4,48,8,256]{3,2,0,1:T(8,128)(2,1)}, bf16[4,48,8,256]{3,2,0,1:T(8,128)(2,1)S(1)}, u32[]{:S(2)}) copy-start(bf16[4,48,8,256]{3,2,0,1:T(8,128)(2,1)S(1)} %fusion.12) | copy-start | bytes 2359300
  21.0 4.8 %collective-permute-start.2 = (bf16[512,256]{1,0:T(8,128)(2,1)S(1)}, bf16[512,256]{1,0:T(8,128)(2,1)S(1)}, u32[]{:S(2)}, u32[]{:S(2)}) collective-permute-start(bf16[512,256]{1,0:T(8,128)(2,1)S(1)} %bitcast.256), channel_id=1, source_target_pairs={{0,1},{1,0},{2,3},{3,2},{4,5},{5,4},{6,7},{7,6},{8,9},{9,8},{10,11... | collective-permute-start | bytes 786440 | tf_op jit(solution)/shard_map/ppermute | solution.py:174
  23.5 1.6 %collective-permute-start.3 = (bf16[57,8,256]{2,1,0:T(8,128)(2,1)S(1)}, bf16[57,8,256]{2,1,0:T(8,128)(2,1)S(1)}, u32[]{:S(2)}, u32[]{:S(2)}) collective-permute-start(bf16[57,8,256]{2,1,0:T(8,128)(2,1)S(1)} %pad_maximum_fusion.3), channel_id=1, source_target_pairs={{0,1},{1,0},{2,3},{3,2},{4,5},{5,4},{6,7},{7,6},{8,9},{9,8},{10,11... | collective-permute-start | bytes 700424 | tf_op jit(solution)/shard_map/ppermute | solution.py:119
  27.0 7.7 %copy-start.3 = (f32[4,4,8,256]{3,2,0,1:T(8,128)}, f32[4,4,8,256]{3,2,0,1:T(8,128)S(1)}, u32[]{:S(2)}) copy-start(f32[4,4,8,256]{3,2,0,1:T(8,128)S(1)} %convolution_bitcast_fusion.5) | copy-start | bytes 393220
  27.1 11.5 %collective-permute-start.5 = (bf16[48,8,256]{2,1,0:T(8,128)(2,1)S(1)}, bf16[48,8,256]{2,1,0:T(8,128)(2,1)S(1)}, u32[]{:S(2)}, u32[]{:S(2)}) collective-permute-start(bf16[48,8,256]{2,1,0:T(8,128)(2,1)S(1)} %copy-done.2), channel_id=1, source_target_pairs={{1,0},{2,1},{3,2},{4,3},{5,4},{6,5},{7,6},{8,7},{9,8},{10,9},{11,1... | collective-permute-start | bytes 589832 | tf_op jit(solution)/shard_map/ppermute | solution.py:80
  29.6 8.0 %collective-permute-start.4 = (bf16[48,8,256]{2,1,0:T(8,128)(2,1)S(1)}, bf16[48,8,256]{2,1,0:T(8,128)(2,1)}, u32[]{:S(2)}, u32[]{:S(2)}) collective-permute-start(bf16[48,8,256]{2,1,0:T(8,128)(2,1)S(1)} %copy-done.2), channel_id=1, source_target_pairs={{0,1},{1,2},{2,3},{3,4},{4,5},{5,6},{6,7},{7,8},{8,9},{9,10},{10,1... | collective-permute-start | bytes 589832 | tf_op jit(solution)/shard_map/ppermute | solution.py:80
  29.7 12.2 %all-to-all-start.1 = ((bf16[16,32,256]{2,1,0:T(8,128)(2,1)}), bf16[16,32,256]{2,1,0:T(8,128)(2,1)S(1)}, u32[]{:S(2)}, u32[]{:S(2)}) async-start(bf16[16,32,256]{2,1,0:T(8,128)(2,1)} %bitcast.71), calls=%async_computation.1 | async-start | bytes 524288 | tf_op jit(solution)/shard_map/all_to_all | solution.py:196
  42.6 5.4 %slice-start = ((f32[4,4,8,256]{3,2,0,1:T(8,128)}), f32[4,1,8,256]{3,2,0,1:T(8,128)S(1)}, s32[]{:S(2)}) async-start(f32[4,4,8,256]{3,2,0,1:T(8,128)} %copy-done.3), calls=%async_computation.3 | async-start | bytes 65536 | tf_op jit(solution)/shard_map/slice | solution.py:154
  42.6 5.4 %slice-start.1 = ((f32[4,4,8,256]{3,2,0,1:T(8,128)}), f32[4,3,8,256]{3,2,0,1:T(8,128)S(1)}, s32[]{:S(2)}) async-start(f32[4,4,8,256]{3,2,0,1:T(8,128)} %copy-done.3), calls=%async_computation.4 | async-start | bytes 196608 | tf_op jit(solution)/shard_map/slice | solution.py:154
  42.6 14.8 %all-to-all-start.2 = ((bf16[16,32,256]{2,1,0:T(8,128)(2,1)}), bf16[16,32,256]{2,1,0:T(8,128)(2,1)S(1)}, u32[]{:S(2)}, u32[]{:S(2)}) async-start(bf16[16,32,256]{2,1,0:T(8,128)(2,1)} %broadcast_in_dim.108), calls=%async_computation.2 | async-start | bytes 524288 | tf_op jit(solution)/shard_map/all_to_all | solution.py:198
  57.5 1.6 %collective-permute-start.6 = (bf16[16,32,256]{2,1,0:T(8,128)(2,1)S(1)}, bf16[16,32,256]{2,1,0:T(8,128)(2,1)S(1)}, u32[]{:S(2)}, u32[]{:S(2)}) collective-permute-start(bf16[16,32,256]{2,1,0:T(8,128)(2,1)S(1)} %all-to-all-done.2), channel_id=1, source_target_pairs={{0,1},{1,0},{2,3},{3,2},{4,5},{5,4},{6,7},{7,6},{8,9},{9,8},{10,11... | collective-permute-start | bytes 786440 | tf_op jit(solution)/shard_map/ppermute | solution.py:213

commit v4 on v3

--- a/solution.py
+++ b/solution.py
@@ -124,8 +124,8 @@
     circle = jnp.moveaxis(circle, 0, 1).reshape(rows, lon_total, channels)
     signal_circle, cot_circle = circle[: SLAB + count], circle[SLAB + count :]
 
-    band_kernel, cycle_kernel, support_width, _ = lax.optimization_barrier(
-        (band_kernel, cycle_kernel, support_width, sent)
+    signal_left, signal_right, band_kernel, cycle_kernel, support_width, _ = lax.optimization_barrier(
+        (signal_left, signal_right, band_kernel, cycle_kernel, support_width, sent)
     )
     coeffs = band_coefficients(band_kernel, support_width, first_row, total_rows, lat_count + 2 * R)
     forward = band_matrices(coeffs[:, R : R + lat_count], lon_count, True)

time: 60.9 us -> 61.8 us (1.015)
  starting transfers between devices: 21.3 us -> 24.3 us
  local copies, waits for them, and re-layouts: 8.97 us -> 7.29 us
  other arithmetic: 5.56 us -> 4.19 us
  waiting for transfers between devices: 15.1 us -> 16.2 us
    ppermute x1, starting transfers between devices: 0.07 us -> 3.1 us  [local(): lax.ppermute(jnp.concatenate([even.reshape((-1,) + even.shape[2:]), facin...]
    all_to_all x1, waiting for transfers between devices: 2.2 us -> 0.01 us  [local(): lax.all_to_all(sent.reshape((-1,) + polar_rows.shape), CHIPS, 0, 0)]
    ppermute x2, waiting for transfers between devices: 0.62 us -> 2.42 us  [sector_edges(): lax.ppermute(field, LON, to_right)]
    ppermute x1, starting transfers between devices: 0.07 us -> 1.53 us  [local(): kept = kept + lax.ppermute(given, 'core', swap).astype(jnp.float32)]
    all_to_all x1, waiting for transfers between devices: 3.3 us -> 4.42 us  [local(): parts = lax.all_to_all(bf16(kept).reshape(group, -1, channels), CHIPS, 0, 0)]
    all_to_all x1, starting transfers between devices: 4.57 us -> 3.54 us  [local(): lax.all_to_all(sent.reshape((-1,) + polar_rows.shape), CHIPS, 0, 0)]
    all_to_all x1, starting transfers between devices: 4.53 us -> 5.21 us  [local(): lax.all_to_all(jnp.broadcast_to(chunk[None], (group,) + chunk.shape), CHI...]
    another operation x2, other arithmetic: 0.7 us -> 0.01 us  [local(): jnp.stack([jnp.stack(row, axis=1) for row in low_rows], axis=1)]
  transfers between devices with their start and end apart: 10 -> 10, of which waited for: 6 -> 6; matrix products, arithmetic and copies ran while one was open for 31% -> 25% of each run, Pallas kernels for 0% -> 0%
where the time goes in v4:
time: 61.8 us; the launch traced here: 61.3 us
  starting transfers between devices  24.3 us (39%)
  waiting for transfers between devices  16.2 us (26%)
  matrix products  7.98 us (13%)
  local copies, waits for them, and re-layouts  7.29 us (12%)
  other arithmetic  4.19 us (7%)
  between operations  1.26 us (2%)
    dot_general x11, matrix products, dot(): return jnp.einsum(spec, a, b, preferred_element_type=jnp.float32)  7.98 us
    ppermute x2, starting transfers between devices, sector_edges(): lax.ppermute(field, LON, to_left)  7.36 us
    all_to_all x1, waiting for transfers between devices, local(): lax.all_to_all(jnp.broadcast_to(chunk[None], (group,) + chunk.shape), CHI...  7.08 us
    all_to_all x1, starting transfers between devices, local(): lax.all_to_all(jnp.broadcast_to(chunk[None], (group,) + chunk.shape), CHI...  5.21 us
    all_to_all x1, waiting for transfers between devices, local(): parts = lax.all_to_all(bf16(kept).reshape(group, -1, channels), CHIPS, 0, 0)  4.42 us
    all_to_all x1, starting transfers between devices, local(): parts = lax.all_to_all(bf16(kept).reshape(group, -1, channels), CHIPS, 0, 0)  3.54 us
    all_to_all x1, starting transfers between devices, local(): lax.all_to_all(sent.reshape((-1,) + polar_rows.shape), CHIPS, 0, 0)  3.54 us
    ppermute x1, starting transfers between devices, local(): lax.ppermute(jnp.concatenate([even.reshape((-1,) + even.shape[2:]), facin...  3.1 us
  transfers between devices with their start and end apart: 10, of which 6 were waited for; matrix products, arithmetic and copies ran while one was open for 25% of the time, Pallas kernels for 0%

profile of v4, /device:TPU:0, one launch (start us, length us, event | category | flops | bytes accessed | tf_op | source)
XLA Modules:
  0.0 61.3 jit_solution(4039566477272931133)
XLA Ops:
  0.6 0.0 copy-start
  0.6 5.5 %collective-permute-start.1 = (bf16[48,8,256]{2,1,0:T(8,128)(2,1)}, bf16[48,8,256]{2,1,0:T(8,128)(2,1)S(1)}, u32[]{:S(2)}, u32[]{:S(2)}) collective-permute-start(bf16[48,8,256]{2,1,0:T(8,128)(2,1)} %param.6), channel_id=1, source_target_pairs={{1,0},{2,1},{3,2},{4,3},{5,4},{6,5},{7,6},{8,7},{9,8},{10,9},{11,1... | collective-permute-start | bytes 589832 | tf_op jit(solution)/shard_map/ppermute | solution.py:80
  6.1 0.0 collective-permute-start
  6.1 1.1 %pad_maximum_fusion.2 = bf16[2,48,8,256]{3,2,1,0:T(8,128)(2,1)S(1)} fusion(bf16[1,48,8,256]{3,2,1,0:T(8,128)(2,1)} %bitcast.255, bf16[1,48,8,256]{3,2,1,0:T(8,128)(2,1)} %bitcast.254), kind=kLoop, calls=%fused_computation.54 | loop fusion | flops 196608 | bytes 786432 | tf_op jit(solution)/shard_map/stack | solution.py:86
  7.2 0.0 copy-start.6
  7.2 0.0 copy-start.5
  7.2 0.0 copy-start.7
  7.3 0.1 pad.134.clone
  7.4 0.1 maximum_maximum_fusion
  7.5 0.1 select_select_fusion
  7.5 0.8 %broadcast_in_dim.68 = bf16[2,8,5,8,256]{4,3,2,1,0:T(8,128)(2,1)} broadcast(bf16[2,5,8,256]{3,2,1,0:T(8,128)(2,1)S(1)} %select_select_fusion), dimensions={0,2,3,4} | broadcast | bytes 368640 | tf_op jit(solution)/shard_map/broadcast_in_dim | solution.py:95
  8.3 3.5 %all-to-all-start = ((bf16[16,5,8,256]{3,2,1,0:T(8,128)(2,1)}), bf16[16,5,8,256]{3,2,1,0:T(8,128)(2,1)S(1)}, u32[]{:S(2)}, u32[]{:S(2)}) async-start(bf16[16,5,8,256]{3,2,1,0:T(8,128)(2,1)} %bitcast.46), calls=%async_computation | async-start | bytes 655360 | tf_op jit(solution)/shard_map/all_to_all | solution.py:96
  12.0 0.1 pad.108.clone
  12.1 0.1 add_select_fusion
  12.1 0.1 add_select_fusion.1
  12.2 0.0 collective-permute-done.1
  12.2 1.9 %collective-permute-done = bf16[48,8,256]{2,1,0:T(8,128)(2,1)S(1)} collective-permute-done((bf16[48,8,256]{2,1,0:T(8,128)(2,1)}, bf16[48,8,256]{2,1,0:T(8,128)(2,1)S(1)}, u32[]{:S(2)}, u32[]{:S(2)}) %collective-permute-start) | collective-permute-done | bytes 196640 | tf_op jit(solution)/shard_map/ppermute | solution.py:80
  14.2 0.1 pad_dynamic-slice_fusion
  14.3 0.1 compare_and_fusion
  14.4 0.1 dynamic-slice_select_fusion
  14.5 0.3 copy-done.4
  14.8 0.2 fusion.43
  15.0 0.4 fusion.13
  15.4 0.0 copy-start.1
  15.4 1.1 %copy.83 = bf16[48,4,8,3,24]{4,2,3,1,0:T(8,128)(2,1)S(1)} copy(bf16[48,4,8,3,24]{0,4,3,1,2:T(8,128)(2,1)S(1)} %fusion.13) | data formatting | bytes 442368 | tf_op jit(solution)/shard_map/convert_element_type | solution.py:24
  16.4 0.9 %constant_dynamic-update-slice_fusion.2 = bf16[48,24,256]{2,1,0:T(8,128)(2,1)S(1)} fusion(bf16[48,8,256]{2,1,0:T(8,128)(2,1)} %copy-done.4), kind=kLoop, calls=%fused_computation.106 | loop fusion | bytes 393216
  17.4 0.1 slice_bitcast_fusion.3
  17.5 0.0 copy-start.2
  17.5 0.7 %fusion.12 = bf16[4,48,8,256]{3,2,0,1:T(8,128)(2,1)S(1)} fusion(bf16[48,4,8,3,24]{4,2,3,1,0:T(8,128)(2,1)S(1)} %copy.83, bf16[48,1,24,256]{3,2,1,0:T(8,128)(2,1)S(1)} %get-tuple-element.38, bf16[48,1,24,256]{3,2,1,0:T(8,128)(2,1)S(1)} %bitcast.250, bf16[48,1,24,256]{3,2,1,0:T(8,128)(2,1)S(1)} %get-tuple-element.37), kind=kOutput, calls=%fused_computation.20 | convolution fusion | flops 58785792 | bytes 2777088 | tf_op jit(solution)/shard_map/ikarm,irmc->ikac/dot_general | solution.py:20
  18.2 0.2 copy-done.2
  18.5 0.5 fusion.11
  18.9 0.4 copy-done.8
  19.4 1.5 %collective-permute-start.2 = (bf16[512,256]{1,0:T(8,128)(2,1)S(1)}, bf16[512,256]{1,0:T(8,128)(2,1)S(1)}, u32[]{:S(2)}, u32[]{:S(2)}) collective-permute-start(bf16[512,256]{1,0:T(8,128)(2,1)S(1)} %bitcast.256), channel_id=1, source_target_pairs={{0,1},{1,0},{2,3},{3,2},{4,5},{5,4},{6,7},{7,6},{8,9},{9,8},{10,11... | collective-permute-start | bytes 786440 | tf_op jit(solution)/shard_map/ppermute | solution.py:174
  21.0 0.1 slice.186
  21.1 0.1 slice.182
  21.1 0.1 maximum_bitcast_fusion.21
  21.2 0.1 slice_select_fusion
  21.5 3.1 %collective-permute-start.3 = (bf16[57,8,256]{2,1,0:T(8,128)(2,1)S(1)}, bf16[57,8,256]{2,1,0:T(8,128)(2,1)S(1)}, u32[]{:S(2)}, u32[]{:S(2)}) collective-permute-start(bf16[57,8,256]{2,1,0:T(8,128)(2,1)S(1)} %pad_maximum_fusion.3), channel_id=1, source_target_pairs={{0,1},{1,0},{2,3},{3,2},{4,5},{5,4},{6,7},{7,6},{8,9},{9,8},{10,11... | collective-permute-start | bytes 700424 | tf_op jit(solution)/shard_map/ppermute | solution.py:119
  24.6 0.3 fusion.18
  24.9 0.8 %collective-permute-done.3 = bf16[57,8,256]{2,1,0:T(8,128)(2,1)S(1)} collective-permute-done((bf16[57,8,256]{2,1,0:T(8,128)(2,1)S(1)}, bf16[57,8,256]{2,1,0:T(8,128)(2,1)S(1)}, u32[]{:S(2)}, u32[]{:S(2)}) %collective-permute-start.3) | collective-permute-done | bytes 233504 | tf_op jit(solution)/shard_map/ppermute | solution.py:119
  25.9 0.2 convolution_bitcast_fusion.4
  26.1 0.3 fusion.15
  26.4 0.0 collective-permute-done.2
  26.4 0.8 %bitcast_add_fusion.1 = bf16[512,256]{1,0:T(8,128)(2,1)} fusion(f32[2,256,256]{2,1,0:T(8,128)S(1)} %fusion.15, f32[2,256,256]{2,1,0:T(8,128)S(1)} %slice_select_fusion, bf16[512,256]{1,0:T(8,128)(2,1)S(1)} %collective-permute-done.2), kind=kLoop, calls=%fused_computation.46 | loop fusion | flops 524288 | bytes 1572864 | tf_op jit(solution)/shard_map/add | solution.py:193
  27.2 0.2 fusion.19
  27.5 0.2 convolution_bitcast_fusion.5
  27.7 0.0 copy-start.3
  27.7 1.9 %collective-permute-start.5 = (bf16[48,8,256]{2,1,0:T(8,128)(2,1)S(1)}, bf16[48,8,256]{2,1,0:T(8,128)(2,1)S(1)}, u32[]{:S(2)}, u32[]{:S(2)}) collective-permute-start(bf16[48,8,256]{2,1,0:T(8,128)(2,1)S(1)} %copy-done.2), channel_id=1, source_target_pairs={{1,0},{2,1},{3,2},{4,3},{5,4},{6,5},{7,6},{8,7},{9,8},{10,9},{11,1... | collective-permute-start | bytes 589832 | tf_op jit(solution)/shard_map/ppermute | solution.py:80
  29.6 0.0 collective-permute-start.4
  29.6 0.1 fusion.84
  29.7 3.5 %all-to-all-start.1 = ((bf16[16,32,256]{2,1,0:T(8,128)(2,1)}), bf16[16,32,256]{2,1,0:T(8,128)(2,1)S(1)}, u32[]{:S(2)}, u32[]{:S(2)}) async-start(bf16[16,32,256]{2,1,0:T(8,128)(2,1)} %bitcast.71), calls=%async_computation.1 | async-start | bytes 524288 | tf_op jit(solution)/shard_map/all_to_all | solution.py:196
  33.3 0.4 fusion.14
  33.6 1.1 %copy.101 = bf16[48,4,8,3,24]{4,2,3,1,0:T(8,128)(2,1)S(1)} copy(bf16[48,4,8,3,24]{0,4,3,1,2:T(8,128)(2,1)S(1)} %fusion.14) | data formatting | bytes 442368 | tf_op jit(solution)/shard_map/convert_element_type | solution.py:24
  34.7 2.2 %fusion.16 = bf16[48,8,256]{2,1,0:T(8,128)(2,1)} fusion(f32[4,1,8,256]{3,2,0,1:T(8,128)S(1)} %constant_dynamic-slice_fusion.1, f32[4,2,8,256]{3,2,0,1:T(8,128)S(1)} %constant_dynamic-slice_fusion, bf16[4,48,8,256]{3,2,0,1:T(8,128)(2,1)} %copy-done.8, pred[]{:T(512)S(6)} %eq.89, bf16[4,256,256]{2,1,0:T(8,128)(2,1)S(1)} %copy-done), kind=kOutput, calls=%fused_computation.27 | convolution fusion | flops 203784192 | bytes 1605633 | tf_op jit(solution)/shard_map/kiac,kce->iae/dot_general | solution.py:20
  36.9 0.5 collective-permute-done.4
  37.5 4.4 %all-to-all-done.1 = bf16[16,32,256]{2,1,0:T(8,128)(2,1)S(1)} async-done(((bf16[16,32,256]{2,1,0:T(8,128)(2,1)}), bf16[16,32,256]{2,1,0:T(8,128)(2,1)S(1)}, u32[]{:S(2)}, u32[]{:S(2)}) %all-to-all-start.1) | async-done | bytes 262176 | tf_op jit(solution)/shard_map/all_to_all | solution.py:196
  42.0 0.7 %broadcast_in_dim.108 = bf16[16,32,256]{2,1,0:T(8,128)(2,1)} broadcast(bf16[32,256]{1,0:T(8,128)(2,1)S(1)} %reduce_sum.12), dimensions={1,2} | broadcast | bytes 278528 | tf_op jit(solution)/shard_map/broadcast_in_dim | solution.py:198
  42.7 5.2 %all-to-all-start.2 = ((bf16[16,32,256]{2,1,0:T(8,128)(2,1)}), bf16[16,32,256]{2,1,0:T(8,128)(2,1)S(1)}, u32[]{:S(2)}, u32[]{:S(2)}) async-start(bf16[16,32,256]{2,1,0:T(8,128)(2,1)} %broadcast_in_dim.108), calls=%async_computation.2 | async-start | bytes 524288 | tf_op jit(solution)/shard_map/all_to_all | solution.py:198
  47.9 0.9 %slice_bitcast_fusion.1 = (bf16[48,1,24,256]{3,2,1,0:T(8,128)(2,1)S(1)}, bf16[48,1,24,256]{3,2,1,0:T(8,128)(2,1)}) fusion(bf16[48,24,256]{2,1,0:T(8,128)(2,1)S(1)} %constant_dynamic-update-slice_fusion.3), kind=kLoop, calls=%fused_computation.40 | loop fusion | bytes 1769472 | tf_op jit(solution)/shard_map/stack | solution.py:50
  48.8 2.7 %fusion.17 = bf16[48,8,256]{2,1,0:T(8,128)(2,1)} fusion(f32[4,1,8,256]{3,2,0,1:T(8,128)S(1)} %slice-done, f32[4,3,8,256]{3,2,0,1:T(8,128)S(1)} %slice-done.1, bf16[48,4,8,3,24]{4,2,3,1,0:T(8,128)(2,1)S(1)} %copy.101, bf16[48,1,24,256]{3,2,1,0:T(8,128)(2,1)} %get-tuple-element.36, bf16[48,1,24,256]{3,2,1,0:T(8,128)(2,1)S(1)} %bitcast.251, ...), kind=kOutput, calls=%fused_computation.28 | convolution fusion | flops 261783552 | bytes 2842625 | tf_op jit(solution)/shard_map/kjbe,kce->jbc/dot_general | solution.py:20
  51.5 7.1 %all-to-all-done.2 = bf16[16,32,256]{2,1,0:T(8,128)(2,1)S(1)} async-done(((bf16[16,32,256]{2,1,0:T(8,128)(2,1)}), bf16[16,32,256]{2,1,0:T(8,128)(2,1)S(1)}, u32[]{:S(2)}, u32[]{:S(2)}) %all-to-all-start.2) | async-done | bytes 262176 | tf_op jit(solution)/shard_map/all_to_all | solution.py:198
  58.6 1.5 %collective-permute-done.6 = bf16[16,32,256]{2,1,0:T(8,128)(2,1)S(1)} collective-permute-done((bf16[16,32,256]{2,1,0:T(8,128)(2,1)S(1)}, bf16[16,32,256]{2,1,0:T(8,128)(2,1)S(1)}, u32[]{:S(2)}, u32[]{:S(2)}) %collective-permute-start.6) | collective-permute-done | bytes 262176 | tf_op jit(solution)/shard_map/ppermute | solution.py:213
  60.1 0.1 pad_maximum_fusion
  60.2 1.1 %convert.2 = f32[4,256,256]{2,1,0:T(8,128)} convert(bf16[4,256,256]{2,1,0:T(8,128)(2,1)S(1)} %bitcast.248) | non-fusion elementwise | flops 262144 | bytes 1572864 | tf_op jit(solution)/shard_map/convert_element_type | solution.py:215
  (64 shorter events, 0.8 us)
Async XLA Ops:
  0.6 34.1 %copy-start = (bf16[4,256,256]{2,1,0:T(8,128)(2,1)S(1)}, bf16[4,256,256]{2,1,0:T(8,128)(2,1)}, u32[]{:S(2)}) copy-start(bf16[4,256,256]{2,1,0:T(8,128)(2,1)} %param.8) | copy-start | bytes 1572868
  0.6 11.6 %collective-permute-start.1 = (bf16[48,8,256]{2,1,0:T(8,128)(2,1)}, bf16[48,8,256]{2,1,0:T(8,128)(2,1)S(1)}, u32[]{:S(2)}, u32[]{:S(2)}) collective-permute-start(bf16[48,8,256]{2,1,0:T(8,128)(2,1)} %param.6), channel_id=1, source_target_pairs={{1,0},{2,1},{3,2},{4,3},{5,4},{6,5},{7,6},{8,7},{9,8},{10,9},{11,1... | collective-permute-start | bytes 589832 | tf_op jit(solution)/shard_map/ppermute | solution.py:80
  6.1 8.0 %collective-permute-start = (bf16[48,8,256]{2,1,0:T(8,128)(2,1)}, bf16[48,8,256]{2,1,0:T(8,128)(2,1)S(1)}, u32[]{:S(2)}, u32[]{:S(2)}) collective-permute-start(bf16[48,8,256]{2,1,0:T(8,128)(2,1)} %param.6), channel_id=1, source_target_pairs={{0,1},{1,2},{2,3},{3,4},{4,5},{5,6},{6,7},{7,8},{8,9},{9,10},{10,1... | collective-permute-start | bytes 589832 | tf_op jit(solution)/shard_map/ppermute | solution.py:80
  7.2 6.9 %copy-start.6 = (bf16[4,4,3,128]{3,1,2,0:T(4,128)(2,1)S(1)}, bf16[4,4,3,128]{3,1,2,0:T(4,128)(2,1)}, u32[]{:S(2)}) copy-start(bf16[4,4,3,128]{3,1,2,0:T(4,128)(2,1)} %param.10) | copy-start | bytes 36868
  7.2 7.0 %copy-start.5 = (bf16[4,96,3,17]{1,0,3,2:T(4,128)(2,1)S(1)}, bf16[4,96,3,17]{1,0,3,2:T(4,128)(2,1)}, u32[]{:S(2)}) copy-start(bf16[4,96,3,17]{1,0,3,2:T(4,128)(2,1)} %param.9) | copy-start | bytes 117508
  7.2 7.0 %copy-start.7 = (s32[96]{0:T(128)S(1)}, s32[96]{0:T(128)}, u32[]{:S(2)}) copy-start(s32[96]{0:T(128)} %param.11) | copy-start | bytes 1156
  8.3 13.0 %all-to-all-start = ((bf16[16,5,8,256]{3,2,1,0:T(8,128)(2,1)}), bf16[16,5,8,256]{3,2,1,0:T(8,128)(2,1)S(1)}, u32[]{:S(2)}, u32[]{:S(2)}) async-start(bf16[16,5,8,256]{3,2,1,0:T(8,128)(2,1)} %bitcast.46), calls=%async_computation | async-start | bytes 655360 | tf_op jit(solution)/shard_map/all_to_all | solution.py:96
  14.1 0.7 %copy-start.4 = (bf16[48,8,256]{2,1,0:T(8,128)(2,1)}, bf16[48,8,256]{2,1,0:T(8,128)(2,1)S(1)}, u32[]{:S(2)}) copy-start(bf16[48,8,256]{2,1,0:T(8,128)(2,1)S(1)} %collective-permute-done) | copy-start | bytes 589828
  15.4 2.0 %copy-start.1 = (bf16[48,8,256]{2,1,0:T(8,128)(2,1)S(1)}, bf16[48,8,256]{2,1,0:T(8,128)(2,1)}, u32[]{:S(2)}) copy-start(bf16[48,8,256]{2,1,0:T(8,128)(2,1)} %param.6) | copy-start | bytes 589828
  17.5 0.9 %copy-start.2 = (bf16[48,8,256]{2,1,0:T(8,128)(2,1)S(1)}, bf16[48,8,256]{2,1,0:T(8,128)(2,1)}, u32[]{:S(2)}) copy-start(bf16[48,8,256]{2,1,0:T(8,128)(2,1)} %param.7) | copy-start | bytes 589828
  18.5 0.9 %copy-start.8 = (bf16[4,48,8,256]{3,2,0,1:T(8,128)(2,1)}, bf16[4,48,8,256]{3,2,0,1:T(8,128)(2,1)S(1)}, u32[]{:S(2)}) copy-start(bf16[4,48,8,256]{3,2,0,1:T(8,128)(2,1)S(1)} %fusion.12) | copy-start | bytes 2359300
  19.4 7.0 %collective-permute-start.2 = (bf16[512,256]{1,0:T(8,128)(2,1)S(1)}, bf16[512,256]{1,0:T(8,128)(2,1)S(1)}, u32[]{:S(2)}, u32[]{:S(2)}) collective-permute-start(bf16[512,256]{1,0:T(8,128)(2,1)S(1)} %bitcast.256), channel_id=1, source_target_pairs={{0,1},{1,0},{2,3},{3,2},{4,5},{5,4},{6,7},{7,6},{8,9},{9,8},{10,11... | collective-permute-start | bytes 786440 | tf_op jit(solution)/shard_map/ppermute | solution.py:174
  21.5 4.2 %collective-permute-start.3 = (bf16[57,8,256]{2,1,0:T(8,128)(2,1)S(1)}, bf16[57,8,256]{2,1,0:T(8,128)(2,1)S(1)}, u32[]{:S(2)}, u32[]{:S(2)}) collective-permute-start(bf16[57,8,256]{2,1,0:T(8,128)(2,1)S(1)} %pad_maximum_fusion.3), channel_id=1, source_target_pairs={{0,1},{1,0},{2,3},{3,2},{4,5},{5,4},{6,7},{7,6},{8,9},{9,8},{10,11... | collective-permute-start | bytes 700424 | tf_op jit(solution)/shard_map/ppermute | solution.py:119
  27.7 7.0 %copy-start.3 = (f32[4,4,8,256]{3,2,0,1:T(8,128)}, f32[4,4,8,256]{3,2,0,1:T(8,128)S(1)}, u32[]{:S(2)}) copy-start(f32[4,4,8,256]{3,2,0,1:T(8,128)S(1)} %convolution_bitcast_fusion.5) | copy-start | bytes 393220
  27.7 9.8 %collective-permute-start.5 = (bf16[48,8,256]{2,1,0:T(8,128)(2,1)S(1)}, bf16[48,8,256]{2,1,0:T(8,128)(2,1)S(1)}, u32[]{:S(2)}, u32[]{:S(2)}) collective-permute-start(bf16[48,8,256]{2,1,0:T(8,128)(2,1)S(1)} %copy-done.2), channel_id=1, source_target_pairs={{1,0},{2,1},{3,2},{4,3},{5,4},{6,5},{7,6},{8,7},{9,8},{10,9},{11,1... | collective-permute-start | bytes 589832 | tf_op jit(solution)/shard_map/ppermute | solution.py:80
  29.6 7.9 %collective-permute-start.4 = (bf16[48,8,256]{2,1,0:T(8,128)(2,1)S(1)}, bf16[48,8,256]{2,1,0:T(8,128)(2,1)S(1)}, u32[]{:S(2)}, u32[]{:S(2)}) collective-permute-start(bf16[48,8,256]{2,1,0:T(8,128)(2,1)S(1)} %copy-done.2), channel_id=1, source_target_pairs={{0,1},{1,2},{2,3},{3,4},{4,5},{5,6},{6,7},{7,8},{8,9},{9,10},{10,1... | collective-permute-start | bytes 589832 | tf_op jit(solution)/shard_map/ppermute | solution.py:80
  29.7 12.3 %all-to-all-start.1 = ((bf16[16,32,256]{2,1,0:T(8,128)(2,1)}), bf16[16,32,256]{2,1,0:T(8,128)(2,1)S(1)}, u32[]{:S(2)}, u32[]{:S(2)}) async-start(bf16[16,32,256]{2,1,0:T(8,128)(2,1)} %bitcast.71), calls=%async_computation.1 | async-start | bytes 524288 | tf_op jit(solution)/shard_map/all_to_all | solution.py:196
  42.7 6.1 %slice-start = ((f32[4,4,8,256]{3,2,0,1:T(8,128)}), f32[4,1,8,256]{3,2,0,1:T(8,128)S(1)}, s32[]{:S(2)}) async-start(f32[4,4,8,256]{3,2,0,1:T(8,128)} %copy-done.3), calls=%async_computation.3 | async-start | bytes 65536 | tf_op jit(solution)/shard_map/slice | solution.py:154
  42.7 6.1 %slice-start.1 = ((f32[4,4,8,256]{3,2,0,1:T(8,128)}), f32[4,3,8,256]{3,2,0,1:T(8,128)S(1)}, s32[]{:S(2)}) async-start(f32[4,4,8,256]{3,2,0,1:T(8,128)} %copy-done.3), calls=%async_computation.4 | async-start | bytes 196608 | tf_op jit(solution)/shard_map/slice | solution.py:154
  42.7 15.9 %all-to-all-start.2 = ((bf16[16,32,256]{2,1,0:T(8,128)(2,1)}), bf16[16,32,256]{2,1,0:T(8,128)(2,1)S(1)}, u32[]{:S(2)}, u32[]{:S(2)}) async-start(bf16[16,32,256]{2,1,0:T(8,128)(2,1)} %broadcast_in_dim.108), calls=%async_computation.2 | async-start | bytes 524288 | tf_op jit(solution)/shard_map/all_to_all | solution.py:198
  58.6 1.5 %collective-permute-start.6 = (bf16[16,32,256]{2,1,0:T(8,128)(2,1)S(1)}, bf16[16,32,256]{2,1,0:T(8,128)(2,1)S(1)}, u32[]{:S(2)}, u32[]{:S(2)}) collective-permute-start(bf16[16,32,256]{2,1,0:T(8,128)(2,1)S(1)} %all-to-all-done.2), channel_id=1, source_target_pairs={{0,1},{1,0},{2,3},{3,2},{4,5},{5,4},{6,7},{7,6},{8,9},{9,8},{10,11... | collective-permute-start | bytes 786440 | tf_op jit(solution)/shard_map/ppermute | solution.py:213

commit v5 on v4

--- a/solution.py
+++ b/solution.py
@@ -82,8 +82,9 @@
     def polar_slab(field, height):
         return lax.dynamic_slice_in_dim(field, jnp.where(is_top, 0, lat_count - height), height, 0)
 
-    signal_left, signal_right = sector_edges(signal)
-    both = lax.optimization_barrier(jnp.stack([signal, cotangent]))
+    signal_left = lax.ppermute(signal, LON, to_right)
+    both, after = lax.optimization_barrier((jnp.stack([signal, cotangent]), signal))
+    signal_right = lax.ppermute(after, LON, to_left)
 
     polar_rows = jnp.concatenate([polar_slab(both[0], SLAB), polar_slab(both[1], P_SIZE)])
     fill = jnp.zeros((SLAB + P_SIZE - 2 * R, lon_count, channels), signal.dtype)

time: 61.8 us -> 61.1 us (0.989)
  starting transfers between devices: 24.3 us -> 20.6 us
  waiting for transfers between devices: 16.2 us -> 19.2 us
    ppermute x2 -> x1, starting transfers between devices: 7.36 us -> 1.69 us  [sector_edges(): lax.ppermute(field, LON, to_left)]
    ppermute x0 -> x2, starting transfers between devices: none -> 5.58 us  [the longest x1 5.08 us: local(): signal_right = lax.ppermute(after, LON, to_left)]
    all_to_all x1, waiting for transfers between devices: 0.01 us -> 4.34 us  [local(): lax.all_to_all(sent.reshape((-1,) + polar_rows.shape), CHIPS, 0, 0)]
    ppermute x1, starting transfers between devices: 3.1 us -> 0.07 us  [local(): lax.ppermute(jnp.concatenate([even.reshape((-1,) + even.shape[2:]), facin...]
    ppermute x2 -> x1, waiting for transfers between devices: 2.42 us -> 0.51 us  [sector_edges(): lax.ppermute(field, LON, to_right)]
    ppermute x1, starting transfers between devices: 1.53 us -> 0.07 us  [local(): kept = kept + lax.ppermute(given, 'core', swap).astype(jnp.float32)]
    all_to_all x1, starting transfers between devices: 3.54 us -> 4.58 us  [local(): lax.all_to_all(sent.reshape((-1,) + polar_rows.shape), CHIPS, 0, 0)]
    unnamed x23, local copies, waits for them, and re-layouts: 1.97 us -> 1.02 us
where the time goes in v5:
time: 61.1 us; the launch traced here: 60.5 us
  starting transfers between devices  20.6 us (34%)
  waiting for transfers between devices  19.2 us (31%)
  matrix products  7.98 us (13%)
  local copies, waits for them, and re-layouts  7.25 us (12%)
  other arithmetic  4.2 us (7%)
  between operations  1.28 us (2%)
    dot_general x11, matrix products, dot(): return jnp.einsum(spec, a, b, preferred_element_type=jnp.float32)  7.98 us
    all_to_all x1, waiting for transfers between devices, local(): lax.all_to_all(jnp.broadcast_to(chunk[None], (group,) + chunk.shape), CHI...  6.98 us
    ppermute x1, starting transfers between devices, local(): signal_right = lax.ppermute(after, LON, to_left)  5.08 us
    all_to_all x1, starting transfers between devices, local(): lax.all_to_all(jnp.broadcast_to(chunk[None], (group,) + chunk.shape), CHI...  5.01 us
    all_to_all x1, waiting for transfers between devices, local(): parts = lax.all_to_all(bf16(kept).reshape(group, -1, channels), CHIPS, 0, 0)  4.72 us
    all_to_all x1, starting transfers between devices, local(): lax.all_to_all(sent.reshape((-1,) + polar_rows.shape), CHIPS, 0, 0)  4.58 us
    all_to_all x1, waiting for transfers between devices, local(): lax.all_to_all(sent.reshape((-1,) + polar_rows.shape), CHIPS, 0, 0)  4.34 us
    all_to_all x1, starting transfers between devices, local(): parts = lax.all_to_all(bf16(kept).reshape(group, -1, channels), CHIPS, 0, 0)  3.54 us
  transfers between devices with their start and end apart: 10, of which 6 were waited for; matrix products, arithmetic and copies ran while one was open for 25% of the time, Pallas kernels for 0%

profile of v5, /device:TPU:0, one launch (start us, length us, event | category | flops | bytes accessed | tf_op | source)
XLA Modules:
  0.0 60.5 jit_solution(896108427907497192)
XLA Ops:
  0.6 0.0 copy-start
  0.6 0.5 collective-permute-start
  1.2 1.1 %pad_maximum_fusion.2 = bf16[2,48,8,256]{3,2,1,0:T(8,128)(2,1)S(1)} fusion(bf16[1,48,8,256]{3,2,1,0:T(8,128)(2,1)} %bitcast.255, bf16[1,48,8,256]{3,2,1,0:T(8,128)(2,1)} %bitcast.254), kind=kLoop, calls=%fused_computation.54 | loop fusion | flops 196608 | bytes 786432 | tf_op jit(solution)/shard_map/stack | solution.py:86
  2.2 0.0 copy-start.6
  2.2 0.0 copy-start.5
  2.2 5.1 %collective-permute-start.1 = (bf16[48,8,256]{2,1,0:T(8,128)(2,1)}, bf16[48,8,256]{2,1,0:T(8,128)(2,1)S(1)}, u32[]{:S(2)}, u32[]{:S(2)}) collective-permute-start(bf16[48,8,256]{2,1,0:T(8,128)(2,1)} %param.6), channel_id=1, source_target_pairs={{1,0},{2,1},{3,2},{4,3},{5,4},{6,5},{7,6},{8,7},{9,8},{10,9},{11,1... | collective-permute-start | bytes 589832 | tf_op jit(solution)/shard_map/ppermute | solution.py:87
  7.4 0.1 pad.134.clone
  7.5 0.1 maximum_maximum_fusion
  7.5 0.1 select_select_fusion
  7.6 0.8 %broadcast_in_dim.68 = bf16[2,8,5,8,256]{4,3,2,1,0:T(8,128)(2,1)} broadcast(bf16[2,5,8,256]{3,2,1,0:T(8,128)(2,1)S(1)} %select_select_fusion), dimensions={0,2,3,4} | broadcast | bytes 368640 | tf_op jit(solution)/shard_map/broadcast_in_dim | solution.py:96
  8.4 4.6 %all-to-all-start = ((bf16[16,5,8,256]{3,2,1,0:T(8,128)(2,1)}), bf16[16,5,8,256]{3,2,1,0:T(8,128)(2,1)S(1)}, u32[]{:S(2)}, u32[]{:S(2)}) async-start(bf16[16,5,8,256]{3,2,1,0:T(8,128)(2,1)} %bitcast.46), calls=%async_computation | async-start | bytes 655360 | tf_op jit(solution)/shard_map/all_to_all | solution.py:97
  13.1 0.1 pad.108.clone
  13.2 0.1 add_select_fusion
  13.3 0.1 add_select_fusion.1
  13.3 0.0 collective-permute-done
  13.3 0.0 collective-permute-done.1
  13.4 0.0 copy-start.4
  13.5 0.1 pad_dynamic-slice_fusion
  13.6 0.1 compare_and_fusion
  13.6 0.1 dynamic-slice_select_fusion
  13.7 0.3 copy-done.4
  14.0 0.2 fusion.43
  14.2 0.4 fusion.13
  14.6 0.0 copy-start.1
  14.6 1.1 %copy.83 = bf16[48,4,8,3,24]{4,2,3,1,0:T(8,128)(2,1)S(1)} copy(bf16[48,4,8,3,24]{0,4,3,1,2:T(8,128)(2,1)S(1)} %fusion.13) | data formatting | bytes 442368 | tf_op jit(solution)/shard_map/convert_element_type | solution.py:24
  15.7 0.9 %constant_dynamic-update-slice_fusion = bf16[48,24,256]{2,1,0:T(8,128)(2,1)S(1)} fusion(bf16[48,24,256]{2,1,0:T(8,128)(2,1)S(1)} %constant_dynamic-update-slice_fusion.1, bf16[48,8,256]{2,1,0:T(8,128)(2,1)} %copy-done.4), kind=kLoop, calls=%fused_computation.104 | loop fusion | bytes 393216 | tf_op jit(solution)/shard_map/concatenate | solution.py:48
  16.7 0.1 slice_bitcast_fusion.3
  16.8 0.0 copy-start.2
  16.8 0.7 %fusion.12 = bf16[4,48,8,256]{3,2,0,1:T(8,128)(2,1)S(1)} fusion(bf16[48,4,8,3,24]{4,2,3,1,0:T(8,128)(2,1)S(1)} %copy.83, bf16[48,1,24,256]{3,2,1,0:T(8,128)(2,1)S(1)} %get-tuple-element.42, bf16[48,1,24,256]{3,2,1,0:T(8,128)(2,1)S(1)} %bitcast.250, bf16[48,1,24,256]{3,2,1,0:T(8,128)(2,1)S(1)} %get-tuple-element.41), kind=kOutput, calls=%fused_computation.20 | convolution fusion | flops 58785792 | bytes 2777088 | tf_op jit(solution)/shard_map/ikarm,irmc->ikac/dot_general | solution.py:20
  17.5 0.2 copy-done.2
  17.7 0.5 fusion.11
  18.2 0.4 copy-done.8
  18.6 0.1 collective-permute-start.2
  18.8 0.1 slice.186
  18.9 0.1 slice.182
  18.9 0.1 maximum_bitcast_fusion.21
  19.0 0.1 slice_select_fusion
  19.1 4.3 %all-to-all-done = bf16[16,5,8,256]{3,2,1,0:T(8,128)(2,1)S(1)} async-done(((bf16[16,5,8,256]{3,2,1,0:T(8,128)(2,1)}), bf16[16,5,8,256]{3,2,1,0:T(8,128)(2,1)S(1)}, u32[]{:S(2)}, u32[]{:S(2)}) %all-to-all-start) | async-done | bytes 327712 | tf_op jit(solution)/shard_map/all_to_all | solution.py:97
  23.6 0.1 collective-permute-start.3
  23.7 0.3 fusion.18
  24.0 1.1 %collective-permute-done.3 = bf16[57,8,256]{2,1,0:T(8,128)(2,1)S(1)} collective-permute-done((bf16[57,8,256]{2,1,0:T(8,128)(2,1)S(1)}, bf16[57,8,256]{2,1,0:T(8,128)(2,1)S(1)}, u32[]{:S(2)}, u32[]{:S(2)}) %collective-permute-start.3) | collective-permute-done | bytes 233504 | tf_op jit(solution)/shard_map/ppermute | solution.py:120
  25.4 0.2 convolution_bitcast_fusion.4
  25.6 0.3 fusion.15
  25.9 0.8 %bitcast_add_fusion.1 = bf16[512,256]{1,0:T(8,128)(2,1)} fusion(f32[2,256,256]{2,1,0:T(8,128)S(1)} %fusion.15, f32[2,256,256]{2,1,0:T(8,128)S(1)} %slice_select_fusion, bf16[512,256]{1,0:T(8,128)(2,1)S(1)} %collective-permute-done.2), kind=kLoop, calls=%fused_computation.46 | loop fusion | flops 524288 | bytes 1572864 | tf_op jit(solution)/shard_map/add | solution.py:194
  26.7 0.2 fusion.19
  26.9 0.2 convolution_bitcast_fusion.5
  27.1 0.0 copy-start.3
  27.1 1.7 %collective-permute-start.5 = (bf16[48,8,256]{2,1,0:T(8,128)(2,1)S(1)}, bf16[48,8,256]{2,1,0:T(8,128)(2,1)S(1)}, u32[]{:S(2)}, u32[]{:S(2)}) collective-permute-start(bf16[48,8,256]{2,1,0:T(8,128)(2,1)S(1)} %copy-done.2), channel_id=1, source_target_pairs={{1,0},{2,1},{3,2},{4,3},{5,4},{6,5},{7,6},{8,7},{9,8},{10,9},{11,1... | collective-permute-start | bytes 589832 | tf_op jit(solution)/shard_map/ppermute | solution.py:80
  28.8 0.1 fusion.84
  28.9 3.5 %all-to-all-start.1 = ((bf16[16,32,256]{2,1,0:T(8,128)(2,1)}), bf16[16,32,256]{2,1,0:T(8,128)(2,1)S(1)}, u32[]{:S(2)}, u32[]{:S(2)}) async-start(bf16[16,32,256]{2,1,0:T(8,128)(2,1)} %bitcast.71), calls=%async_computation.1 | async-start | bytes 524288 | tf_op jit(solution)/shard_map/all_to_all | solution.py:197
  32.5 0.4 fusion.14
  32.9 1.1 %copy.101 = bf16[48,4,8,3,24]{4,2,3,1,0:T(8,128)(2,1)S(1)} copy(bf16[48,4,8,3,24]{0,4,3,1,2:T(8,128)(2,1)S(1)} %fusion.14) | data formatting | bytes 442368 | tf_op jit(solution)/shard_map/convert_element_type | solution.py:24
  34.0 2.2 %fusion.16 = bf16[48,8,256]{2,1,0:T(8,128)(2,1)} fusion(f32[4,1,8,256]{3,2,0,1:T(8,128)S(1)} %constant_dynamic-slice_fusion.1, f32[4,2,8,256]{3,2,0,1:T(8,128)S(1)} %constant_dynamic-slice_fusion, bf16[4,48,8,256]{3,2,0,1:T(8,128)(2,1)} %copy-done.8, pred[]{:T(512)S(6)} %eq.89, bf16[4,256,256]{2,1,0:T(8,128)(2,1)S(1)} %copy-done), kind=kOutput, calls=%fused_computation.27 | convolution fusion | flops 203784192 | bytes 1605633 | tf_op jit(solution)/shard_map/kiac,kce->iae/dot_general | solution.py:20
  36.1 0.5 collective-permute-done.4
  36.7 4.7 %all-to-all-done.1 = bf16[16,32,256]{2,1,0:T(8,128)(2,1)S(1)} async-done(((bf16[16,32,256]{2,1,0:T(8,128)(2,1)}), bf16[16,32,256]{2,1,0:T(8,128)(2,1)S(1)}, u32[]{:S(2)}, u32[]{:S(2)}) %all-to-all-start.1) | async-done | bytes 262176 | tf_op jit(solution)/shard_map/all_to_all | solution.py:197
  41.5 0.7 %broadcast_in_dim.108 = bf16[16,32,256]{2,1,0:T(8,128)(2,1)} broadcast(bf16[32,256]{1,0:T(8,128)(2,1)S(1)} %reduce_sum.12), dimensions={1,2} | broadcast | bytes 278528 | tf_op jit(solution)/shard_map/broadcast_in_dim | solution.py:199
  42.2 5.0 %all-to-all-start.2 = ((bf16[16,32,256]{2,1,0:T(8,128)(2,1)}), bf16[16,32,256]{2,1,0:T(8,128)(2,1)S(1)}, u32[]{:S(2)}, u32[]{:S(2)}) async-start(bf16[16,32,256]{2,1,0:T(8,128)(2,1)} %broadcast_in_dim.108), calls=%async_computation.2 | async-start | bytes 524288 | tf_op jit(solution)/shard_map/all_to_all | solution.py:199
  47.2 0.9 %slice_bitcast_fusion.1 = (bf16[48,1,24,256]{3,2,1,0:T(8,128)(2,1)S(1)}, bf16[48,1,24,256]{3,2,1,0:T(8,128)(2,1)}) fusion(bf16[48,24,256]{2,1,0:T(8,128)(2,1)S(1)} %constant_dynamic-update-slice_fusion.3), kind=kLoop, calls=%fused_computation.40 | loop fusion | bytes 1769472 | tf_op jit(solution)/shard_map/stack | solution.py:50
  48.1 2.7 %fusion.17 = bf16[48,8,256]{2,1,0:T(8,128)(2,1)} fusion(f32[4,1,8,256]{3,2,0,1:T(8,128)S(1)} %slice-done, f32[4,3,8,256]{3,2,0,1:T(8,128)S(1)} %slice-done.1, bf16[48,4,8,3,24]{4,2,3,1,0:T(8,128)(2,1)S(1)} %copy.101, bf16[48,1,24,256]{3,2,1,0:T(8,128)(2,1)} %get-tuple-element.40, bf16[48,1,24,256]{3,2,1,0:T(8,128)(2,1)S(1)} %bitcast.251, ...), kind=kOutput, calls=%fused_computation.28 | convolution fusion | flops 261783552 | bytes 2842625 | tf_op jit(solution)/shard_map/kjbe,kce->jbc/dot_general | solution.py:20
  50.8 7.0 %all-to-all-done.2 = bf16[16,32,256]{2,1,0:T(8,128)(2,1)S(1)} async-done(((bf16[16,32,256]{2,1,0:T(8,128)(2,1)}), bf16[16,32,256]{2,1,0:T(8,128)(2,1)S(1)}, u32[]{:S(2)}, u32[]{:S(2)}) %all-to-all-start.2) | async-done | bytes 262176 | tf_op jit(solution)/shard_map/all_to_all | solution.py:199
  57.8 0.0 collective-permute-start.6
  57.8 1.5 %collective-permute-done.6 = bf16[16,32,256]{2,1,0:T(8,128)(2,1)S(1)} collective-permute-done((bf16[16,32,256]{2,1,0:T(8,128)(2,1)S(1)}, bf16[16,32,256]{2,1,0:T(8,128)(2,1)S(1)}, u32[]{:S(2)}, u32[]{:S(2)}) %collective-permute-start.6) | collective-permute-done | bytes 262176 | tf_op jit(solution)/shard_map/ppermute | solution.py:214
  59.4 0.1 pad_maximum_fusion
  59.4 1.1 %convert.2 = f32[4,256,256]{2,1,0:T(8,128)} convert(bf16[4,256,256]{2,1,0:T(8,128)(2,1)S(1)} %bitcast.248) | non-fusion elementwise | flops 262144 | bytes 1572864 | tf_op jit(solution)/shard_map/convert_element_type | solution.py:216
  (64 shorter events, 0.8 us)
Async XLA Ops:
  0.6 33.3 %copy-start = (bf16[4,256,256]{2,1,0:T(8,128)(2,1)S(1)}, bf16[4,256,256]{2,1,0:T(8,128)(2,1)}, u32[]{:S(2)}) copy-start(bf16[4,256,256]{2,1,0:T(8,128)(2,1)} %param.8) | copy-start | bytes 1572868
  0.6 12.7 %collective-permute-start = (bf16[48,8,256]{2,1,0:T(8,128)(2,1)}, bf16[48,8,256]{2,1,0:T(8,128)(2,1)S(1)}, u32[]{:S(2)}, u32[]{:S(2)}) collective-permute-start(bf16[48,8,256]{2,1,0:T(8,128)(2,1)} %param.6), channel_id=1, source_target_pairs={{0,1},{1,2},{2,3},{3,4},{4,5},{5,6},{6,7},{7,8},{8,9},{9,10},{10,1... | collective-permute-start | bytes 589832 | tf_op jit(solution)/shard_map/ppermute | solution.py:85
  2.2 11.1 %copy-start.6 = (bf16[4,4,3,128]{3,1,2,0:T(4,128)(2,1)S(1)}, bf16[4,4,3,128]{3,1,2,0:T(4,128)(2,1)}, u32[]{:S(2)}) copy-start(bf16[4,4,3,128]{3,1,2,0:T(4,128)(2,1)} %param.10) | copy-start | bytes 36868
  2.2 11.2 %copy-start.5 = (bf16[4,96,3,17]{1,0,3,2:T(4,128)(2,1)S(1)}, bf16[4,96,3,17]{1,0,3,2:T(4,128)(2,1)}, u32[]{:S(2)}) copy-start(bf16[4,96,3,17]{1,0,3,2:T(4,128)(2,1)} %param.9) | copy-start | bytes 117508
  2.2 11.1 %collective-permute-start.1 = (bf16[48,8,256]{2,1,0:T(8,128)(2,1)}, bf16[48,8,256]{2,1,0:T(8,128)(2,1)S(1)}, u32[]{:S(2)}, u32[]{:S(2)}) collective-permute-start(bf16[48,8,256]{2,1,0:T(8,128)(2,1)} %param.6), channel_id=1, source_target_pairs={{1,0},{2,1},{3,2},{4,3},{5,4},{6,5},{7,6},{8,7},{9,8},{10,9},{11,1... | collective-permute-start | bytes 589832 | tf_op jit(solution)/shard_map/ppermute | solution.py:87
  7.3 6.1 %copy-start.7 = (s32[96]{0:T(128)S(1)}, s32[96]{0:T(128)}, u32[]{:S(2)}) copy-start(s32[96]{0:T(128)} %param.11) | copy-start | bytes 1156
  8.4 15.1 %all-to-all-start = ((bf16[16,5,8,256]{3,2,1,0:T(8,128)(2,1)}), bf16[16,5,8,256]{3,2,1,0:T(8,128)(2,1)S(1)}, u32[]{:S(2)}, u32[]{:S(2)}) async-start(bf16[16,5,8,256]{3,2,1,0:T(8,128)(2,1)} %bitcast.46), calls=%async_computation | async-start | bytes 655360 | tf_op jit(solution)/shard_map/all_to_all | solution.py:97
  13.4 0.7 %copy-start.4 = (bf16[48,8,256]{2,1,0:T(8,128)(2,1)}, bf16[48,8,256]{2,1,0:T(8,128)(2,1)S(1)}, u32[]{:S(2)}) copy-start(bf16[48,8,256]{2,1,0:T(8,128)(2,1)S(1)} %collective-permute-done.1) | copy-start | bytes 589828
  14.6 1.1 %copy-start.1 = (bf16[48,8,256]{2,1,0:T(8,128)(2,1)S(1)}, bf16[48,8,256]{2,1,0:T(8,128)(2,1)}, u32[]{:S(2)}) copy-start(bf16[48,8,256]{2,1,0:T(8,128)(2,1)} %param.6) | copy-start | bytes 589828
  16.8 0.9 %copy-start.2 = (bf16[48,8,256]{2,1,0:T(8,128)(2,1)S(1)}, bf16[48,8,256]{2,1,0:T(8,128)(2,1)}, u32[]{:S(2)}) copy-start(bf16[48,8,256]{2,1,0:T(8,128)(2,1)} %param.7) | copy-start | bytes 589828
  17.7 0.9 %copy-start.8 = (bf16[4,48,8,256]{3,2,0,1:T(8,128)(2,1)}, bf16[4,48,8,256]{3,2,0,1:T(8,128)(2,1)S(1)}, u32[]{:S(2)}) copy-start(bf16[4,48,8,256]{3,2,0,1:T(8,128)(2,1)S(1)} %fusion.12) | copy-start | bytes 2359300
  18.6 7.2 %collective-permute-start.2 = (bf16[512,256]{1,0:T(8,128)(2,1)S(1)}, bf16[512,256]{1,0:T(8,128)(2,1)S(1)}, u32[]{:S(2)}, u32[]{:S(2)}) collective-permute-start(bf16[512,256]{1,0:T(8,128)(2,1)S(1)} %bitcast.256), channel_id=1, source_target_pairs={{0,1},{1,0},{2,3},{3,2},{4,5},{5,4},{6,7},{7,6},{8,9},{9,8},{10,11... | collective-permute-start | bytes 786440 | tf_op jit(solution)/shard_map/ppermute | solution.py:175
  23.6 1.6 %collective-permute-start.3 = (bf16[57,8,256]{2,1,0:T(8,128)(2,1)S(1)}, bf16[57,8,256]{2,1,0:T(8,128)(2,1)S(1)}, u32[]{:S(2)}, u32[]{:S(2)}) collective-permute-start(bf16[57,8,256]{2,1,0:T(8,128)(2,1)S(1)} %pad_maximum_fusion.3), channel_id=1, source_target_pairs={{0,1},{1,0},{2,3},{3,2},{4,5},{5,4},{6,7},{7,6},{8,9},{9,8},{10,11... | collective-permute-start | bytes 700424 | tf_op jit(solution)/shard_map/ppermute | solution.py:120
  27.1 6.8 %copy-start.3 = (f32[4,4,8,256]{3,2,0,1:T(8,128)}, f32[4,4,8,256]{3,2,0,1:T(8,128)S(1)}, u32[]{:S(2)}) copy-start(f32[4,4,8,256]{3,2,0,1:T(8,128)S(1)} %convolution_bitcast_fusion.5) | copy-start | bytes 393220
  27.1 9.6 %collective-permute-start.5 = (bf16[48,8,256]{2,1,0:T(8,128)(2,1)S(1)}, bf16[48,8,256]{2,1,0:T(8,128)(2,1)S(1)}, u32[]{:S(2)}, u32[]{:S(2)}) collective-permute-start(bf16[48,8,256]{2,1,0:T(8,128)(2,1)S(1)} %copy-done.2), channel_id=1, source_target_pairs={{1,0},{2,1},{3,2},{4,3},{5,4},{6,5},{7,6},{8,7},{9,8},{10,9},{11,1... | collective-permute-start | bytes 589832 | tf_op jit(solution)/shard_map/ppermute | solution.py:80
  28.8 7.9 %collective-permute-start.4 = (bf16[48,8,256]{2,1,0:T(8,128)(2,1)S(1)}, bf16[48,8,256]{2,1,0:T(8,128)(2,1)S(1)}, u32[]{:S(2)}, u32[]{:S(2)}) collective-permute-start(bf16[48,8,256]{2,1,0:T(8,128)(2,1)S(1)} %copy-done.2), channel_id=1, source_target_pairs={{0,1},{1,2},{2,3},{3,4},{4,5},{5,6},{6,7},{7,8},{8,9},{9,10},{10,1... | collective-permute-start | bytes 589832 | tf_op jit(solution)/shard_map/ppermute | solution.py:80
  28.9 12.6 %all-to-all-start.1 = ((bf16[16,32,256]{2,1,0:T(8,128)(2,1)}), bf16[16,32,256]{2,1,0:T(8,128)(2,1)S(1)}, u32[]{:S(2)}, u32[]{:S(2)}) async-start(bf16[16,32,256]{2,1,0:T(8,128)(2,1)} %bitcast.71), calls=%async_computation.1 | async-start | bytes 524288 | tf_op jit(solution)/shard_map/all_to_all | solution.py:197
  42.2 5.9 %slice-start = ((f32[4,4,8,256]{3,2,0,1:T(8,128)}), f32[4,1,8,256]{3,2,0,1:T(8,128)S(1)}, s32[]{:S(2)}) async-start(f32[4,4,8,256]{3,2,0,1:T(8,128)} %copy-done.3), calls=%async_computation.3 | async-start | bytes 65536 | tf_op jit(solution)/shard_map/slice | solution.py:155
  42.2 5.9 %slice-start.1 = ((f32[4,4,8,256]{3,2,0,1:T(8,128)}), f32[4,3,8,256]{3,2,0,1:T(8,128)S(1)}, s32[]{:S(2)}) async-start(f32[4,4,8,256]{3,2,0,1:T(8,128)} %copy-done.3), calls=%async_computation.4 | async-start | bytes 196608 | tf_op jit(solution)/shard_map/slice | solution.py:155
  42.2 15.6 %all-to-all-start.2 = ((bf16[16,32,256]{2,1,0:T(8,128)(2,1)}), bf16[16,32,256]{2,1,0:T(8,128)(2,1)S(1)}, u32[]{:S(2)}, u32[]{:S(2)}) async-start(bf16[16,32,256]{2,1,0:T(8,128)(2,1)} %broadcast_in_dim.108), calls=%async_computation.2 | async-start | bytes 524288 | tf_op jit(solution)/shard_map/all_to_all | solution.py:199
  57.8 1.5 %collective-permute-start.6 = (bf16[16,32,256]{2,1,0:T(8,128)(2,1)S(1)}, bf16[16,32,256]{2,1,0:T(8,128)(2,1)S(1)}, u32[]{:S(2)}, u32[]{:S(2)}) collective-permute-start(bf16[16,32,256]{2,1,0:T(8,128)(2,1)S(1)} %all-to-all-done.2), channel_id=1, source_target_pairs={{0,1},{1,0},{2,3},{3,2},{4,5},{5,4},{6,7},{7,6},{8,9},{9,8},{10,11... | collective-permute-start | bytes 786440 | tf_op jit(solution)/shard_map/ppermute | solution.py:214

commit v6 on v5

--- a/solution.py
+++ b/solution.py
@@ -172,6 +172,8 @@
     partial = (dot("kiac,iae->kce", banded, cotangent) * scale).reshape(2, -1, channels)
     given = bf16(jnp.where(core == 0, partial[1], partial[0]))
     kept = jnp.where(core == 0, partial[0], partial[1])
+    given, late = lax.optimization_barrier((given, cotangent))
+    cot_left, cot_right = sector_edges(late)
     kept = kept + lax.ppermute(given, "core", swap).astype(jnp.float32)
 
     slab_kernel, edge_forward, edge_adjoint, _ = lax.optimization_barrier((slab_kernel, edge_forward, edge_adjoint, given))
@@ -197,8 +199,7 @@
     parts = lax.all_to_all(bf16(kept).reshape(group, -1, channels), CHIPS, 0, 0)
     chunk = bf16(jnp.sum(parts.astype(jnp.float32), axis=0))
     half = lax.all_to_all(jnp.broadcast_to(chunk[None], (group,) + chunk.shape), CHIPS, 0, 0)
-    coeffs, adjoint_kernel, extra, late, kept = lax.optimization_barrier((coeffs, adjoint_kernel, extra, cotangent, kept))
-    cot_left, cot_right = sector_edges(late)
+    coeffs, adjoint_kernel, extra, kept = lax.optimization_barrier((coeffs, adjoint_kernel, extra, kept))
     own_extra = lax.dynamic_slice_in_dim(extra, core * lon_count, lon_count, 2)
     filtered = bf16(banded + placed(own_extra, P_SIZE))
     conv_output = bf16(dot("kiac,kce->iae", filtered, weights))
@@ -206,6 +207,7 @@
     adjoint_rows = jnp.stack([coeffs[:, t : t + lat_count, 2 * R - t] for t in range(TAPS)], axis=2)
     adjoint = band_matrices(adjoint_rows, lon_count, False)
     adjoint_cycle = bf16(dot("kspd,dbm->ksbpm", adjoint_kernel, bf16(opposite[None] == lags)))
+    cot_left, cot_right, _ = lax.optimization_barrier((cot_left, cot_right, chunk))
     spread = dot("ikarm,irme->ikae", adjoint, windows(cot_left, cotangent, cot_right))
     spread = jnp.moveaxis(spread, 1, 0)
     spread = spread + placed(dot("ksbpm,pme->ksbe", adjoint_cycle, cot_circle), SLAB)

time: 61.1 us -> 60.6 us (level)
  waiting for transfers between devices: 19.2 us -> 13.3 us
  starting transfers between devices: 20.6 us -> 23.6 us
  local copies, waits for them, and re-layouts: 7.25 us -> 8.66 us
  matrix products: 7.98 us -> 8.9 us
    all_to_all x1, waiting for transfers between devices: 4.34 us -> 0.27 us  [local(): lax.all_to_all(sent.reshape((-1,) + polar_rows.shape), CHIPS, 0, 0)]
    all_to_all x1, starting transfers between devices: 3.54 us -> 6.85 us  [local(): parts = lax.all_to_all(bf16(kept).reshape(group, -1, channels), CHIPS, 0, 0)]
    all_to_all x1, waiting for transfers between devices: 6.98 us -> 4.56 us  [local(): lax.all_to_all(jnp.broadcast_to(chunk[None], (group,) + chunk.shape), CHI...]
    all_to_all x1, starting transfers between devices: 5.01 us -> 3.53 us  [local(): lax.all_to_all(jnp.broadcast_to(chunk[None], (group,) + chunk.shape), CHI...]
    unnamed x23 -> x21, local copies, waits for them, and re-layouts: 1.02 us -> 2.42 us
    all_to_all x1, waiting for transfers between devices: 4.72 us -> 6.05 us  [local(): parts = lax.all_to_all(bf16(kept).reshape(group, -1, channels), CHIPS, 0, 0)]
    ppermute x1, starting transfers between devices: 1.69 us -> 2.68 us  [sector_edges(): lax.ppermute(field, LON, to_left)]
    dot_general x11, matrix products: 7.98 us -> 8.9 us  [dot(): return jnp.einsum(spec, a, b, preferred_element_type=jnp.float32)]
  transfers between devices with their start and end apart: 10 -> 10, of which waited for: 6 -> 5; matrix products, arithmetic and copies ran while one was open for 25% -> 31% of each run, Pallas kernels for 0% -> 0%
where the time goes in v6:
time: 60.6 us; the launch traced here: 60 us
  starting transfers between devices  23.6 us (39%)
  waiting for transfers between devices  13.3 us (22%)
  matrix products  8.9 us (15%)
  local copies, waits for them, and re-layouts  8.66 us (14%)
  other arithmetic  4.23 us (7%)
  between operations  1.27 us (2%)
    dot_general x11, matrix products, dot(): return jnp.einsum(spec, a, b, preferred_element_type=jnp.float32)  8.9 us
    all_to_all x1, starting transfers between devices, local(): parts = lax.all_to_all(bf16(kept).reshape(group, -1, channels), CHIPS, 0, 0)  6.85 us
    all_to_all x1, waiting for transfers between devices, local(): parts = lax.all_to_all(bf16(kept).reshape(group, -1, channels), CHIPS, 0, 0)  6.05 us
    ppermute x1, starting transfers between devices, local(): signal_right = lax.ppermute(after, LON, to_left)  5.08 us
    all_to_all x1, starting transfers between devices, local(): lax.all_to_all(sent.reshape((-1,) + polar_rows.shape), CHIPS, 0, 0)  4.58 us
    all_to_all x1, waiting for transfers between devices, local(): lax.all_to_all(jnp.broadcast_to(chunk[None], (group,) + chunk.shape), CHI...  4.56 us
    all_to_all x1, starting transfers between devices, local(): lax.all_to_all(jnp.broadcast_to(chunk[None], (group,) + chunk.shape), CHI...  3.53 us
    ppermute x1, starting transfers between devices, sector_edges(): lax.ppermute(field, LON, to_left)  2.68 us
  transfers between devices with their start and end apart: 10, of which 5 were waited for; matrix products, arithmetic and copies ran while one was open for 31% of the time, Pallas kernels for 0%

profile of v6, /device:TPU:0, one launch (start us, length us, event | category | flops | bytes accessed | tf_op | source)
XLA Modules:
  0.0 60.0 jit_solution(14401727053329189046)
XLA Ops:
  0.6 0.0 copy-start
  0.6 0.5 collective-permute-start
  1.2 1.1 %pad_maximum_fusion.2 = bf16[2,48,8,256]{3,2,1,0:T(8,128)(2,1)S(1)} fusion(bf16[1,48,8,256]{3,2,1,0:T(8,128)(2,1)} %bitcast.3, bf16[1,48,8,256]{3,2,1,0:T(8,128)(2,1)} %bitcast.254), kind=kLoop, calls=%fused_computation.54 | loop fusion | flops 196608 | bytes 786432 | tf_op jit(solution)/shard_map/stack | solution.py:86
  2.2 0.0 copy-start.5
  2.2 0.0 copy-start.4
  2.2 5.1 %collective-permute-start.1 = (bf16[48,8,256]{2,1,0:T(8,128)(2,1)}, bf16[48,8,256]{2,1,0:T(8,128)(2,1)S(1)}, u32[]{:S(2)}, u32[]{:S(2)}) collective-permute-start(bf16[48,8,256]{2,1,0:T(8,128)(2,1)} %param.6), channel_id=1, source_target_pairs={{1,0},{2,1},{3,2},{4,3},{5,4},{6,5},{7,6},{8,7},{9,8},{10,9},{11,1... | collective-permute-start | bytes 589832 | tf_op jit(solution)/shard_map/ppermute | solution.py:87
  7.4 0.1 pad.134.clone
  7.5 0.1 maximum_maximum_fusion
  7.5 0.1 select_select_fusion
  7.6 0.8 %broadcast_in_dim.68 = bf16[2,8,5,8,256]{4,3,2,1,0:T(8,128)(2,1)} broadcast(bf16[2,5,8,256]{3,2,1,0:T(8,128)(2,1)S(1)} %select_select_fusion), dimensions={0,2,3,4} | broadcast | bytes 368640 | tf_op jit(solution)/shard_map/broadcast_in_dim | solution.py:96
  8.4 4.6 %all-to-all-start = ((bf16[16,5,8,256]{3,2,1,0:T(8,128)(2,1)}), bf16[16,5,8,256]{3,2,1,0:T(8,128)(2,1)S(1)}, u32[]{:S(2)}, u32[]{:S(2)}) async-start(bf16[16,5,8,256]{3,2,1,0:T(8,128)(2,1)} %bitcast.46), calls=%async_computation | async-start | bytes 655360 | tf_op jit(solution)/shard_map/all_to_all | solution.py:97
  13.1 0.1 pad.108.clone
  13.2 0.1 add_select_fusion
  13.3 0.1 add_select_fusion.1
  13.4 0.0 copy-start.3
  13.4 0.1 pad_dynamic-slice_fusion
  13.5 0.5 copy-done.3
  14.0 0.1 compare_and_fusion
  14.1 0.1 dynamic-slice_select_fusion
  14.2 0.2 fusion.43
  14.4 0.4 fusion.13
  14.8 0.0 copy-start.1
  14.8 1.1 %copy.83 = bf16[48,4,8,3,24]{4,2,3,1,0:T(8,128)(2,1)S(1)} copy(bf16[48,4,8,3,24]{0,4,3,1,2:T(8,128)(2,1)S(1)} %fusion.13) | data formatting | bytes 442368 | tf_op jit(solution)/shard_map/convert_element_type | solution.py:24
  15.9 0.9 %constant_dynamic-update-slice_fusion = bf16[48,24,256]{2,1,0:T(8,128)(2,1)S(1)} fusion(bf16[48,24,256]{2,1,0:T(8,128)(2,1)S(1)} %constant_dynamic-update-slice_fusion.1, bf16[48,8,256]{2,1,0:T(8,128)(2,1)} %copy-done.3), kind=kLoop, calls=%fused_computation.104 | loop fusion | bytes 393216 | tf_op jit(solution)/shard_map/concatenate | solution.py:48
  16.9 0.1 slice_bitcast_fusion.3
  17.0 0.7 %fusion.12 = bf16[4,48,8,256]{3,2,0,1:T(8,128)(2,1)S(1)} fusion(bf16[48,4,8,3,24]{4,2,3,1,0:T(8,128)(2,1)S(1)} %copy.83, bf16[48,1,24,256]{3,2,1,0:T(8,128)(2,1)S(1)} %get-tuple-element.48, bf16[48,1,24,256]{3,2,1,0:T(8,128)(2,1)S(1)} %bitcast.250, bf16[48,1,24,256]{3,2,1,0:T(8,128)(2,1)S(1)} %get-tuple-element.47), kind=kOutput, calls=%fused_computation.20 | convolution fusion | flops 58785792 | bytes 2777088 | tf_op jit(solution)/shard_map/ikarm,irmc->ikac/dot_general | solution.py:20
  17.7 0.0 copy-start.7
  17.7 0.9 %copy-done.7 = bf16[4,48,8,256]{3,2,0,1:T(8,128)(2,1)} copy-done((bf16[4,48,8,256]{3,2,0,1:T(8,128)(2,1)}, bf16[4,48,8,256]{3,2,0,1:T(8,128)(2,1)S(1)}, u32[]{:S(2)}) %copy-start.7) | copy-done | bytes 786456
  18.5 1.4 %fusion.11 = f32[4,256,256]{2,1,0:T(8,128)S(1)} fusion(bf16[4,48,8,256]{3,2,0,1:T(8,128)(2,1)S(1)} %fusion.12, bf16[48,8,256]{2,1,0:T(8,128)(2,1)} %param.7), kind=kOutput, calls=%fused_computation.17 | convolution fusion | flops 201588736 | bytes 2031616 | tf_op jit(solution)/shard_map/kiac,iae->kce/dot_general | solution.py:20
  20.0 0.1 select_convert_fusion
  20.0 2.7 %collective-permute-start.5 = (bf16[48,8,256]{2,1,0:T(8,128)(2,1)}, bf16[48,8,256]{2,1,0:T(8,128)(2,1)S(1)}, u32[]{:S(2)}, u32[]{:S(2)}) collective-permute-start(bf16[48,8,256]{2,1,0:T(8,128)(2,1)} %param.7), channel_id=1, source_target_pairs={{1,0},{2,1},{3,2},{4,3},{5,4},{6,5},{7,6},{8,7},{9,8},{10,9},{11,1... | collective-permute-start | bytes 589832 | tf_op jit(solution)/shard_map/ppermute | solution.py:80
  22.7 0.1 collective-permute-start.2
  22.9 0.1 slice.186
  22.9 0.1 slice.182
  23.0 0.1 maximum_bitcast_fusion.21
  23.1 0.1 slice_select_fusion
  23.2 0.3 all-to-all-done
  23.6 0.3 collective-permute-start.3
  23.9 0.3 fusion.18
  24.2 0.9 %collective-permute-done.3 = bf16[57,8,256]{2,1,0:T(8,128)(2,1)S(1)} collective-permute-done((bf16[57,8,256]{2,1,0:T(8,128)(2,1)S(1)}, bf16[57,8,256]{2,1,0:T(8,128)(2,1)S(1)}, u32[]{:S(2)}, u32[]{:S(2)}) %collective-permute-start.3) | collective-permute-done | bytes 233504 | tf_op jit(solution)/shard_map/ppermute | solution.py:120
  25.2 0.1 broadcast_select_fusion.1
  25.4 0.2 convolution_bitcast_fusion.4
  25.6 0.3 fusion.15
  25.9 0.8 %bitcast_add_fusion.1 = bf16[512,256]{1,0:T(8,128)(2,1)} fusion(f32[2,256,256]{2,1,0:T(8,128)S(1)} %fusion.15, f32[2,256,256]{2,1,0:T(8,128)S(1)} %slice_select_fusion, bf16[512,256]{1,0:T(8,128)(2,1)S(1)} %collective-permute-done.2), kind=kLoop, calls=%fused_computation.46 | loop fusion | flops 524288 | bytes 1572864 | tf_op jit(solution)/shard_map/add | solution.py:196
  26.7 0.1 fusion.84
  26.8 6.9 %all-to-all-start.1 = ((bf16[16,32,256]{2,1,0:T(8,128)(2,1)}), bf16[16,32,256]{2,1,0:T(8,128)(2,1)S(1)}, u32[]{:S(2)}, u32[]{:S(2)}) async-start(bf16[16,32,256]{2,1,0:T(8,128)(2,1)} %bitcast.71), calls=%async_computation.1 | async-start | bytes 524288 | tf_op jit(solution)/shard_map/all_to_all | solution.py:199
  33.6 0.2 fusion.19
  33.9 0.4 fusion.14
  34.3 0.2 convolution_bitcast_fusion.5
  34.5 1.1 %copy.101 = bf16[48,4,8,3,24]{4,2,3,1,0:T(8,128)(2,1)S(1)} copy(bf16[48,4,8,3,24]{0,4,3,1,2:T(8,128)(2,1)S(1)} %fusion.14) | data formatting | bytes 442368 | tf_op jit(solution)/shard_map/convert_element_type | solution.py:24
  35.6 2.2 %fusion.16 = bf16[48,8,256]{2,1,0:T(8,128)(2,1)} fusion(f32[4,1,8,256]{3,2,0,1:T(8,128)S(1)} %constant_dynamic-slice_fusion.1, f32[4,2,8,256]{3,2,0,1:T(8,128)S(1)} %constant_dynamic-slice_fusion, bf16[4,48,8,256]{3,2,0,1:T(8,128)(2,1)} %copy-done.7, pred[]{:T(512)S(6)} %eq.89, bf16[4,256,256]{2,1,0:T(8,128)(2,1)S(1)} %copy-done), kind=kOutput, calls=%fused_computation.27 | convolution fusion | flops 203784192 | bytes 1605633 | tf_op jit(solution)/shard_map/kiac,kce->iae/dot_general | solution.py:20
  37.8 6.1 %all-to-all-done.1 = bf16[16,32,256]{2,1,0:T(8,128)(2,1)S(1)} async-done(((bf16[16,32,256]{2,1,0:T(8,128)(2,1)}), bf16[16,32,256]{2,1,0:T(8,128)(2,1)S(1)}, u32[]{:S(2)}, u32[]{:S(2)}) %all-to-all-start.1) | async-done | bytes 262176 | tf_op jit(solution)/shard_map/all_to_all | solution.py:199
  43.9 0.7 %broadcast_in_dim.108 = bf16[16,32,256]{2,1,0:T(8,128)(2,1)} broadcast(bf16[32,256]{1,0:T(8,128)(2,1)S(1)} %reduce_sum.12), dimensions={1,2} | broadcast | bytes 278528 | tf_op jit(solution)/shard_map/broadcast_in_dim | solution.py:201
  44.6 3.5 %all-to-all-start.2 = ((bf16[16,32,256]{2,1,0:T(8,128)(2,1)}), bf16[16,32,256]{2,1,0:T(8,128)(2,1)S(1)}, u32[]{:S(2)}, u32[]{:S(2)}) async-start(bf16[16,32,256]{2,1,0:T(8,128)(2,1)} %broadcast_in_dim.108), calls=%async_computation.2 | async-start | bytes 524288 | tf_op jit(solution)/shard_map/all_to_all | solution.py:201
  48.2 0.9 %constant_dynamic-update-slice_fusion.4 = bf16[48,24,256]{2,1,0:T(8,128)(2,1)S(1)} fusion(bf16[48,24,256]{2,1,0:T(8,128)(2,1)S(1)} %constant_dynamic-update-slice_fusion.5, bf16[48,8,256]{2,1,0:T(8,128)(2,1)} %param.7), kind=kLoop, calls=%fused_computation.108 | loop fusion | bytes 393216
  49.1 0.0 slice-start
  49.1 0.0 slice-start.1
  49.1 0.9 %slice_bitcast_fusion.1 = (bf16[48,1,24,256]{3,2,1,0:T(8,128)(2,1)S(1)}, bf16[48,1,24,256]{3,2,1,0:T(8,128)(2,1)}) fusion(bf16[48,24,256]{2,1,0:T(8,128)(2,1)S(1)} %constant_dynamic-update-slice_fusion.3), kind=kLoop, calls=%fused_computation.40 | loop fusion | bytes 1769472 | tf_op jit(solution)/shard_map/stack | solution.py:50
  50.0 2.7 %fusion.17 = bf16[48,8,256]{2,1,0:T(8,128)(2,1)} fusion(f32[4,1,8,256]{3,2,0,1:T(8,128)S(1)} %slice-done, f32[4,3,8,256]{3,2,0,1:T(8,128)S(1)} %slice-done.1, bf16[48,4,8,3,24]{4,2,3,1,0:T(8,128)(2,1)S(1)} %copy.101, bf16[48,1,24,256]{3,2,1,0:T(8,128)(2,1)} %get-tuple-element.46, bf16[48,1,24,256]{3,2,1,0:T(8,128)(2,1)S(1)} %bitcast.251, ...), kind=kOutput, calls=%fused_computation.28 | convolution fusion | flops 261783552 | bytes 2842625 | tf_op jit(solution)/shard_map/kjbe,kce->jbc/dot_general | solution.py:20
  52.7 4.6 %all-to-all-done.2 = bf16[16,32,256]{2,1,0:T(8,128)(2,1)S(1)} async-done(((bf16[16,32,256]{2,1,0:T(8,128)(2,1)}), bf16[16,32,256]{2,1,0:T(8,128)(2,1)S(1)}, u32[]{:S(2)}, u32[]{:S(2)}) %all-to-all-start.2) | async-done | bytes 262176 | tf_op jit(solution)/shard_map/all_to_all | solution.py:201
  57.3 1.5 %collective-permute-done.6 = bf16[16,32,256]{2,1,0:T(8,128)(2,1)S(1)} collective-permute-done((bf16[16,32,256]{2,1,0:T(8,128)(2,1)S(1)}, bf16[16,32,256]{2,1,0:T(8,128)(2,1)S(1)}, u32[]{:S(2)}, u32[]{:S(2)}) %collective-permute-start.6) | collective-permute-done | bytes 262176 | tf_op jit(solution)/shard_map/ppermute | solution.py:216
  58.8 0.1 select_bitcast_fusion.1
  58.9 0.1 pad_maximum_fusion
  59.0 1.1 %convert.2 = f32[4,256,256]{2,1,0:T(8,128)} convert(bf16[4,256,256]{2,1,0:T(8,128)(2,1)S(1)} %bitcast.248) | non-fusion elementwise | flops 262144 | bytes 1572864 | tf_op jit(solution)/shard_map/convert_element_type | solution.py:218
  (62 shorter events, 0.6 us)
Async XLA Ops:
  0.6 34.9 %copy-start = (bf16[4,256,256]{2,1,0:T(8,128)(2,1)S(1)}, bf16[4,256,256]{2,1,0:T(8,128)(2,1)}, u32[]{:S(2)}) copy-start(bf16[4,256,256]{2,1,0:T(8,128)(2,1)} %param.8) | copy-start | bytes 1572868
  0.6 12.7 %collective-permute-start = (bf16[48,8,256]{2,1,0:T(8,128)(2,1)}, bf16[48,8,256]{2,1,0:T(8,128)(2,1)S(1)}, u32[]{:S(2)}, u32[]{:S(2)}) collective-permute-start(bf16[48,8,256]{2,1,0:T(8,128)(2,1)} %param.6), channel_id=1, source_target_pairs={{0,1},{1,2},{2,3},{3,4},{4,5},{5,6},{6,7},{7,8},{8,9},{9,10},{10,1... | collective-permute-start | bytes 589832 | tf_op jit(solution)/shard_map/ppermute | solution.py:85
  2.2 11.1 %copy-start.5 = (bf16[4,4,3,128]{3,1,2,0:T(4,128)(2,1)S(1)}, bf16[4,4,3,128]{3,1,2,0:T(4,128)(2,1)}, u32[]{:S(2)}) copy-start(bf16[4,4,3,128]{3,1,2,0:T(4,128)(2,1)} %param.10) | copy-start | bytes 36868
  2.2 11.2 %copy-start.4 = (bf16[4,96,3,17]{1,0,3,2:T(4,128)(2,1)S(1)}, bf16[4,96,3,17]{1,0,3,2:T(4,128)(2,1)}, u32[]{:S(2)}) copy-start(bf16[4,96,3,17]{1,0,3,2:T(4,128)(2,1)} %param.9) | copy-start | bytes 117508
  2.2 11.1 %collective-permute-start.1 = (bf16[48,8,256]{2,1,0:T(8,128)(2,1)}, bf16[48,8,256]{2,1,0:T(8,128)(2,1)S(1)}, u32[]{:S(2)}, u32[]{:S(2)}) collective-permute-start(bf16[48,8,256]{2,1,0:T(8,128)(2,1)} %param.6), channel_id=1, source_target_pairs={{1,0},{2,1},{3,2},{4,3},{5,4},{6,5},{7,6},{8,7},{9,8},{10,9},{11,1... | collective-permute-start | bytes 589832 | tf_op jit(solution)/shard_map/ppermute | solution.py:87
  7.3 6.1 %copy-start.6 = (s32[96]{0:T(128)S(1)}, s32[96]{0:T(128)}, u32[]{:S(2)}) copy-start(s32[96]{0:T(128)} %param.11) | copy-start | bytes 1156
  8.4 15.1 %all-to-all-start = ((bf16[16,5,8,256]{3,2,1,0:T(8,128)(2,1)}), bf16[16,5,8,256]{3,2,1,0:T(8,128)(2,1)S(1)}, u32[]{:S(2)}, u32[]{:S(2)}) async-start(bf16[16,5,8,256]{3,2,1,0:T(8,128)(2,1)} %bitcast.46), calls=%async_computation | async-start | bytes 655360 | tf_op jit(solution)/shard_map/all_to_all | solution.py:97
  13.4 0.7 %copy-start.3 = (bf16[48,8,256]{2,1,0:T(8,128)(2,1)}, bf16[48,8,256]{2,1,0:T(8,128)(2,1)S(1)}, u32[]{:S(2)}) copy-start(bf16[48,8,256]{2,1,0:T(8,128)(2,1)S(1)} %collective-permute-done.1) | copy-start | bytes 589828
  14.8 1.1 %copy-start.1 = (bf16[48,8,256]{2,1,0:T(8,128)(2,1)S(1)}, bf16[48,8,256]{2,1,0:T(8,128)(2,1)}, u32[]{:S(2)}) copy-start(bf16[48,8,256]{2,1,0:T(8,128)(2,1)} %param.6) | copy-start | bytes 589828
  17.7 0.9 %copy-start.7 = (bf16[4,48,8,256]{3,2,0,1:T(8,128)(2,1)}, bf16[4,48,8,256]{3,2,0,1:T(8,128)(2,1)S(1)}, u32[]{:S(2)}) copy-start(bf16[4,48,8,256]{3,2,0,1:T(8,128)(2,1)S(1)} %fusion.12) | copy-start | bytes 2359300
  20.0 23.8 %collective-permute-start.5 = (bf16[48,8,256]{2,1,0:T(8,128)(2,1)}, bf16[48,8,256]{2,1,0:T(8,128)(2,1)S(1)}, u32[]{:S(2)}, u32[]{:S(2)}) collective-permute-start(bf16[48,8,256]{2,1,0:T(8,128)(2,1)} %param.7), channel_id=1, source_target_pairs={{1,0},{2,1},{3,2},{4,3},{5,4},{6,5},{7,6},{8,7},{9,8},{10,9},{11,1... | collective-permute-start | bytes 589832 | tf_op jit(solution)/shard_map/ppermute | solution.py:80
  22.7 21.2 %collective-permute-start.4 = (bf16[48,8,256]{2,1,0:T(8,128)(2,1)}, bf16[48,8,256]{2,1,0:T(8,128)(2,1)S(1)}, u32[]{:S(2)}, u32[]{:S(2)}) collective-permute-start(bf16[48,8,256]{2,1,0:T(8,128)(2,1)} %param.7), channel_id=1, source_target_pairs={{0,1},{1,2},{2,3},{3,4},{4,5},{5,6},{6,7},{7,8},{8,9},{9,10},{10,1... | collective-permute-start | bytes 589832 | tf_op jit(solution)/shard_map/ppermute | solution.py:80
  22.7 3.2 %collective-permute-start.2 = (bf16[512,256]{1,0:T(8,128)(2,1)S(1)}, bf16[512,256]{1,0:T(8,128)(2,1)S(1)}, u32[]{:S(2)}, u32[]{:S(2)}) collective-permute-start(bf16[512,256]{1,0:T(8,128)(2,1)S(1)} %bitcast.255), channel_id=1, source_target_pairs={{0,1},{1,0},{2,3},{3,2},{4,5},{5,4},{6,7},{7,6},{8,9},{9,8},{10,11... | collective-permute-start | bytes 786440 | tf_op jit(solution)/shard_map/ppermute | solution.py:177
  23.6 1.6 %collective-permute-start.3 = (bf16[57,8,256]{2,1,0:T(8,128)(2,1)S(1)}, bf16[57,8,256]{2,1,0:T(8,128)(2,1)S(1)}, u32[]{:S(2)}, u32[]{:S(2)}) collective-permute-start(bf16[57,8,256]{2,1,0:T(8,128)(2,1)S(1)} %pad_maximum_fusion.3), channel_id=1, source_target_pairs={{0,1},{1,0},{2,3},{3,2},{4,5},{5,4},{6,7},{7,6},{8,9},{9,8},{10,11... | collective-permute-start | bytes 700424 | tf_op jit(solution)/shard_map/ppermute | solution.py:120
  26.8 17.0 %all-to-all-start.1 = ((bf16[16,32,256]{2,1,0:T(8,128)(2,1)}), bf16[16,32,256]{2,1,0:T(8,128)(2,1)S(1)}, u32[]{:S(2)}, u32[]{:S(2)}) async-start(bf16[16,32,256]{2,1,0:T(8,128)(2,1)} %bitcast.71), calls=%async_computation.1 | async-start | bytes 524288 | tf_op jit(solution)/shard_map/all_to_all | solution.py:199
  34.5 3.3 %copy-start.2 = (f32[4,4,8,256]{3,2,0,1:T(8,128)}, f32[4,4,8,256]{3,2,0,1:T(8,128)S(1)}, u32[]{:S(2)}) copy-start(f32[4,4,8,256]{3,2,0,1:T(8,128)S(1)} %convolution_bitcast_fusion.5) | copy-start | bytes 393220
  44.6 12.7 %all-to-all-start.2 = ((bf16[16,32,256]{2,1,0:T(8,128)(2,1)}), bf16[16,32,256]{2,1,0:T(8,128)(2,1)S(1)}, u32[]{:S(2)}, u32[]{:S(2)}) async-start(bf16[16,32,256]{2,1,0:T(8,128)(2,1)} %broadcast_in_dim.108), calls=%async_computation.2 | async-start | bytes 524288 | tf_op jit(solution)/shard_map/all_to_all | solution.py:201
  49.1 0.9 %slice-start = ((f32[4,4,8,256]{3,2,0,1:T(8,128)}), f32[4,1,8,256]{3,2,0,1:T(8,128)S(1)}, s32[]{:S(2)}) async-start(f32[4,4,8,256]{3,2,0,1:T(8,128)} %copy-done.2), calls=%async_computation.3 | async-start | bytes 65536 | tf_op jit(solution)/shard_map/slice | solution.py:155
  49.1 0.9 %slice-start.1 = ((f32[4,4,8,256]{3,2,0,1:T(8,128)}), f32[4,3,8,256]{3,2,0,1:T(8,128)S(1)}, s32[]{:S(2)}) async-start(f32[4,4,8,256]{3,2,0,1:T(8,128)} %copy-done.2), calls=%async_computation.4 | async-start | bytes 196608 | tf_op jit(solution)/shard_map/slice | solution.py:155
  57.3 1.5 %collective-permute-start.6 = (bf16[16,32,256]{2,1,0:T(8,128)(2,1)S(1)}, bf16[16,32,256]{2,1,0:T(8,128)(2,1)S(1)}, u32[]{:S(2)}, u32[]{:S(2)}) collective-permute-start(bf16[16,32,256]{2,1,0:T(8,128)(2,1)S(1)} %all-to-all-done.2), channel_id=1, source_target_pairs={{0,1},{1,0},{2,3},{3,2},{4,5},{5,4},{6,7},{7,6},{8,9},{9,8},{10,11... | collective-permute-start | bytes 786440 | tf_op jit(solution)/shard_map/ppermute | solution.py:216

commit v7 on v2

--- a/solution.py
+++ b/solution.py
@@ -174,9 +174,9 @@
         return out + rows(edge[:, :R], 0) + rows(edge[:, R:], lat_count - R)
 
     banded = dot("ikarm,irmc->ikac", forward, windows(signal_left, signal, signal_right))
-    banded = jnp.moveaxis(banded, 1, 0)
+    banded = bf16(jnp.moveaxis(banded, 1, 0))
     scale = 1.0 / math.sqrt(total_rows * lon_total)
-    partial = (dot("kiac,iae->kce", bf16(banded), cotangent) * scale).reshape(2, -1, channels)
+    partial = (dot("kiac,iae->kce", banded, cotangent) * scale).reshape(2, -1, channels)
     given = bf16(jnp.where(core == 0, partial[1], partial[0]))
     kept = jnp.where(core == 0, partial[0], partial[1])
     given, late = lax.optimization_barrier((given, cotangent))

time: 60.6 us -> 59.3 us (0.979)
  starting transfers between devices: 23 us -> 21.8 us
    all_to_all x1, waiting for transfers between devices: 0.01 us -> 1.04 us  [local(): lax.all_to_all(sent.reshape((-1,) + polar_rows.shape), CHIPS, 0, 0)]
    all_to_all x1, waiting for transfers between devices: 5.63 us -> 4.67 us  [local(): lax.all_to_all(jnp.broadcast_to(chunk[None], (group,) + chunk.shape), CHI...]
    concatenate x2, local copies, waits for them, and re-layouts: 0.03 us -> 0.99 us  [windows(): ext = jnp.concatenate([left, field, right], axis=1)]
    optimization_barrier x2, local copies, waits for them, and re-layouts: 0.83 us -> 0.02 us  [local(): lax.optimization_barrier((signal_left, signal_right, band_kernel, cycle_k...]
    all_to_all x1, starting transfers between devices: 4.22 us -> 3.53 us  [local(): parts = lax.all_to_all(bf16(kept).reshape(group, -1, channels), CHIPS, 0, 0)]
  transfers between devices with their start and end apart: 10 -> 10, of which waited for: 4 -> 5; matrix products, arithmetic and copies ran while one was open for 32% -> 33% of each run, Pallas kernels for 0% -> 0%
where the time goes in v7:
time: 59.3 us; the launch traced here: 58.6 us
  starting transfers between devices  21.8 us (37%)
  waiting for transfers between devices  14.6 us (25%)
  local copies, waits for them, and re-layouts  9.1 us (15%)
  matrix products  7.99 us (13%)
  other arithmetic  3.88 us (7%)
  between operations  1.24 us (2%)
    ppermute x2, starting transfers between devices, sector_edges(): lax.ppermute(field, LON, to_left)  9.46 us
    dot_general x11, matrix products, dot(): return jnp.einsum(spec, a, b, preferred_element_type=jnp.float32)  7.99 us
    all_to_all x1, waiting for transfers between devices, local(): parts = lax.all_to_all(bf16(kept).reshape(group, -1, channels), CHIPS, 0, 0)  6.19 us
    all_to_all x1, waiting for transfers between devices, local(): lax.all_to_all(jnp.broadcast_to(chunk[None], (group,) + chunk.shape), CHI...  4.67 us
    all_to_all x1, starting transfers between devices, local(): lax.all_to_all(sent.reshape((-1,) + polar_rows.shape), CHIPS, 0, 0)  4.57 us
    all_to_all x1, starting transfers between devices, local(): parts = lax.all_to_all(bf16(kept).reshape(group, -1, channels), CHIPS, 0, 0)  3.53 us
    all_to_all x1, starting transfers between devices, local(): lax.all_to_all(jnp.broadcast_to(chunk[None], (group,) + chunk.shape), CHI...  3.53 us
    convert_element_type x2, local copies, waits for them, and re-layouts, bf16(): return x.astype(jnp.bfloat16)  2.12 us
  transfers between devices with their start and end apart: 10, of which 5 were waited for; matrix products, arithmetic and copies ran while one was open for 33% of the time, Pallas kernels for 0%

profile of v7, /device:TPU:0, one launch (start us, length us, event | category | flops | bytes accessed | tf_op | source)
XLA Modules:
  0.0 58.6 jit_solution(18035869203601114143)
XLA Ops:
  0.6 0.0 copy-start
  0.7 0.5 collective-permute-start
  1.2 5.0 %collective-permute-start.1 = (bf16[48,8,256]{2,1,0:T(8,128)(2,1)}, bf16[48,8,256]{2,1,0:T(8,128)(2,1)S(1)}, u32[]{:S(2)}, u32[]{:S(2)}) collective-permute-start(bf16[48,8,256]{2,1,0:T(8,128)(2,1)} %param.6), channel_id=1, source_target_pairs={{1,0},{2,1},{3,2},{4,3},{5,4},{6,5},{7,6},{8,7},{9,8},{10,9},{11,1... | collective-permute-start | bytes 589832 | tf_op jit(solution)/shard_map/ppermute | solution.py:80
  6.2 0.7 %fusion.83 = (bf16[1,8,256]{2,1,0:T(8,128)(2,1)S(1)}, bf16[1,8,256]{2,1,0:T(8,128)(2,1)S(1)}) fusion(bf16[48,8,256]{2,1,0:T(8,128)(2,1)} %param.6), kind=kLoop, calls=%fused_computation.183 | loop fusion | bytes 16384 | tf_op jit(solution)/shard_map/slice | solution.py:90
  6.9 0.7 %fusion.84 = (bf16[1,8,256]{2,1,0:T(8,128)(2,1)S(1)}, bf16[1,8,256]{2,1,0:T(8,128)(2,1)S(1)}, bf16[1,8,256]{2,1,0:T(8,128)(2,1)S(1)}) fusion(bf16[48,8,256]{2,1,0:T(8,128)(2,1)} %param.7, pred[]{:T(512)S(6)} %eq.89), kind=kLoop, calls=%fused_computation.184 | loop fusion | flops 2048 | bytes 20481 | tf_op jit(solution)/shard_map/slice | solution.py:90
  7.6 0.7 %constant_dynamic-slice_fusion.3 = bf16[2,8,256]{2,1,0:T(8,128)(2,1)S(1)} fusion(bf16[48,8,256]{2,1,0:T(8,128)(2,1)} %param.7, s32[]{:T(128)S(6)} %select_n.192), kind=kLoop, calls=%fused_computation.149 | loop fusion | bytes 16388 | tf_op jit(solution)/shard_map/dynamic_slice | solution.py:83
  8.3 0.7 %constant_dynamic-slice_fusion.4 = bf16[3,8,256]{2,1,0:T(8,128)(2,1)S(1)} fusion(bf16[48,8,256]{2,1,0:T(8,128)(2,1)} %param.6, s32[]{:T(128)S(6)} %select_n.191), kind=kLoop, calls=%fused_computation.150 | loop fusion | bytes 24580 | tf_op jit(solution)/shard_map/dynamic_slice | solution.py:83
  9.1 0.1 pad.134.clone
  9.1 0.1 maximum_maximum_fusion
  9.2 0.1 select_select_fusion
  9.3 0.8 %broadcast_in_dim.68 = bf16[2,8,5,8,256]{4,3,2,1,0:T(8,128)(2,1)} broadcast(bf16[2,5,8,256]{3,2,1,0:T(8,128)(2,1)S(1)} %select_select_fusion), dimensions={0,2,3,4} | broadcast | bytes 368640 | tf_op jit(solution)/shard_map/broadcast_in_dim | solution.py:94
  10.0 4.6 %all-to-all-start = ((bf16[16,5,8,256]{3,2,1,0:T(8,128)(2,1)}), bf16[16,5,8,256]{3,2,1,0:T(8,128)(2,1)S(1)}, u32[]{:S(2)}, u32[]{:S(2)}) async-start(bf16[16,5,8,256]{3,2,1,0:T(8,128)(2,1)} %bitcast.37), calls=%async_computation | async-start | bytes 655360 | tf_op jit(solution)/shard_map/all_to_all | solution.py:95
  14.7 0.1 add_select_fusion
  14.8 0.1 pad.108.clone
  14.9 0.1 add_select_fusion.1
  15.0 0.1 pad_dynamic-slice_fusion
  15.1 0.1 compare_and_fusion
  15.2 0.1 dynamic-slice_select_fusion
  15.3 0.2 fusion.43
  15.5 0.4 fusion.13
  15.9 0.0 copy-start.2
  15.9 1.1 %copy.83 = bf16[48,4,8,3,24]{4,2,3,1,0:T(8,128)(2,1)S(1)} copy(bf16[48,4,8,3,24]{0,4,3,1,2:T(8,128)(2,1)S(1)} %fusion.13) | data formatting | bytes 442368 | tf_op jit(solution)/shard_map/convert_element_type | solution.py:24
  17.0 0.1 slice_bitcast_fusion.3
  17.1 0.0 copy-start.3
  17.1 0.7 %fusion.12 = bf16[4,48,8,256]{3,2,0,1:T(8,128)(2,1)S(1)} fusion(bf16[48,4,8,3,24]{4,2,3,1,0:T(8,128)(2,1)S(1)} %copy.83, bf16[48,1,24,256]{3,2,1,0:T(8,128)(2,1)S(1)} %get-tuple-element.38, bf16[48,1,24,256]{3,2,1,0:T(8,128)(2,1)S(1)} %bitcast.229, bf16[48,1,24,256]{3,2,1,0:T(8,128)(2,1)S(1)} %get-tuple-element.37), kind=kOutput, calls=%fused_computation.20 | convolution fusion | flops 58785792 | bytes 2777088 | tf_op jit(solution)/shard_map/ikarm,irmc->ikac/dot_general | solution.py:20
  17.8 0.2 copy-done.3
  18.1 0.5 fusion.11
  18.5 0.4 copy-done.7
  19.0 0.1 collective-permute-start.4
  19.0 4.4 %collective-permute-start.5 = (bf16[48,8,256]{2,1,0:T(8,128)(2,1)S(1)}, bf16[48,8,256]{2,1,0:T(8,128)(2,1)}, u32[]{:S(2)}, u32[]{:S(2)}) collective-permute-start(bf16[48,8,256]{2,1,0:T(8,128)(2,1)S(1)} %copy-done.3), channel_id=1, source_target_pairs={{1,0},{2,1},{3,2},{4,3},{5,4},{6,5},{7,6},{8,7},{9,8},{10,9},{11,1... | collective-permute-start | bytes 589832 | tf_op jit(solution)/shard_map/ppermute | solution.py:80
  23.5 0.1 slice.188
  23.5 0.1 slice.174
  23.7 0.1 collective-permute-start.2
  23.7 0.1 maximum_bitcast_fusion.21
  23.9 0.1 slice_select_fusion
  24.0 1.0 %all-to-all-done = bf16[16,5,8,256]{3,2,1,0:T(8,128)(2,1)S(1)} async-done(((bf16[16,5,8,256]{3,2,1,0:T(8,128)(2,1)}), bf16[16,5,8,256]{3,2,1,0:T(8,128)(2,1)S(1)}, u32[]{:S(2)}, u32[]{:S(2)}) %all-to-all-start) | async-done | bytes 327712 | tf_op jit(solution)/shard_map/all_to_all | solution.py:95
  25.2 0.1 collective-permute-start.3
  25.3 0.3 fusion.18
  25.6 1.1 %collective-permute-done.3 = bf16[57,8,256]{2,1,0:T(8,128)(2,1)S(1)} collective-permute-done((bf16[57,8,256]{2,1,0:T(8,128)(2,1)S(1)}, bf16[57,8,256]{2,1,0:T(8,128)(2,1)S(1)}, u32[]{:S(2)}, u32[]{:S(2)}) %collective-permute-start.3) | collective-permute-done | bytes 233504 | tf_op jit(solution)/shard_map/ppermute | solution.py:118
  26.8 0.1 broadcast_select_fusion.1
  27.0 0.2 convolution_bitcast_fusion.4
  27.2 0.3 fusion.15
  27.5 0.8 %bitcast_add_fusion.1 = bf16[512,256]{1,0:T(8,128)(2,1)} fusion(f32[2,256,256]{2,1,0:T(8,128)S(1)} %fusion.15, f32[2,256,256]{2,1,0:T(8,128)S(1)} %slice_select_fusion, bf16[512,256]{1,0:T(8,128)(2,1)S(1)} %collective-permute-done.2), kind=kLoop, calls=%fused_computation.46 | loop fusion | flops 524288 | bytes 1572864 | tf_op jit(solution)/shard_map/add | solution.py:192
  28.3 3.5 %all-to-all-start.1 = ((bf16[16,32,256]{2,1,0:T(8,128)(2,1)}), bf16[16,32,256]{2,1,0:T(8,128)(2,1)S(1)}, u32[]{:S(2)}, u32[]{:S(2)}) async-start(bf16[16,32,256]{2,1,0:T(8,128)(2,1)} %bitcast.62), calls=%async_computation.1 | async-start | bytes 524288 | tf_op jit(solution)/shard_map/all_to_all | solution.py:195
  31.8 0.1 fusion.85
  31.9 0.2 fusion.19
  32.2 0.4 fusion.14
  32.6 0.2 convolution_bitcast_fusion.5
  32.7 0.0 copy-start.1
  32.8 1.1 %copy.101 = bf16[48,4,8,3,24]{4,2,3,1,0:T(8,128)(2,1)S(1)} copy(bf16[48,4,8,3,24]{0,4,3,1,2:T(8,128)(2,1)S(1)} %fusion.14) | data formatting | bytes 442368 | tf_op jit(solution)/shard_map/convert_element_type | solution.py:24
  33.9 2.2 %fusion.16 = bf16[48,8,256]{2,1,0:T(8,128)(2,1)} fusion(f32[4,1,8,256]{3,2,0,1:T(8,128)S(1)} %constant_dynamic-slice_fusion.1, f32[4,2,8,256]{3,2,0,1:T(8,128)S(1)} %constant_dynamic-slice_fusion, bf16[4,48,8,256]{3,2,0,1:T(8,128)(2,1)} %copy-done.7, pred[]{:T(512)S(6)} %eq.89, bf16[4,256,256]{2,1,0:T(8,128)(2,1)S(1)} %copy-done), kind=kOutput, calls=%fused_computation.27 | convolution fusion | flops 203784192 | bytes 1605633 | tf_op jit(solution)/shard_map/kiac,kce->iae/dot_general | solution.py:20
  36.1 6.2 %all-to-all-done.1 = bf16[16,32,256]{2,1,0:T(8,128)(2,1)S(1)} async-done(((bf16[16,32,256]{2,1,0:T(8,128)(2,1)}), bf16[16,32,256]{2,1,0:T(8,128)(2,1)S(1)}, u32[]{:S(2)}, u32[]{:S(2)}) %all-to-all-start.1) | async-done | bytes 262176 | tf_op jit(solution)/shard_map/all_to_all | solution.py:195
  42.3 0.7 %broadcast_in_dim.107 = bf16[16,32,256]{2,1,0:T(8,128)(2,1)} broadcast(bf16[32,256]{1,0:T(8,128)(2,1)S(1)} %reduce_sum.12), dimensions={1,2} | broadcast | bytes 278528 | tf_op jit(solution)/shard_map/broadcast_in_dim | solution.py:197
  43.0 3.5 %all-to-all-start.2 = ((bf16[16,32,256]{2,1,0:T(8,128)(2,1)}), bf16[16,32,256]{2,1,0:T(8,128)(2,1)S(1)}, u32[]{:S(2)}, u32[]{:S(2)}) async-start(bf16[16,32,256]{2,1,0:T(8,128)(2,1)} %broadcast_in_dim.107), calls=%async_computation.2 | async-start | bytes 524288 | tf_op jit(solution)/shard_map/all_to_all | solution.py:197
  46.6 0.0 slice-start
  46.6 0.0 slice-start.1
  46.6 1.0 %constant_dynamic-update-slice_fusion.3 = bf16[48,24,256]{2,1,0:T(8,128)(2,1)S(1)} fusion(bf16[48,24,256]{2,1,0:T(8,128)(2,1)S(1)} %constant_dynamic-update-slice_fusion.4, bf16[48,8,256]{2,1,0:T(8,128)(2,1)} %collective-permute-done.5), kind=kLoop, calls=%fused_computation.106 | loop fusion | bytes 393216 | tf_op jit(solution)/shard_map/concatenate | solution.py:48
  47.6 0.9 %slice_bitcast_fusion.1 = (bf16[48,1,24,256]{3,2,1,0:T(8,128)(2,1)S(1)}, bf16[48,1,24,256]{3,2,1,0:T(8,128)(2,1)}) fusion(bf16[48,24,256]{2,1,0:T(8,128)(2,1)S(1)} %constant_dynamic-update-slice_fusion.3), kind=kLoop, calls=%fused_computation.40 | loop fusion | bytes 1769472 | tf_op jit(solution)/shard_map/stack | solution.py:50
  48.5 2.7 %fusion.17 = bf16[48,8,256]{2,1,0:T(8,128)(2,1)} fusion(f32[4,1,8,256]{3,2,0,1:T(8,128)S(1)} %slice-done, f32[4,3,8,256]{3,2,0,1:T(8,128)S(1)} %slice-done.1, bf16[48,4,8,3,24]{4,2,3,1,0:T(8,128)(2,1)S(1)} %copy.101, bf16[48,1,24,256]{3,2,1,0:T(8,128)(2,1)} %get-tuple-element.36, bf16[48,1,24,256]{3,2,1,0:T(8,128)(2,1)S(1)} %bitcast.230, ...), kind=kOutput, calls=%fused_computation.28 | convolution fusion | flops 261783552 | bytes 2842625 | tf_op jit(solution)/shard_map/kjbe,kce->jbc/dot_general | solution.py:20
  51.2 4.7 %all-to-all-done.2 = bf16[16,32,256]{2,1,0:T(8,128)(2,1)S(1)} async-done(((bf16[16,32,256]{2,1,0:T(8,128)(2,1)}), bf16[16,32,256]{2,1,0:T(8,128)(2,1)S(1)}, u32[]{:S(2)}, u32[]{:S(2)}) %all-to-all-start.2) | async-done | bytes 262176 | tf_op jit(solution)/shard_map/all_to_all | solution.py:197
  55.9 1.5 %collective-permute-done.6 = bf16[16,32,256]{2,1,0:T(8,128)(2,1)S(1)} collective-permute-done((bf16[16,32,256]{2,1,0:T(8,128)(2,1)S(1)}, bf16[16,32,256]{2,1,0:T(8,128)(2,1)S(1)}, u32[]{:S(2)}, u32[]{:S(2)}) %collective-permute-start.6) | collective-permute-done | bytes 262176 | tf_op jit(solution)/shard_map/ppermute | solution.py:212
  57.4 0.1 select_bitcast_fusion.1
  57.5 0.1 pad_maximum_fusion
  57.5 1.1 %convert.2 = f32[4,256,256]{2,1,0:T(8,128)} convert(bf16[4,256,256]{2,1,0:T(8,128)(2,1)S(1)} %bitcast.227) | non-fusion elementwise | flops 262144 | bytes 1572864 | tf_op jit(solution)/shard_map/convert_element_type | solution.py:214
  (62 shorter events, 0.6 us)
Async XLA Ops:
  0.6 33.2 %copy-start = (bf16[4,256,256]{2,1,0:T(8,128)(2,1)S(1)}, bf16[4,256,256]{2,1,0:T(8,128)(2,1)}, u32[]{:S(2)}) copy-start(bf16[4,256,256]{2,1,0:T(8,128)(2,1)} %param.8) | copy-start | bytes 1572868
  0.6 14.3 %copy-start.4 = (bf16[4,96,3,17]{1,0,3,2:T(4,128)(2,1)S(1)}, bf16[4,96,3,17]{1,0,3,2:T(4,128)(2,1)}, u32[]{:S(2)}) copy-start(bf16[4,96,3,17]{1,0,3,2:T(4,128)(2,1)} %param.9) | copy-start | bytes 117508
  0.7 14.4 %copy-start.6 = (s32[96]{0:T(128)S(1)}, s32[96]{0:T(128)}, u32[]{:S(2)}) copy-start(s32[96]{0:T(128)} %param.11) | copy-start | bytes 1156
  0.7 14.3 %collective-permute-start = (bf16[48,8,256]{2,1,0:T(8,128)(2,1)}, bf16[48,8,256]{2,1,0:T(8,128)(2,1)S(1)}, u32[]{:S(2)}, u32[]{:S(2)}) collective-permute-start(bf16[48,8,256]{2,1,0:T(8,128)(2,1)} %param.6), channel_id=1, source_target_pairs={{0,1},{1,2},{2,3},{3,4},{4,5},{5,6},{6,7},{7,8},{8,9},{9,10},{10,1... | collective-permute-start | bytes 589832 | tf_op jit(solution)/shard_map/ppermute | solution.py:80
  1.2 13.8 %collective-permute-start.1 = (bf16[48,8,256]{2,1,0:T(8,128)(2,1)}, bf16[48,8,256]{2,1,0:T(8,128)(2,1)S(1)}, u32[]{:S(2)}, u32[]{:S(2)}) collective-permute-start(bf16[48,8,256]{2,1,0:T(8,128)(2,1)} %param.6), channel_id=1, source_target_pairs={{1,0},{2,1},{3,2},{4,3},{5,4},{6,5},{7,6},{8,7},{9,8},{10,9},{11,1... | collective-permute-start | bytes 589832 | tf_op jit(solution)/shard_map/ppermute | solution.py:80
  10.0 15.0 %all-to-all-start = ((bf16[16,5,8,256]{3,2,1,0:T(8,128)(2,1)}), bf16[16,5,8,256]{3,2,1,0:T(8,128)(2,1)S(1)}, u32[]{:S(2)}, u32[]{:S(2)}) async-start(bf16[16,5,8,256]{3,2,1,0:T(8,128)(2,1)} %bitcast.37), calls=%async_computation | async-start | bytes 655360 | tf_op jit(solution)/shard_map/all_to_all | solution.py:95
  15.9 1.1 %copy-start.2 = (bf16[48,8,256]{2,1,0:T(8,128)(2,1)S(1)}, bf16[48,8,256]{2,1,0:T(8,128)(2,1)}, u32[]{:S(2)}) copy-start(bf16[48,8,256]{2,1,0:T(8,128)(2,1)} %param.6) | copy-start | bytes 589828
  17.1 0.9 %copy-start.3 = (bf16[48,8,256]{2,1,0:T(8,128)(2,1)S(1)}, bf16[48,8,256]{2,1,0:T(8,128)(2,1)}, u32[]{:S(2)}) copy-start(bf16[48,8,256]{2,1,0:T(8,128)(2,1)} %param.7) | copy-start | bytes 589828
  18.0 0.9 %copy-start.7 = (bf16[4,48,8,256]{3,2,0,1:T(8,128)(2,1)}, bf16[4,48,8,256]{3,2,0,1:T(8,128)(2,1)S(1)}, u32[]{:S(2)}) copy-start(bf16[4,48,8,256]{3,2,0,1:T(8,128)(2,1)S(1)} %fusion.12) | copy-start | bytes 2359300
  18.1 5.6 %copy-start.5 = (bf16[4,4,3,128]{3,1,2,0:T(4,128)(2,1)S(1)}, bf16[4,4,3,128]{3,1,2,0:T(4,128)(2,1)}, u32[]{:S(2)}) copy-start(bf16[4,4,3,128]{3,1,2,0:T(4,128)(2,1)} %param.10) | copy-start | bytes 36868
  19.0 27.6 %collective-permute-start.4 = (bf16[48,8,256]{2,1,0:T(8,128)(2,1)S(1)}, bf16[48,8,256]{2,1,0:T(8,128)(2,1)S(1)}, u32[]{:S(2)}, u32[]{:S(2)}) collective-permute-start(bf16[48,8,256]{2,1,0:T(8,128)(2,1)S(1)} %copy-done.3), channel_id=1, source_target_pairs={{0,1},{1,2},{2,3},{3,4},{4,5},{5,6},{6,7},{7,8},{8,9},{9,10},{10,1... | collective-permute-start | bytes 589832 | tf_op jit(solution)/shard_map/ppermute | solution.py:80
  19.0 27.5 %collective-permute-start.5 = (bf16[48,8,256]{2,1,0:T(8,128)(2,1)S(1)}, bf16[48,8,256]{2,1,0:T(8,128)(2,1)}, u32[]{:S(2)}, u32[]{:S(2)}) collective-permute-start(bf16[48,8,256]{2,1,0:T(8,128)(2,1)S(1)} %copy-done.3), channel_id=1, source_target_pairs={{1,0},{2,1},{3,2},{4,3},{5,4},{6,5},{7,6},{8,7},{9,8},{10,9},{11,1... | collective-permute-start | bytes 589832 | tf_op jit(solution)/shard_map/ppermute | solution.py:80
  23.7 3.8 %collective-permute-start.2 = (bf16[512,256]{1,0:T(8,128)(2,1)S(1)}, bf16[512,256]{1,0:T(8,128)(2,1)S(1)}, u32[]{:S(2)}, u32[]{:S(2)}) collective-permute-start(bf16[512,256]{1,0:T(8,128)(2,1)S(1)} %bitcast.233), channel_id=1, source_target_pairs={{0,1},{1,0},{2,3},{3,2},{4,5},{5,4},{6,7},{7,6},{8,9},{9,8},{10,11... | collective-permute-start | bytes 786440 | tf_op jit(solution)/shard_map/ppermute | solution.py:184
  25.2 1.6 %collective-permute-start.3 = (bf16[57,8,256]{2,1,0:T(8,128)(2,1)S(1)}, bf16[57,8,256]{2,1,0:T(8,128)(2,1)S(1)}, u32[]{:S(2)}, u32[]{:S(2)}) collective-permute-start(bf16[57,8,256]{2,1,0:T(8,128)(2,1)S(1)} %pad_maximum_fusion.2), channel_id=1, source_target_pairs={{0,1},{1,0},{2,3},{3,2},{4,5},{5,4},{6,7},{7,6},{8,9},{9,8},{10,11... | collective-permute-start | bytes 700424 | tf_op jit(solution)/shard_map/ppermute | solution.py:118
  28.3 13.9 %all-to-all-start.1 = ((bf16[16,32,256]{2,1,0:T(8,128)(2,1)}), bf16[16,32,256]{2,1,0:T(8,128)(2,1)S(1)}, u32[]{:S(2)}, u32[]{:S(2)}) async-start(bf16[16,32,256]{2,1,0:T(8,128)(2,1)} %bitcast.62), calls=%async_computation.1 | async-start | bytes 524288 | tf_op jit(solution)/shard_map/all_to_all | solution.py:195
  32.7 3.3 %copy-start.1 = (f32[4,4,8,256]{3,2,0,1:T(8,128)}, f32[4,4,8,256]{3,2,0,1:T(8,128)S(1)}, u32[]{:S(2)}) copy-start(f32[4,4,8,256]{3,2,0,1:T(8,128)S(1)} %convolution_bitcast_fusion.5) | copy-start | bytes 393220
  43.0 12.9 %all-to-all-start.2 = ((bf16[16,32,256]{2,1,0:T(8,128)(2,1)}), bf16[16,32,256]{2,1,0:T(8,128)(2,1)S(1)}, u32[]{:S(2)}, u32[]{:S(2)}) async-start(bf16[16,32,256]{2,1,0:T(8,128)(2,1)} %broadcast_in_dim.107), calls=%async_computation.2 | async-start | bytes 524288 | tf_op jit(solution)/shard_map/all_to_all | solution.py:197
  46.6 1.9 %slice-start = ((f32[4,4,8,256]{3,2,0,1:T(8,128)}), f32[4,1,8,256]{3,2,0,1:T(8,128)S(1)}, s32[]{:S(2)}) async-start(f32[4,4,8,256]{3,2,0,1:T(8,128)} %copy-done.1), calls=%async_computation.3 | async-start | bytes 65536 | tf_op jit(solution)/shard_map/slice | solution.py:162
  46.6 1.9 %slice-start.1 = ((f32[4,4,8,256]{3,2,0,1:T(8,128)}), f32[4,3,8,256]{3,2,0,1:T(8,128)S(1)}, s32[]{:S(2)}) async-start(f32[4,4,8,256]{3,2,0,1:T(8,128)} %copy-done.1), calls=%async_computation.4 | async-start | bytes 196608 | tf_op jit(solution)/shard_map/slice | solution.py:162
  55.9 1.5 %collective-permute-start.6 = (bf16[16,32,256]{2,1,0:T(8,128)(2,1)S(1)}, bf16[16,32,256]{2,1,0:T(8,128)(2,1)S(1)}, u32[]{:S(2)}, u32[]{:S(2)}) collective-permute-start(bf16[16,32,256]{2,1,0:T(8,128)(2,1)S(1)} %all-to-all-done.2), channel_id=1, source_target_pairs={{0,1},{1,0},{2,3},{3,2},{4,5},{5,4},{6,7},{7,6},{8,9},{9,8},{10,11... | collective-permute-start | bytes 786440 | tf_op jit(solution)/shard_map/ppermute | solution.py:212
